TPU v7x, 32 devices: a whole 2x2x4 slice. The times are simulated.
32 devices in a mesh: dp: 4 (over z), seq: 8 (over y, x, core).
Axes of the slice: x: 2, y: 2, z: 4, core: 2. Of those that a mesh axis runs over, the one named last changes fastest.
Arguments:
- inputs: bfloat16 [2, 4, 1024, 2048], P(None, 'dp', 'seq'), may hold values from -6 to 6
- lengths: int32 [2, 4], P(None, 'dp'), may hold values from 256 to 1024, as said below
- first_gain: float32 [2048], replicated, may hold values from 0.5 to 1.5
- input_weight: bfloat16 [2048, 8192], P(('dp', 'seq')), may hold values from -0.125 to 0.125
- decay_weight: bfloat16 [2048, 32], replicated, may hold values from -0.125 to 0.125
- conv_weight: float32 [4, 6144], replicated, may hold values from -3 to 3
- decay_log: float32 [16], replicated, may hold values from -12 to -2
- decay_bias: float32 [16], replicated, may hold values from -1.5 to 1
- head_gain: float32 [128], replicated, may hold values from 0.5 to 1.5
- output_weight: bfloat16 [2048, 2048], P(('dp', 'seq')), may hold values from -0.1875 to 0.1875
- second_gain: float32 [2048], replicated, may hold values from 0.5 to 1.5
- gate_up_weight: bfloat16 [2048, 11264], P(('dp', 'seq')), may hold values from -0.125 to 0.125
- down_weight: bfloat16 [5632, 2048], P(('dp', 'seq')), may hold values from -0.15625 to 0.15625
- cotangent: bfloat16 [2, 4, 1024, 2048], P(None, 'dp', 'seq'), may hold values from -6 to 6
Outputs:
- result: float32 [2, 4, 1024, 2048], P(None, 'dp', 'seq')
- inputs_grad: float32 [2, 4, 1024, 2048], P(None, 'dp', 'seq')
- first_gain_grad: float32 [2048], replicated
- input_weight_grad: float32 [2048, 8192], P(('dp', 'seq'))
- decay_weight_grad: float32 [2048, 32], replicated
- conv_weight_grad: float32 [4, 6144], replicated
- decay_log_grad: float32 [16], replicated
- decay_bias_grad: float32 [16], replicated
- head_gain_grad: float32 [128], replicated
- output_weight_grad: float32 [2048, 2048], P(('dp', 'seq'))
- second_gain_grad: float32 [2048], replicated
- gate_up_grad: float32 [2048, 11264], P(('dp', 'seq'))
- down_grad: float32 [5632, 2048], P(('dp', 'seq'))
Inputs may be any that keep to these rules, and one draw needn't show every extreme that they name: `lengths`: in each aligned group of 1 column, one entry over both micro-batches equals 1024.
All inputs are finite; a program needn't handle non-finite values.
Results may differ from a plain program's by a relative error of at most 0.015.
Values may be sent and summed in bfloat16 or wider, within the bound.
A program may use at most 512 MiB of HBM per device.

v0:
```python
import jax
import jax.numpy as jnp
from jax import lax
from jax.sharding import PartitionSpec as P

SPAN = 64


HIGH = lax.Precision.HIGHEST


def shifted(value, axis, steps):
    count = lax.axis_size(axis)
    initial, last = (max(0, -steps), min(count, count - steps))
    return lax.ppermute(value, axis, [(source, source + steps) for source in range(initial, last)])


def rms_norm(values, gain):
    return values * lax.rsqrt(jnp.mean(values * values, -1, keepdims=True) + 1e-05) * gain


def unit_norm(vectors):
    return vectors * lax.rsqrt(jnp.sum(vectors * vectors, -1, keepdims=True) + 1e-06)


def swish_product(gate_part, up_part):
    return jax.nn.silu(gate_part) * up_part


def unit_inverse(strict_lower):
    extent = strict_lower.shape[-1]
    identity_matrix = jnp.eye(extent, dtype=jnp.float32)
    inverse = identity_matrix - strict_lower
    power_term = strict_lower
    for level_index in range(1, (extent - 1).bit_length()):
        power_term = jnp.einsum("bhij,bhjk->bhik", power_term, power_term, precision=HIGH)
        inverse = jnp.einsum(
            "bhij,bhjk->bhik", inverse, identity_matrix + power_term, precision=HIGH
        )
    return inverse


def span_step(memory, pieces):
    queries, probes, writes, decays, strengths = pieces
    extent = decays.shape[-1]
    running = jnp.cumsum(decays, axis=-1)
    spread = running[..., :, None] - running[..., None, :]
    row_index = lax.broadcasted_iota(jnp.int32, (extent, extent), 0)
    col_index = lax.broadcasted_iota(jnp.int32, (extent, extent), 1)
    faded = jnp.exp(jnp.minimum(spread, 0.0))
    inclusive = jnp.where(col_index <= row_index, faded, 0.0) * strengths[..., None, :]
    strict_mask = jnp.where(col_index < row_index, faded, 0.0) * strengths[..., None, :]
    strict_lower = strict_mask * jnp.einsum("bhtd,bhsd->bhts", probes, probes, precision=HIGH)
    scale_in = jnp.exp(running)[..., None]
    target = writes - scale_in * jnp.einsum("bhtd,bhde->bhte", probes, memory, precision=HIGH)
    fresh_values = jnp.einsum("bhts,bhse->bhte", unit_inverse(strict_lower), target, precision=HIGH)
    mixing = inclusive * jnp.einsum("bhtd,bhsd->bhts", queries, probes, precision=HIGH)
    outputs = scale_in * jnp.einsum("bhtd,bhde->bhte", queries, memory, precision=HIGH)
    outputs = outputs + jnp.einsum("bhts,bhse->bhte", mixing, fresh_values, precision=HIGH)
    remaining = jnp.exp(running[..., -1:] - running) * strengths
    memory = jnp.exp(running[..., -1])[..., None, None] * memory + jnp.einsum(
        "bhsd,bhse->bhde", probes * remaining[..., None], fresh_values, precision=HIGH
    )
    return (memory, outputs)


def delta_local(queries, probes, writes, decays, strengths, memory):
    seq_count, head_count, length, head_size = queries.shape
    blocks = length // SPAN

    def arrange(tensor):
        shaped = tensor.reshape(tensor.shape[:2] + (blocks, SPAN) + tensor.shape[3:])
        return jnp.moveaxis(shaped, 2, 0)

    pieces = (
        arrange(queries),
        arrange(probes),
        arrange(writes),
        arrange(decays),
        arrange(strengths),
    )
    memory, outputs = lax.scan(span_step, memory, pieces)
    outputs = jnp.moveaxis(outputs, 0, 2)
    return (outputs.reshape(seq_count, head_count, length, outputs.shape[-1]), memory)


def prepare(packed, logits, conv_weight, decay_log, decay_bias):
    seq_count, length, logit_width = logits.shape
    head_count = decay_log.shape[0]
    tap_count = conv_weight.shape[0]
    convolved = conv_weight[0] * packed[:, 0:length]
    for tap_index in range(1, tap_count):
        convolved = convolved + conv_weight[tap_index] * packed[:, tap_index : tap_index + length]
    active = jax.nn.silu(convolved)
    key_width = active.shape[-1] // 3
    head_size = key_width // head_count

    def split_heads(portion):
        return jnp.transpose(
            portion.reshape(seq_count, length, head_count, head_size), (0, 2, 1, 3)
        )

    queries = unit_norm(split_heads(active[..., :key_width])) * head_size ** (-0.5)
    probes = unit_norm(split_heads(active[..., key_width : 2 * key_width]))
    writes = split_heads(active[..., 2 * key_width :])
    decays = jnp.transpose(
        -jnp.exp(decay_log) * jax.nn.softplus(logits[..., :head_count] + decay_bias), (0, 2, 1)
    )
    strengths = jnp.transpose(jax.nn.sigmoid(logits[..., head_count:]), (0, 2, 1))
    return (queries, probes, writes, decays, strengths)


def mixer_core(packed, logits, conv_weight, decay_log, decay_bias, memory):
    queries, probes, writes, decays, strengths = prepare(
        packed, logits, conv_weight, decay_log, decay_bias
    )
    return delta_local(queries, probes, writes, decays, strengths, memory)


def finish(mixer_out, gate_raw, head_gain):
    seq_count, head_count, length, head_size = mixer_out.shape
    normal_out = rms_norm(mixer_out, head_gain)
    flat_rows = jnp.transpose(normal_out, (0, 2, 1, 3)).reshape(
        seq_count, length, head_count * head_size
    )
    return flat_rows * jax.nn.silu(gate_raw)


def carry_forward(transfer, offset):

    def turn_step(step_index, incoming):
        leaving = jnp.einsum("bhij,bhjk->bhik", transfer, incoming, precision=HIGH) + offset
        return shifted(leaving.astype(jnp.bfloat16), "seq", 1).astype(leaving.dtype)

    return lax.fori_loop(0, lax.axis_size("seq") - 1, turn_step, jnp.zeros_like(offset))


def carry_back(transfer, source):
    flipped = jnp.swapaxes(transfer, 2, 3)

    def turn_step(step_index, incoming):
        leaving = jnp.einsum("bhij,bhjk->bhik", flipped, incoming, precision=HIGH) + source
        return shifted(leaving.astype(jnp.bfloat16), "seq", -1).astype(leaving.dtype)

    return lax.fori_loop(0, lax.axis_size("seq") - 1, turn_step, jnp.zeros_like(source))


def per_device(
    inputs,
    lengths,
    first_gain,
    input_weight,
    decay_weight,
    conv_weight,
    decay_log,
    decay_bias,
    head_gain,
    output_weight,
    second_gain,
    gate_up_weight,
    down_weight,
    cotangent,
):
    micro_count, seq_local, length, model_width = inputs.shape
    seq_count = micro_count * seq_local
    row_count = seq_count * length
    head_count = decay_log.shape[0]
    key_width = input_weight.shape[1] // 4
    head_size = key_width // head_count
    tap_count = conv_weight.shape[0]
    tokens = inputs.reshape(row_count, model_width).astype(jnp.float32)
    positions = lax.axis_index("seq") * length + lax.broadcasted_iota(
        jnp.int32, (micro_count, seq_local, length), 2
    )
    valid_rows = (positions < lengths[:, :, None]).astype(jnp.float32).reshape(row_count, 1)
    in_full, out_full, gate_up_full, down_full = (
        lax.all_gather(input_weight, ("dp", "seq"), axis=0, tiled=True),
        lax.all_gather(output_weight, ("dp", "seq"), axis=0, tiled=True),
        lax.all_gather(gate_up_weight, ("dp", "seq"), axis=0, tiled=True),
        lax.all_gather(down_weight, ("dp", "seq"), axis=0, tiled=True),
    )
    normed, first_pullback = jax.vjp(rms_norm, tokens, first_gain)
    normed_low = normed.astype(jnp.bfloat16)
    projected = jnp.dot(normed_low, in_full, preferred_element_type=jnp.float32)
    mixed_low = (
        projected[:, : 3 * key_width].astype(jnp.bfloat16).reshape(seq_count, length, 3 * key_width)
    )
    gate_raw = projected[:, 3 * key_width :].reshape(seq_count, length, key_width)
    logits = jnp.dot(normed_low, decay_weight, preferred_element_type=jnp.float32).reshape(
        seq_count, length, 2 * head_count
    )
    left_edge = shifted(mixed_low[:, length - tap_count + 1 :], "seq", 1)
    packed = jnp.concatenate([left_edge, mixed_low], 1).astype(jnp.float32)
    queries, probes, writes, decays, strengths = prepare(
        packed, logits, conv_weight, decay_log, decay_bias
    )
    blank_state = jnp.zeros((seq_count, head_count, head_size, head_size), jnp.float32)
    identity_maps = jnp.broadcast_to(jnp.eye(head_size, dtype=jnp.float32), blank_state.shape)
    joined_writes = jnp.concatenate([writes, jnp.zeros_like(writes)], -1)
    joined_outputs, joined_end = delta_local(
        queries,
        probes,
        joined_writes,
        decays,
        strengths,
        jnp.concatenate([blank_state, identity_maps], -1),
    )
    own_out = joined_outputs[..., :head_size]
    carry_out = joined_outputs[..., head_size:]
    offset = joined_end[..., :head_size]
    transfer = joined_end[..., head_size:]
    state_in = carry_forward(transfer, offset)
    mixer_out = own_out + jnp.einsum("bhtd,bhde->bhte", carry_out, state_in, precision=HIGH)
    gated_rows, finish_pullback = jax.vjp(finish, mixer_out, gate_raw, head_gain)
    gated_low = gated_rows.reshape(row_count, key_width).astype(jnp.bfloat16)
    hidden = tokens + jnp.dot(gated_low, out_full, preferred_element_type=jnp.float32)
    second, second_pullback = jax.vjp(rms_norm, hidden, second_gain)
    second_low = second.astype(jnp.bfloat16)
    gate_up = jnp.dot(second_low, gate_up_full, preferred_element_type=jnp.float32)
    ffn_width = gate_up.shape[1] // 2
    activated, swish_pullback = jax.vjp(
        swish_product, gate_up[:, :ffn_width], gate_up[:, ffn_width:]
    )
    activated_low = activated.astype(jnp.bfloat16)
    final_rows = hidden + jnp.dot(activated_low, down_full, preferred_element_type=jnp.float32)
    result = valid_rows * final_rows
    in_full, out_full, gate_up_full, down_full = (
        lax.all_gather(input_weight, ("dp", "seq"), axis=0, tiled=True),
        lax.all_gather(output_weight, ("dp", "seq"), axis=0, tiled=True),
        lax.all_gather(gate_up_weight, ("dp", "seq"), axis=0, tiled=True),
        lax.all_gather(down_weight, ("dp", "seq"), axis=0, tiled=True),
    )
    upstream = valid_rows * cotangent.reshape(row_count, model_width).astype(jnp.float32)
    out_err = upstream.astype(jnp.bfloat16)
    down_term = jnp.einsum("nf,nd->fd", activated_low, out_err, preferred_element_type=jnp.float32)
    activated_grad = jnp.einsum("nd,fd->nf", out_err, down_full, preferred_element_type=jnp.float32)
    gate_grad, up_grad = swish_pullback(activated_grad)
    gate_up_err = jnp.concatenate([gate_grad, up_grad], 1).astype(jnp.bfloat16)
    gate_up_term = jnp.einsum(
        "nd,nf->df", second_low, gate_up_err, preferred_element_type=jnp.float32
    )
    second_grad = jnp.einsum(
        "nf,df->nd", gate_up_err, gate_up_full, preferred_element_type=jnp.float32
    )
    hidden_part, second_gain_grad = second_pullback(second_grad)
    hidden_grad = upstream + hidden_part
    gate_up_share, down_share = (
        lax.psum_scatter(gate_up_term, ("dp", "seq"), scatter_dimension=0, tiled=True),
        lax.psum_scatter(down_term, ("dp", "seq"), scatter_dimension=0, tiled=True),
    )
    branch_err = hidden_grad.astype(jnp.bfloat16)
    output_term = jnp.einsum("nk,nd->kd", gated_low, branch_err, preferred_element_type=jnp.float32)
    gated_grad = jnp.einsum("nd,kd->nk", branch_err, out_full, preferred_element_type=jnp.float32)
    mixer_grad, gate_raw_grad, head_gain_grad = finish_pullback(
        gated_grad.reshape(seq_count, length, key_width)
    )
    source = jnp.einsum("bhtd,bhte->bhde", carry_out, mixer_grad, precision=HIGH)
    state_out_grad = carry_back(transfer, source)
    _, core_pullback = jax.vjp(
        mixer_core, packed, logits, conv_weight, decay_log, decay_bias, state_in
    )
    packed_grad, logits_grad, conv_grad, decay_log_grad, decay_bias_grad, _ = core_pullback(
        (mixer_grad, state_out_grad)
    )
    edge_grad = shifted(packed_grad[:, : tap_count - 1].astype(jnp.bfloat16), "seq", -1).astype(
        jnp.float32
    )
    mixed_grad = packed_grad[:, tap_count - 1 :] + jnp.pad(
        edge_grad, ((0, 0), (length - tap_count + 1, 0), (0, 0))
    )
    in_err = jnp.concatenate(
        [mixed_grad.reshape(row_count, 3 * key_width), gate_raw_grad.reshape(row_count, key_width)],
        1,
    ).astype(jnp.bfloat16)
    input_term = jnp.einsum("nd,nk->dk", normed_low, in_err, preferred_element_type=jnp.float32)
    logits_flat = logits_grad.reshape(row_count, 2 * head_count)
    decay_weight_grad = jnp.einsum(
        "nd,nk->dk", normed_low.astype(jnp.float32), logits_flat, precision=HIGH
    )
    normed_grad = jnp.einsum("nk,dk->nd", in_err, in_full, preferred_element_type=jnp.float32)
    normed_grad = normed_grad + jnp.einsum(
        "nk,dk->nd", logits_flat, decay_weight.astype(jnp.float32), precision=HIGH
    )
    token_part, first_gain_grad = first_pullback(normed_grad)
    inputs_grad = hidden_grad + token_part
    input_share, output_share = (
        lax.psum_scatter(input_term, ("dp", "seq"), scatter_dimension=0, tiled=True),
        lax.psum_scatter(output_term, ("dp", "seq"), scatter_dimension=0, tiled=True),
    )
    small_sums = lax.psum(
        (
            first_gain_grad,
            decay_weight_grad,
            conv_grad,
            decay_log_grad,
            decay_bias_grad,
            head_gain_grad,
            second_gain_grad,
        ),
        ("dp", "seq"),
    )
    return (
        result.reshape(inputs.shape),
        inputs_grad.reshape(inputs.shape),
        small_sums[0],
        input_share,
        small_sums[1],
        small_sums[2],
        small_sums[3],
        small_sums[4],
        small_sums[5],
        output_share,
        small_sums[6],
        gate_up_share,
        down_share,
    )


def solution(mesh):
    in_specs = (
        P(None, "dp", "seq", None),
        P(None, "dp"),
        P(),
        P(("dp", "seq"), None),
        P(),
        P(),
        P(),
        P(),
        P(),
        P(("dp", "seq"), None),
        P(),
        P(("dp", "seq"), None),
        P(("dp", "seq"), None),
        P(None, "dp", "seq", None),
    )
    out_specs = (
        P(None, "dp", "seq", None),
        P(None, "dp", "seq", None),
        P(),
        P(("dp", "seq"), None),
        P(),
        P(),
        P(),
        P(),
        P(),
        P(("dp", "seq"), None),
        P(),
        P(("dp", "seq"), None),
        P(("dp", "seq"), None),
    )
    return jax.shard_map(
        per_device, mesh=mesh, in_specs=in_specs, out_specs=out_specs, check_vma=False
    )
```

profile of v0, /device:TPU:1, one launch (start us, length us, event | category | flops | bytes accessed | tf_op | source)
XLA Modules:
  0.0 3811.9 jit_solution(5757756794725683401)
XLA Ops:
  18.7 189.6 %all-gather.5.cloned.1.call-done = bf16[2048,8192]{1,0:T(8,128)(2,1)} async-done(((bf16[64,8192]{1,0:T(8,128)(2,1)}), bf16[2048,8192]{1,0:T(8,128)(2,1)}) %all-gather.5.cloned.1.call-update) | async-done | bytes 33554448 | tf_op jit(solution)/shard_map/all_gather | solution.py:177
  208.3 17.3 fusion.371
  242.8 11.4 fusion.295
  275.0 102.8 %while.152 = (s32[]{:T(128)}, f32[2,16,128,256]{3,2,1,0:T(8,128)}, f32[2,2,16,64,256]{4,3,2,1,0:T(8,128)}, f32[2,2,16,64]{3,2,1,0:T(8,128)S(1)}, f32[2,2,16,64,1...) while((s32[]{:T(128)}, f32[2,16,128,256]{3,2,1,0:T(8,128)}, ...), condition=%wide.region_5.6_spmd, body=%wide.region_3.5_spmd.sunk | while | flops 4637214720 | bytes 159206368 | solution.py:82
  294.7 7.0 fusion.663
  334.0 6.3 fusion.663
  377.8 5.4 copy.343
  396.5 241.5 %while.155 = (s32[]{:T(128)}, f32[2,16,128,128]{3,2,1,0:T(8,128)}, f32[2,16,128,128]{3,2,1,0:T(8,128)}, f32[2,16,128,128]{3,2,1,0:T(8,128)}, s32[]{:T(128)}, /*index=5*/s32[]{:T(128)}) while((s32[]{:T(128)}, f32[2,16,128,128]{3,2,1,0:T(8,128)}, f32[2,16,128,128]{3,2,1,0:T(8,128)}, f32[2,16,128,128]{3,2,1,0:T(8,128)}, s32[]{:T(128)}, ...), condition=%wide.region_7.8_spmd.clone, body=%wide.region_6.7_spmd.clone.sunk | while | flops 807403520 | bytes 14680183 | solution.py:135
  396.5 5.4 add_convert_fusion.4
  403.9 25.0 collective-permute-done
  430.5 6.1 add_convert_fusion.4
  440.8 34.5 collective-permute-done
  476.9 6.1 add_convert_fusion.4
  487.2 33.5 collective-permute-done
  522.3 7.1 add_convert_fusion.4
  533.2 12.0 collective-permute-done
  546.8 6.8 add_convert_fusion.4
  557.3 12.0 collective-permute-done
  570.9 6.1 add_convert_fusion.4
  581.2 15.7 collective-permute-done
  598.5 6.1 add_convert_fusion.4
  608.8 27.6 collective-permute-done
  638.0 5.5 multiply_reduce_fusion.10
  652.5 8.1 multiply_reduce_fusion.9
  661.8 124.3 %while.154 = (s32[]{:T(128)}, f32[2,16,128,128]{3,2,1,0:T(8,128)}, f32[2,2,16,64,64]{4,3,2,1,0:T(8,128)}, f32[2,2,16,64,64]{4,3,2,1,0:T(8,128)}, f32[2,2,16,1,64...) while((s32[]{:T(128)}, f32[2,16,128,128]{3,2,1,0:T(8,128)}, ...), condition=%wide.region_16.17_spmd.clone.clone, body=%wide.region_14.16_spmd.clone.clone.sunk | while | flops 2826846208 | bytes 336448416 | solution.py:82
  662.8 5.1 fusion.778
  674.4 5.8 bitcast_dynamic-update-slice_fusion.44
  732.4 5.7 bitcast_dynamic-update-slice_fusion.44
  786.1 25.0 fusion.360
  811.1 25.8 fusion.298
  836.9 22.5 multiply_reduce_fusion.4
  862.5 9.0 fusion.308
  884.9 168.6 %while.156 = (s32[]{:T(128)}, f32[2,16,128,128]{3,2,1,0:T(8,128)}, f32[2,16,128,128]{3,2,1,0:T(8,128)}, f32[2,16,128,128]{3,2,1,0:T(8,128)}, s32[]{:T(128)}, /*index=5*/s32[]{:T(128)}) while((s32[]{:T(128)}, f32[2,16,128,128]{3,2,1,0:T(8,128)}, f32[2,16,128,128]{3,2,1,0:T(8,128)}, f32[2,16,128,128]{3,2,1,0:T(8,128)}, ...), condition=%wide.region_13.14_spmd.clone, body=%wide.region_12.13_spmd.clone.sunk | while | flops 807403520 | bytes 14680183 | solution.py:145
  884.9 5.4 add_convert_fusion.5
  892.3 15.4 collective-permute-done.1
  909.3 6.1 add_convert_fusion.5
  917.3 14.4 collective-permute-done.1
  933.4 6.1 add_convert_fusion.5
  941.4 14.4 collective-permute-done.1
  957.4 6.1 add_convert_fusion.5
  965.4 14.4 collective-permute-done.1
  981.4 6.1 add_convert_fusion.5
  989.4 14.4 collective-permute-done.1
  1005.5 6.1 add_convert_fusion.5
  1013.4 14.4 collective-permute-done.1
  1029.5 6.1 add_convert_fusion.5
  1037.5 14.4 collective-permute-done.1
  1059.5 196.2 %while.153 = (s32[]{:T(128)}, f32[2,16,128,128]{3,2,1,0:T(8,128)}, f32[2,2,16,64,128]{4,3,0,2,1:T(8,128)}, f32[2,2,16,64,128]{4,3,0,2,1:T(8,128)}, f32[2,2,16,64...) while((s32[]{:T(128)}, f32[2,16,128,128]{3,2,1,0:T(8,128)}, ...), condition=%wide.region_28.29_spmd.clone, body=%wide.region_17.28_spmd.clone.sunk | while | flops 6051743744 | bytes 377061632 | solution.py:82
  1270.3 7.2 add_add_fusion.3
  1278.9 15.1 multiply_reduce_fusion.3
  1294.8 10.1 fusion.333
  1306.7 19.4 fusion.372
  1326.9 6.6 broadcast_multiply_fusion
  1333.4 11.6 pad_add_fusion
  1358.6 8.8 fusion.294
  1370.6 26.7 fusion.302
  1398.9 34.8 fusion.300
  1434.4 13.0 fusion.304
  1447.5 16.9 fusion.303
  1469.1 51.1 %all-reduce.18 = (f32[2048]{0:T(1024)}, f32[16]{0:T(128)}, f32[16]{0:T(128)}, f32[128]{0:T(128)}, f32[2048]{0:T(1024)}) all-reduce(f32[2048]{0:T(1024)S(1)} %get-tuple-element.2961, f32[16]{0:T(128)S(1)} %negate_multiply_fusion, f32[16]{0:T(128)S(1)} %copy-done.169, ...), channel_id=1, replica_groups=mesh['dp'=4,'seq'=8] {'dp','seq'}, use_global_device_ids=true, to_apply=%region_33.34 | all-reduce | flops 4256 | bytes 34048 | tf_op jit(solution)/shard_map/psum | solution.py:290
  1523.7 92.7 %reduce-scatter.7.cloned.1.call-done = f32[64,2048]{1,0:T(8,128)} async-done(((f32[2048,2048]{1,0:T(8,128)}), f32[64,2048]{1,0:T(8,128)}) %reduce-scatter.7.cloned.1.call-update) | async-done | bytes 524304 | tf_op jit(solution)/shard_map/reduce_scatter | solution.py:288
  1616.4 497.0 %reduce-scatter.11.cloned.1.call-done = f32[176,2048]{1,0:T(8,128)} async-done(((f32[5632,2048]{1,0:T(8,128)}), f32[176,2048]{1,0:T(8,128)}) %reduce-scatter.11.cloned.1.call-update) | async-done | bytes 1441808 | tf_op jit(solution)/shard_map/reduce_scatter | solution.py:249
  2113.4 711.5 %reduce-scatter.5.cloned.1.call-done = f32[64,8192]{1,0:T(8,128)} async-done(((f32[2048,8192]{1,0:T(8,128)}), f32[64,8192]{1,0:T(8,128)}) %reduce-scatter.5.cloned.1.call-update) | async-done | bytes 2097168 | tf_op jit(solution)/shard_map/reduce_scatter | solution.py:287
  2824.9 976.8 %reduce-scatter.9.cloned.1.call-done = f32[64,11264]{1,0:T(8,128)} async-done(((f32[2048,11264]{1,0:T(8,128)}), f32[64,11264]{1,0:T(8,128)}) %reduce-scatter.9.cloned.1.call-update) | async-done | bytes 2883600 | tf_op jit(solution)/shard_map/reduce_scatter | solution.py:248
  (932 shorter events, 555.1 us)
Async XLA Ops:
  7.2 201.0 %all-gather.5.cloned.1.call-start = ((), (), s32[]{:S(2)}) async-start(), calls=%async_computation.4 | async-start | bytes 34603008 | tf_op jit(solution)/shard_map/all_gather | solution.py:177
  8.0 644.5 %all-gather.7.cloned.1.call-start = ((), (), s32[]{:S(2)}) async-start(), calls=%async_computation.5 | async-start | bytes 8650752 | tf_op jit(solution)/shard_map/all_gather | solution.py:178
  8.7 777.3 %all-gather.9.cloned.1.call-start = ((), (), s32[]{:S(2)}) async-start(), calls=%async_computation.6 | async-start | bytes 47579136 | tf_op jit(solution)/shard_map/all_gather | solution.py:179
  9.5 801.6 %all-gather.11.cloned.1.call-start = ((), (), s32[]{:S(2)}) async-start(), calls=%async_computation.7 | async-start | bytes 23789568 | tf_op jit(solution)/shard_map/all_gather | solution.py:180
  10.0 1513.6 %all-reduce.22.cloned.1.call-start = ((), (), s32[]{:S(2)}) async-start(), calls=%async_computation.12 | async-start | bytes 720896 | tf_op jit(solution)/shard_map/psum | solution.py:290
  10.4 7.8 copy-start.151
  18.5 189.7 %copy-start.111 = (bf16[256,2048]{1,0:T(8,128)(2,1)}, bf16[256,2048]{1,0:T(8,128)(2,1)S(1)}, u32[]{:S(2)}) copy-start(bf16[256,2048]{1,0:T(8,128)(2,1)S(1)} %fusion.317) | copy-start | bytes 3145732
  18.6 224.2 %copy-start.125 = (f32[1,6144]{1,0:T(1,128)}, f32[1,6144]{1,0:T(1,128)S(1)}, u32[]{:S(2)}) copy-start(f32[1,6144]{1,0:T(1,128)S(1)} %get-tuple-element.3291) | copy-start | bytes 73732
  18.6 224.2 %copy-start.127 = (f32[1,6144]{1,0:T(1,128)}, f32[1,6144]{1,0:T(1,128)S(1)}, u32[]{:S(2)}) copy-start(f32[1,6144]{1,0:T(1,128)S(1)} %get-tuple-element.3292) | copy-start | bytes 73732
  18.6 224.2 %copy-start.129 = (f32[1,6144]{1,0:T(1,128)}, f32[1,6144]{1,0:T(1,128)S(1)}, u32[]{:S(2)}) copy-start(f32[1,6144]{1,0:T(1,128)S(1)} %get-tuple-element.3293) | copy-start | bytes 73732
  18.7 224.2 %copy-start.131 = (f32[1,6144]{1,0:T(1,128)}, f32[1,6144]{1,0:T(1,128)S(1)}, u32[]{:S(2)}) copy-start(f32[1,6144]{1,0:T(1,128)S(1)} %get-tuple-element.3294) | copy-start | bytes 73732
  228.9 6.9 collective-permute-start.2
  242.8 11.5 copy-start.12
  402.0 26.9 collective-permute-start
  436.5 38.8 %collective-permute-start = (bf16[2,16,128,128]{3,2,1,0:T(8,128)(2,1)}, bf16[2,16,128,128]{3,2,1,0:T(8,128)(2,1)S(1)}, u32[]{:S(2)}, u32[]{:S(2)}) collective-permute-start(bf16[2,16,128,128]{3,2,1,0:T(8,128)(2,1)} %add_convert_fusion.4), channel_id=1, source_target_pairs={{0,1},{1,2},{2,3},{3,4},{4,5},{5,6},{6,7},{8,9},{9,10},{10,11},{11... | collective-permute-start | bytes 3145736 | tf_op jit(solution)/shard_map/while/body/eval_jaxpr/ppermute | solution.py:15
  482.9 37.8 collective-permute-start
  529.4 15.9 collective-permute-start
  553.6 15.7 collective-permute-start
  576.9 20.0 collective-permute-start
  604.6 31.9 collective-permute-start
  652.5 9.3 copy-start.155
  660.5 198.9 %copy-start.121 = (f32[256]{0:T(256)}, f32[256]{0:T(256)S(1)}, u32[]{:S(2)}) copy-start(f32[256]{0:T(256)S(1)} %fusion.354) | copy-start | bytes 3076
  661.8 124.3 %copy-start.119 = (f32[2048]{0:T(1024)S(1)}, f32[2048]{0:T(1024)}, u32[]{:S(2)}) copy-start(f32[2048]{0:T(1024)} %param.34) | copy-start | bytes 24580
  786.1 25.0 copy-start.117
  836.9 22.5 copy-start.163
  836.9 22.6 copy-start.113
  836.9 22.6 copy-start.157
  862.5 9.0 copy-start.43
  862.5 9.4 copy-start.124
  890.4 17.4 collective-permute-start.1
  915.4 16.3 collective-permute-start.1
  939.5 16.3 collective-permute-start.1
  963.5 16.3 collective-permute-start.1
  987.5 16.3 collective-permute-start.1
  1011.5 16.3 collective-permute-start.1
  1035.6 16.3 collective-permute-start.1
  1080.0 7.7 copy-start.104
  1122.7 9.3 copy-start.74
  1124.6 7.5 copy-start.57
  1124.6 7.5 copy-start.60
  1174.6 7.7 copy-start.104
  1217.2 9.3 copy-start.74
  1219.1 7.5 copy-start.57
  1219.1 7.5 copy-start.60
  1257.7 7.6 copy-start.45
  1265.3 13.5 slice-start
  1265.4 13.5 slice-start.1
  1270.3 7.2 copy-start.135
  1270.3 7.2 copy-start.116
  1270.3 8.5 slice-start.2
  1294.7 321.7 %reduce-scatter.7.cloned.1.call-start = ((), (), s32[]{:S(2)}) async-start(), calls=%async_computation.9 | async-start | bytes 17301504 | tf_op jit(solution)/shard_map/reduce_scatter | solution.py:288
  1304.9 808.5 %reduce-scatter.11.cloned.1.call-start = ((), (), s32[]{:S(2)}) async-start(), calls=%async_computation.11 | async-start | bytes 47579136 | tf_op jit(solution)/shard_map/reduce_scatter | solution.py:249
  1326.1 1498.8 %reduce-scatter.5.cloned.1.call-start = ((), (), s32[]{:S(2)}) async-start(), calls=%async_computation.8 | async-start | bytes 69206016 | tf_op jit(solution)/shard_map/reduce_scatter | solution.py:287
  1351.4 5.7 collective-permute-start.3
  1370.6 26.7 copy-start.97
  1397.3 2404.4 %reduce-scatter.9.cloned.1.call-start = ((), (), s32[]{:S(2)}) async-start(), calls=%async_computation.10 | async-start | bytes 95158272 | tf_op jit(solution)/shard_map/reduce_scatter | solution.py:248
  1434.4 13.0 copy-start.118
  1447.4 17.0 copy-start.42
  1447.4 17.0 copy-start.134
  1447.4 17.0 copy-start.136
  1447.4 17.0 copy-start.146
  1447.4 17.0 copy-start.152
  1464.4 55.7 %copy-start.154 = (f32[2,128]{1,0:T(2,128)S(1)}, f32[2,128]{1,0:T(2,128)}, u32[]{:S(2)}) copy-start(f32[2,128]{1,0:T(2,128)} %copy-done.153) | copy-start | bytes 3076
  1464.5 55.7 %copy-start.44 = (f32[256,2048]{1,0:T(8,128)S(1)}, f32[256,2048]{1,0:T(8,128)}, u32[]{:S(2)}) copy-start(f32[256,2048]{1,0:T(8,128)} %copy-done.43) | copy-start | bytes 6291460
  (229 other events, 691.5 us)
Sparse Core Ops, SparseCore 0:
  10.9 197.2 all-gather.4
  211.1 75.6 all-gather.6
  289.7 281.7 all-gather.8
  574.1 152.0 all-gather.10
  1294.8 134.2 all-reduce.21
  1432.0 184.3 reduce-scatter.6
  1619.4 493.9 reduce-scatter.10
  2116.4 708.4 reduce-scatter.4
  2828.0 973.6 reduce-scatter.8
where the time goes:
time: 3820 us; the launch traced here: 3810 us
  waiting for transfers between devices  2740 us (72%)
  matrix products  617 us (16%)
  local copies, waits for them, and re-layouts  155 us (4%)
  other arithmetic  146 us (4%)
  blocking collectives  51.1 us (1%)
  starting transfers between devices  45.5 us (1%)
  loops' own time  44.9 us (1%)
    reduce_scatter x1, waiting for transfers between devices, per_device(): lax.psum_scatter(gate_up_term, ('dp', 'seq'), scatter_dimension=0, tiled=...  977 us
    reduce_scatter x1, waiting for transfers between devices, per_device(): lax.psum_scatter(input_term, ('dp', 'seq'), scatter_dimension=0, tiled=True)  712 us
    reduce_scatter x1, waiting for transfers between devices, per_device(): lax.psum_scatter(down_term, ('dp', 'seq'), scatter_dimension=0, tiled=True)  497 us
    ppermute x16, waiting for transfers between devices, shifted(): lax.ppermute(value, axis, [(source, source + steps) for source in range(i...  266 us
    all_gather x1, waiting for transfers between devices, per_device(): lax.all_gather(input_weight, ('dp', 'seq'), axis=0, tiled=True)  190 us
    reduce_scatter x1, waiting for transfers between devices, per_device(): lax.psum_scatter(output_term, ('dp', 'seq'), scatter_dimension=0, tiled=T...  92.7 us
  transfers between devices with their start and end apart: 25, of which 20 were waited for; matrix products, arithmetic and copies ran while one was open for 13% of the time, Pallas kernels for 0%

commit v1 on v0

--- a/solution.py
+++ b/solution.py
@@ -1,9 +1,14 @@
+import functools
+
 import jax
 import jax.numpy as jnp
 from jax import lax
+from jax.experimental import pallas as pl
+from jax.experimental.pallas import tpu as pltpu
 from jax.sharding import PartitionSpec as P
 
 SPAN = 64
+VMEM_LIMIT = 48 * 1024 * 1024
 
 
 HIGH = lax.Precision.HIGHEST
@@ -224,12 +229,6 @@
     activated_low = activated.astype(jnp.bfloat16)
     final_rows = hidden + jnp.dot(activated_low, down_full, preferred_element_type=jnp.float32)
     result = valid_rows * final_rows
-    in_full, out_full, gate_up_full, down_full = (
-        lax.all_gather(input_weight, ("dp", "seq"), axis=0, tiled=True),
-        lax.all_gather(output_weight, ("dp", "seq"), axis=0, tiled=True),
-        lax.all_gather(gate_up_weight, ("dp", "seq"), axis=0, tiled=True),
-        lax.all_gather(down_weight, ("dp", "seq"), axis=0, tiled=True),
-    )
     upstream = valid_rows * cotangent.reshape(row_count, model_width).astype(jnp.float32)
     out_err = upstream.astype(jnp.bfloat16)
     down_term = jnp.einsum("nf,nd->fd", activated_low, out_err, preferred_element_type=jnp.float32)
@@ -245,8 +244,8 @@
     hidden_part, second_gain_grad = second_pullback(second_grad)
     hidden_grad = upstream + hidden_part
     gate_up_share, down_share = (
-        lax.psum_scatter(gate_up_term, ("dp", "seq"), scatter_dimension=0, tiled=True),
-        lax.psum_scatter(down_term, ("dp", "seq"), scatter_dimension=0, tiled=True),
+        scatter_rows(gate_up_term.astype(BF16), ("dp", "seq")).astype(F32),
+        scatter_rows(down_term.astype(BF16), ("dp", "seq")).astype(F32),
     )
     branch_err = hidden_grad.astype(jnp.bfloat16)
     output_term = jnp.einsum("nk,nd->kd", gated_low, branch_err, preferred_element_type=jnp.float32)
@@ -284,8 +283,8 @@
     token_part, first_gain_grad = first_pullback(normed_grad)
     inputs_grad = hidden_grad + token_part
     input_share, output_share = (
-        lax.psum_scatter(input_term, ("dp", "seq"), scatter_dimension=0, tiled=True),
-        lax.psum_scatter(output_term, ("dp", "seq"), scatter_dimension=0, tiled=True),
+        scatter_rows(input_term.astype(BF16), ("dp", "seq")).astype(F32),
+        scatter_rows(output_term.astype(BF16), ("dp", "seq")).astype(F32),
     )
     small_sums = lax.psum(
         (
@@ -311,6 +310,1171 @@
         small_sums[5],
         output_share,
         small_sums[6],
+        gate_up_share,
+        down_share,
+    )
+
+
+F32 = jnp.float32
+BF16 = jnp.bfloat16
+
+
+def parts(value):
+    top = value.astype(BF16)
+    return (top, (value - top.astype(F32)).astype(BF16))
+
+
+def contract(left, right, right_dim):
+    lhs = jnp.concatenate([left[0], left[1], left[0]], 1)
+    rhs = jnp.concatenate([right[0], right[0], right[1]], right_dim)
+    return lax.dot_general(lhs, rhs, (((1,), (right_dim,)), ((), ())), preferred_element_type=F32)
+
+
+def mm(left, right):
+    return contract(left, right, 0)
+
+
+def mm_nt(left, right):
+    return contract(left, right, 1)
+
+
+def ones_dot(ones, value):
+    first = value.astype(BF16)
+    rest = value - first.astype(F32)
+    second = rest.astype(BF16)
+    third = (rest - second.astype(F32)).astype(BF16)
+    return (
+        jnp.dot(ones, first, preferred_element_type=F32)
+        + jnp.dot(ones, second, preferred_element_type=F32)
+        + jnp.dot(ones, third, preferred_element_type=F32)
+    )
+
+
+def lower_inverse(strict_lower, row_index, col_index):
+    extent = strict_lower.shape[0]
+
+    def below(width):
+        same = (row_index // (2 * width)) == (col_index // (2 * width))
+        return same & ((row_index // width) % 2 == 1) & ((col_index // width) % 2 == 0)
+
+    inverse = jnp.where(row_index == col_index, 1.0, 0.0) - jnp.where(below(1), strict_lower, 0.0)
+    width = 2
+    while width < extent:
+        block = jnp.where(below(width), strict_lower, 0.0)
+        split = parts(inverse)
+        inverse = inverse - mm(parts(mm(split, parts(block))), split)
+        width *= 2
+    return inverse
+
+
+def active_rows(before, rows, taps):
+    extended = jnp.concatenate([before, rows], 0)
+    count = rows.shape[0]
+    tap_count = taps.shape[0]
+    start = before.shape[0] - tap_count + 1
+    shifts = [extended[start + j : start + j + count] for j in range(tap_count)]
+    total = taps[0:1] * shifts[0]
+    for j in range(1, tap_count):
+        total = total + taps[j : j + 1] * shifts[j]
+    return (total, shifts)
+
+
+def soft_plus(value):
+    return jnp.maximum(value, 0.0) + jnp.log(1.0 + jnp.exp(-jnp.abs(value)))
+
+
+def sigmoid(value):
+    return 1.0 / (1.0 + jnp.exp(-value))
+
+
+def unit(vectors):
+    scale = lax.rsqrt(jnp.sum(vectors * vectors, -1, keepdims=True) + 1e-06)
+    return (vectors * scale, scale)
+
+
+def unit_back(vectors, scale, grad):
+    inner = jnp.sum(vectors * grad, -1, keepdims=True)
+    return scale * grad - vectors * (scale * scale * scale * inner)
+
+
+def decay_terms(logit, param_ref, heads, ones):
+    shifted_logit = logit + param_ref[1:2, :]
+    lane = lax.broadcasted_iota(jnp.int32, logit.shape, 1)
+    decays = jnp.where(lane < heads, -jnp.exp(param_ref[0:1, :]) * soft_plus(shifted_logit), 0.0)
+    strengths = sigmoid(logit)
+    running = ones_dot(ones, decays)
+    return (shifted_logit, decays, strengths, running)
+
+
+def mixer_forward(
+    mixed_ref,
+    gate_ref,
+    logit_ref,
+    taps_ref,
+    param_ref,
+    gain_ref,
+    gated_ref,
+    memory_ref,
+    inverse_ref,
+    fresh_ref,
+    out_ref,
+    state_ref,
+    halo_ref,
+):
+    seqs, span, _ = mixed_ref.shape
+    heads, head_size = memory_ref.shape[1], memory_ref.shape[2]
+
+    @pl.when(pl.program_id(0) == 0)
+    def _():
+        state_ref[...] = jnp.zeros_like(state_ref)
+        halo_ref[...] = jnp.zeros_like(halo_ref)
+
+    row_index = lax.broadcasted_iota(jnp.int32, (span, span), 0)
+    col_index = lax.broadcasted_iota(jnp.int32, (span, span), 1)
+    ones = jnp.where(col_index <= row_index, 1.0, 0.0).astype(BF16)
+    taps = taps_ref[...]
+    width = heads * head_size
+    for m in range(seqs):
+        rows = mixed_ref[m].astype(F32)
+        convolved, _ = active_rows(halo_ref[m], rows, taps)
+        halo_ref[m] = rows[span - 8 :]
+        active = convolved * sigmoid(convolved)
+        _, decays, strengths, running = decay_terms(logit_ref[m], param_ref, heads, ones)
+        running_rows = jnp.transpose(running)
+        strength_rows = jnp.transpose(strengths)
+        for h in range(heads):
+            own = slice(h * head_size, (h + 1) * head_size)
+            queries = unit(active[:, own])[0] * head_size ** (-0.5)
+            probes = unit(active[:, width + h * head_size : width + (h + 1) * head_size])[0]
+            writes = active[:, 2 * width + h * head_size : 2 * width + (h + 1) * head_size]
+            run = running[:, h : h + 1]
+            last = running[span - 1 : span, h : h + 1]
+            weight_row = strength_rows[heads + h : heads + h + 1, :]
+            weight_col = strengths[:, heads + h : heads + h + 1]
+            faded = jnp.exp(jnp.minimum(run - running_rows[h : h + 1, :], 0.0)) * weight_row
+            probe_parts = parts(probes)
+            query_parts = parts(queries)
+            strict = jnp.where(col_index < row_index, faded * mm_nt(probe_parts, probe_parts), 0.0)
+            mixing = jnp.where(col_index <= row_index, faded * mm_nt(query_parts, probe_parts), 0.0)
+            inverse = lower_inverse(strict, row_index, col_index)
+            scale_in = jnp.exp(run)
+            both = mm(
+                parts(inverse), parts(jnp.concatenate([writes, scale_in * probes], 1))
+            )
+            memory = state_ref[m, h]
+            memory_parts = parts(memory)
+            reads = mm(
+                parts(jnp.concatenate([both[:, head_size:], scale_in * queries], 0)), memory_parts
+            )
+            fresh = both[:, :head_size] - reads[:span]
+            fresh_parts = parts(fresh)
+            mixer_out = reads[span:] + mm(parts(mixing), fresh_parts)
+            kept = jnp.transpose(jnp.exp(last - run) * weight_col * probes)
+            state_ref[m, h] = jnp.exp(last) * memory + mm(parts(kept), fresh_parts)
+            memory_ref[m, h] = memory
+            inverse_ref[m, h] = inverse
+            fresh_ref[m, :, own] = fresh
+            out_ref[m, :, own] = mixer_out
+            scale = lax.rsqrt(jnp.mean(mixer_out * mixer_out, -1, keepdims=True) + 1e-05)
+            gate = gate_ref[m, :, own]
+            gated_ref[m, :, own] = (
+                mixer_out * scale * gain_ref[...] * (gate * sigmoid(gate))
+            ).astype(BF16)
+
+
+def mixer_backward(
+    mixed_ref,
+    before_ref,
+    gate_ref,
+    logit_ref,
+    taps_ref,
+    param_ref,
+    gain_ref,
+    memory_ref,
+    inverse_ref,
+    fresh_ref,
+    out_ref,
+    grad_ref,
+    error_ref,
+    logit_grad_ref,
+    taps_grad_ref,
+    param_grad_ref,
+    gain_grad_ref,
+    state_ref,
+    halo_ref,
+):
+    seqs, span, _ = mixed_ref.shape
+    heads, head_size = memory_ref.shape[1], memory_ref.shape[2]
+    step = pl.program_id(0)
+
+    @pl.when(step == 0)
+    def _():
+        state_ref[...] = jnp.zeros_like(state_ref)
+        halo_ref[...] = jnp.zeros_like(halo_ref)
+        taps_grad_ref[...] = jnp.zeros_like(taps_grad_ref)
+        param_grad_ref[...] = jnp.zeros_like(param_grad_ref)
+        gain_grad_ref[...] = jnp.zeros_like(gain_grad_ref)
+
+    first = step == pl.num_programs(0) - 1
+    row_index = lax.broadcasted_iota(jnp.int32, (span, span), 0)
+    col_index = lax.broadcasted_iota(jnp.int32, (span, span), 1)
+    ones = jnp.where(col_index <= row_index, 1.0, 0.0).astype(BF16)
+    ones_back = jnp.where(col_index >= row_index, 1.0, 0.0).astype(BF16)
+    taps = taps_ref[...]
+    tap_count = taps.shape[0]
+    width = heads * head_size
+    gain = gain_ref[...]
+    edge = before_ref.shape[1]
+    for m in range(seqs):
+        rows = mixed_ref[m].astype(F32)
+        before = jnp.where(first, 0.0, before_ref[m].astype(F32))[edge - 8 :]
+        convolved, shifts = active_rows(before, rows, taps)
+        opening = sigmoid(convolved)
+        active = convolved * opening
+        logit = logit_ref[m]
+        shifted_logit, decays, strengths, running = decay_terms(logit, param_ref, heads, ones)
+        running_rows = jnp.transpose(running)
+        strength_rows = jnp.transpose(strengths)
+        active_grads = [None] * (3 * heads)
+        gate_grads = [None] * heads
+        col_terms = jnp.zeros((span, span), F32)
+        row_terms = jnp.zeros((span, span), F32)
+        for h in range(heads):
+            own = slice(h * head_size, (h + 1) * head_size)
+            raw_queries = active[:, own]
+            raw_probes = active[:, width + h * head_size : width + (h + 1) * head_size]
+            queries, query_scale = unit(raw_queries)
+            queries = queries * head_size ** (-0.5)
+            probes, probe_scale = unit(raw_probes)
+            mixer_out = out_ref[m, :, own]
+            gate = gate_ref[m, :, own]
+            gated_grad = grad_ref[m, :, own].astype(F32)
+            scale = lax.rsqrt(jnp.mean(mixer_out * mixer_out, -1, keepdims=True) + 1e-05)
+            gate_open = sigmoid(gate)
+            normal = mixer_out * scale
+            gate_grads[h] = gated_grad * normal * gain * (gate_open * (1.0 + gate * (1.0 - gate_open)))
+            normal_grad = gated_grad * (gate * gate_open)
+            gain_grad_ref[0:1, :] += jnp.sum(normal_grad * normal, 0, keepdims=True)
+            weighted = normal_grad * gain
+            out_grad = scale * (
+                weighted - normal * jnp.mean(weighted * normal, -1, keepdims=True)
+            )
+
+            run = running[:, h : h + 1]
+            last = running[span - 1 : span, h : h + 1]
+            weight_row = strength_rows[heads + h : heads + h + 1, :]
+            weight_col = strengths[:, heads + h : heads + h + 1]
+            faded = jnp.exp(jnp.minimum(run - running_rows[h : h + 1, :], 0.0))
+            scale_in = jnp.exp(run)
+            end_scale = jnp.exp(last)
+            remaining = jnp.exp(last - run)
+            kept = remaining * weight_col
+
+            memory = memory_ref[m, h]
+            fresh = fresh_ref[m, :, own]
+            state_grad = state_ref[m, h]
+            probe_parts = parts(probes)
+            query_parts = parts(queries)
+            fresh_parts = parts(fresh)
+            memory_parts = parts(memory)
+            state_grad_parts = parts(state_grad)
+            products = mm_nt(parts(jnp.concatenate([queries, probes], 0)), probe_parts)
+            fade_query = jnp.where(col_index <= row_index, faded * products[:span], 0.0)
+            fade_probe = jnp.where(col_index < row_index, faded * products[span:], 0.0)
+            out_grad_parts = parts(out_grad)
+            probe_state = mm(probe_parts, state_grad_parts)
+            fresh_grad = (
+                mm(parts(jnp.transpose(fade_query * weight_row)), out_grad_parts)
+                + kept * probe_state
+            )
+            solved = mm(parts(jnp.transpose(inverse_ref[m, h])), parts(fresh_grad))
+            turned_queries = parts(jnp.transpose(queries))
+            turned_probes = parts(jnp.transpose(probes))
+            state_ref[m, h] = (
+                end_scale * state_grad
+                + mm(turned_queries, parts(scale_in * out_grad))
+                - mm(turned_probes, parts(scale_in * solved))
+            )
+            joined = parts(jnp.concatenate([out_grad, solved], 0))
+            outer = mm_nt(joined, fresh_parts)
+            mixing_grad = jnp.where(col_index <= row_index, outer[:span], 0.0)
+            strict_grad = jnp.where(col_index < row_index, -outer[span:], 0.0)
+            through = mm_nt(joined, memory_parts)
+            out_state = scale_in * through[:span]
+            solved_state = scale_in * through[span:]
+            spread = faded * weight_row
+            mix_fade = mixing_grad * spread
+            strict_fade = strict_grad * spread
+            on_probes = mm(parts(jnp.concatenate([mix_fade, strict_fade], 0)), probe_parts)
+            query_grad = out_state + on_probes[:span]
+            probe_grad = (
+                kept * mm_nt(fresh_parts, state_grad_parts)
+                - solved_state
+                + on_probes[span:]
+                + mm(parts(jnp.transpose(mix_fade)), query_parts)
+                + mm(parts(jnp.transpose(strict_fade)), probe_parts)
+            )
+            pairs = mixing_grad * fade_query + strict_grad * fade_probe
+            weighted_pairs = pairs * weight_row
+            probe_fresh = jnp.sum(probe_state * fresh, -1, keepdims=True)
+            run_col = (
+                jnp.sum(out_state * queries - solved_state * probes, -1, keepdims=True)
+                + jnp.sum(weighted_pairs, -1, keepdims=True)
+                - kept * probe_fresh
+            )
+            last_grad = jnp.sum(kept * probe_fresh, 0, keepdims=True) + end_scale * jnp.sum(
+                jnp.sum(state_grad * memory, -1, keepdims=True), 0, keepdims=True
+            )
+            run_col = run_col + jnp.where(row_index[:, 0:1] == span - 1, last_grad, 0.0)
+            col_terms = jnp.where(col_index == h, run_col, col_terms)
+            col_terms = jnp.where(col_index == heads + h, remaining * probe_fresh, col_terms)
+            row_terms = jnp.where(
+                row_index == h, -jnp.sum(weighted_pairs, 0, keepdims=True), row_terms
+            )
+            row_terms = jnp.where(
+                row_index == heads + h, jnp.sum(pairs, 0, keepdims=True), row_terms
+            )
+            active_grads[h] = unit_back(raw_queries, query_scale, query_grad) * head_size ** (-0.5)
+            active_grads[heads + h] = unit_back(raw_probes, probe_scale, probe_grad)
+            active_grads[2 * heads + h] = solved
+
+        terms = col_terms + jnp.transpose(row_terms)
+        decay_grad = ones_dot(ones_back, terms)
+        shifted_grad = decay_grad * -jnp.exp(param_ref[0:1, :]) * sigmoid(shifted_logit)
+        logit_grad = jnp.where(
+            col_index < heads,
+            shifted_grad,
+            jnp.where(col_index < 2 * heads, terms * strengths * (1.0 - strengths), 0.0),
+        )
+        logit_grad_ref[m] = logit_grad
+        decay_lane = col_index[0:1] < heads
+        param_grad_ref[0:1, :] += jnp.sum(
+            jnp.where(decay_lane, decay_grad * decays, 0.0), 0, keepdims=True
+        )
+        param_grad_ref[1:2, :] += jnp.sum(
+            jnp.where(decay_lane, shifted_grad, 0.0), 0, keepdims=True
+        )
+        conv_grad = jnp.concatenate(active_grads, 1) * (
+            opening * (1.0 + convolved * (1.0 - opening))
+        )
+        extended = jnp.concatenate([conv_grad, halo_ref[m]], 0)
+        halo_ref[m] = conv_grad[:8]
+        mixed_grad = jnp.zeros_like(conv_grad)
+        for j in range(tap_count):
+            reach = tap_count - 1 - j
+            mixed_grad = mixed_grad + taps[j : j + 1] * extended[reach : reach + span]
+            taps_grad_ref[j : j + 1, :] += jnp.sum(conv_grad * shifts[j], 0, keepdims=True)
+        error_ref[m] = jnp.concatenate([mixed_grad] + gate_grads, 1).astype(BF16)
+
+
+def run_forward(mixed, gate, logits, taps, params, gain, heads):
+    steps, seqs, span, _ = mixed.shape
+    head_size = gain.shape[1]
+    width = heads * head_size
+
+    def rows(columns):
+        return pl.BlockSpec((None, seqs, span, columns), lambda j: (j, 0, 0, 0))
+
+    def squares():
+        return pl.BlockSpec((None, seqs, heads, head_size, head_size), lambda j: (j, 0, 0, 0, 0))
+
+    def whole(array):
+        return pl.BlockSpec(array.shape, lambda j: (0, 0))
+
+    square = jax.ShapeDtypeStruct((steps, seqs, heads, head_size, head_size), F32)
+    lower = jax.ShapeDtypeStruct((steps, seqs, heads, span, span), F32)
+    flat = jax.ShapeDtypeStruct((steps, seqs, span, width), F32)
+    return pl.pallas_call(
+        mixer_forward,
+        grid=(steps,),
+        in_specs=[
+            rows(3 * width),
+            rows(width),
+            rows(logits.shape[-1]),
+            whole(taps),
+            whole(params),
+            whole(gain),
+        ],
+        out_specs=[rows(width), squares(), squares(), rows(width), rows(width)],
+        out_shape=[
+            jax.ShapeDtypeStruct((steps, seqs, span, width), BF16),
+            square,
+            lower,
+            flat,
+            flat,
+        ],
+        scratch_shapes=[
+            pltpu.VMEM((seqs, heads, head_size, head_size), F32),
+            pltpu.VMEM((seqs, 8, 3 * width), F32),
+        ],
+        compiler_params=pltpu.CompilerParams(vmem_limit_bytes=VMEM_LIMIT),
+        cost_estimate=pl.CostEstimate(
+            flops=steps * seqs * heads * 120 * span**3,
+            bytes_accessed=steps * seqs * span * width * 30,
+            transcendentals=0,
+        ),
+        name="mixer_forward",
+    )(mixed, gate, logits, taps, params, gain)
+
+
+def run_backward(mixed, gate, logits, taps, params, gain, memory, inverse, fresh, out, grad):
+    steps, seqs, span, _ = mixed.shape
+    heads, head_size = memory.shape[2], memory.shape[3]
+    width = heads * head_size
+    edge = 16
+
+    def rows(columns):
+        return pl.BlockSpec((None, seqs, span, columns), lambda j: (steps - 1 - j, 0, 0, 0))
+
+    def squares():
+        return pl.BlockSpec(
+            (None, seqs, heads, head_size, head_size), lambda j: (steps - 1 - j, 0, 0, 0, 0)
+        )
+
+    def whole(shape):
+        return pl.BlockSpec(shape, lambda j: (0, 0))
+
+    before = pl.BlockSpec(
+        (None, seqs, edge, 3 * width),
+        lambda j: (jnp.maximum(steps - 2 - j, 0), 0, span // edge - 1, 0),
+    )
+    return pl.pallas_call(
+        mixer_backward,
+        grid=(steps,),
+        in_specs=[
+            rows(3 * width),
+            before,
+            rows(width),
+            rows(logits.shape[-1]),
+            whole(taps.shape),
+            whole(params.shape),
+            whole(gain.shape),
+            squares(),
+            squares(),
+            rows(width),
+            rows(width),
+            rows(width),
+        ],
+        out_specs=[
+            rows(4 * width),
+            rows(logits.shape[-1]),
+            whole((8, 3 * width)),
+            whole((8, logits.shape[-1])),
+            whole((8, head_size)),
+        ],
+        out_shape=[
+            jax.ShapeDtypeStruct((steps, seqs, span, 4 * width), BF16),
+            jax.ShapeDtypeStruct(logits.shape, F32),
+            jax.ShapeDtypeStruct((8, 3 * width), F32),
+            jax.ShapeDtypeStruct((8, logits.shape[-1]), F32),
+            jax.ShapeDtypeStruct((8, head_size), F32),
+        ],
+        scratch_shapes=[
+            pltpu.VMEM((seqs, heads, head_size, head_size), F32),
+            pltpu.VMEM((seqs, 8, 3 * width), F32),
+        ],
+        compiler_params=pltpu.CompilerParams(vmem_limit_bytes=VMEM_LIMIT),
+        cost_estimate=pl.CostEstimate(
+            flops=steps * seqs * heads * 120 * span**3,
+            bytes_accessed=steps * seqs * span * width * 40,
+            transcendentals=0,
+        ),
+        name="mixer_backward",
+    )(mixed, mixed, gate, logits, taps, params, gain, memory, inverse, fresh, out, grad)
+
+
+def gather_rows(value, axis):
+    return lax.all_gather(value, axis, axis=0, tiled=True)
+
+
+def scatter_rows(value, axis):
+    return lax.psum_scatter(value, axis, scatter_dimension=0, tiled=True)
+
+
+def plane_peers():
+    me = lax.axis_index("seq")
+    sibling = me + 1 - 2 * (me % 2)
+    across = me + 2 - 4 * ((me // 2) % 2)
+    along = me + 4 - 8 * (me // 4)
+    return (me, sibling, across, along)
+
+
+def greet(peers):
+    barrier = pltpu.get_barrier_semaphore()
+    for peer in peers:
+        pl.semaphore_signal(
+            barrier, inc=1, device_id={"seq": peer}, device_id_type=pl.DeviceIdType.MESH
+        )
+    pl.semaphore_wait(barrier, len(peers))
+
+
+def send_to(peer, source, target, send_sem, recv_sem):
+    return pltpu.make_async_remote_copy(
+        src_ref=source,
+        dst_ref=target,
+        send_sem=send_sem,
+        recv_sem=recv_sem,
+        device_id={"seq": peer},
+        device_id_type=pl.DeviceIdType.MESH,
+    )
+
+
+def gather_phases(own_ref, all_ref, send_sems, recv_sems, local_sem, start):
+    me, sibling, across, along = plane_peers()
+    far = along + across - me
+    half = own_ref.shape[0] // 2
+    upper, lower = pl.ds(0, half), pl.ds(half, half)
+    copies = []
+
+    def send(peer, source, target):
+        k = start + len(copies)
+        copy = send_to(peer, source, target, send_sems.at[k], recv_sems.at[k])
+        copy.start()
+        copies.append(copy)
+
+    keep = pltpu.make_async_copy(own_ref, all_ref.at[me], local_sem)
+    keep.start()
+    send(across, own_ref, all_ref.at[me])
+    send(along, own_ref, all_ref.at[me])
+    send(sibling, own_ref, all_ref.at[me])
+    yield
+    copies[0].wait_recv()
+    send(along, all_ref.at[across, upper], all_ref.at[across, upper])
+    copies[1].wait_recv()
+    send(across, all_ref.at[along, lower], all_ref.at[along, lower])
+    send(sibling, all_ref.at[across], all_ref.at[across])
+    send(sibling, all_ref.at[along], all_ref.at[along])
+    yield
+    copies[3].wait_recv()
+    send(sibling, all_ref.at[far, upper], all_ref.at[far, upper])
+    copies[4].wait_recv()
+    send(sibling, all_ref.at[far, lower], all_ref.at[far, lower])
+    yield
+    for k in (2, 5, 6, 7, 8):
+        copies[k].wait_recv()
+    for copy in copies:
+        copy.wait_send()
+    keep.wait()
+    yield
+
+
+def plane_gather_kernel(own_ref, all_ref, send_sems, recv_sems, local_sem):
+    greet(plane_peers()[1:])
+    for _ in gather_phases(own_ref, all_ref, send_sems, recv_sems, local_sem, 0):
+        pass
+
+
+def chain_phases(all_ref, up_send, up_recv, down_send, down_recv):
+    depth = all_ref.shape[0]
+    place = lax.axis_index("dp")
+    above, below = lax.rem(place + 1, depth), lax.rem(place + depth - 1, depth)
+
+    def hop(slot, peer, send_sem, recv_sem):
+        return pltpu.make_async_remote_copy(
+            src_ref=all_ref.at[slot],
+            dst_ref=all_ref.at[slot],
+            send_sem=send_sem,
+            recv_sem=recv_sem,
+            device_id={"dp": peer},
+            device_id_type=pl.DeviceIdType.MESH,
+        )
+
+    ups, downs = [], []
+    for t in range(depth - 1):
+        up = hop(lax.rem(place + depth - t, depth), above, up_send.at[t], up_recv.at[t])
+        down = hop(lax.rem(place + t, depth), below, down_send.at[t], down_recv.at[t])
+        ups.append(up)
+        downs.append(down)
+        pl.when((place < depth - 1) & (place >= t))(up.start)
+        pl.when((place > 0) & (place + t < depth))(down.start)
+        yield
+        pl.when(place > t)(up.wait_recv)
+        pl.when(place + t + 1 < depth)(down.wait_recv)
+    for t in range(depth - 1):
+        pl.when((place < depth - 1) & (place >= t))(ups[t].wait_send)
+        pl.when((place > 0) & (place + t < depth))(downs[t].wait_send)
+    yield
+
+
+def exchange_copies(cut_ref, land, send_sems, recv_sems, start):
+    ring = cut_ref.shape[0]
+    me = lax.axis_index("seq")
+    copies = []
+    for k in range(1, ring):
+        peer = lax.rem(me + k, ring)
+        copy = send_to(
+            peer, cut_ref.at[peer], land, send_sems.at[start + k - 1], recv_sems.at[start + k - 1]
+        )
+        copy.start()
+        copies.append(copy)
+    return copies
+
+
+def plane_open_kernel(
+    first_ref,
+    second_ref,
+    early_ref,
+    later_ref,
+    first_all_ref,
+    second_all_ref,
+    early_all_ref,
+    later_all_ref,
+    send_sems,
+    recv_sems,
+    local_sems,
+    up_send,
+    up_recv,
+    down_send,
+    down_recv,
+):
+    place, me = lax.axis_index("dp"), lax.axis_index("seq")
+    depth, ring = early_all_ref.shape[0], early_ref.shape[0]
+    rows = early_ref.shape[1]
+    barrier = pltpu.get_barrier_semaphore()
+    for k in range(1, ring):
+        pl.semaphore_signal(
+            barrier,
+            inc=1,
+            device_id={"seq": lax.rem(me + k, ring)},
+            device_id_type=pl.DeviceIdType.MESH,
+        )
+    for k in range(1, depth):
+        pl.semaphore_signal(
+            barrier,
+            inc=1,
+            device_id={"dp": lax.rem(place + k, depth)},
+            device_id_type=pl.DeviceIdType.MESH,
+        )
+    pl.semaphore_wait(barrier, ring + depth - 2)
+    spot = early_all_ref.at[place, pl.ds(pl.multiple_of(me * rows, rows), rows)]
+    keep_early = pltpu.make_async_copy(early_ref.at[me], spot, local_sems.at[0])
+    keep_early.start()
+    keep_later = pltpu.make_async_copy(later_ref.at[me], later_all_ref.at[me], local_sems.at[1])
+    keep_later.start()
+    early = exchange_copies(early_ref, spot, send_sems, recv_sems, 0)
+    for copy in early:
+        copy.wait_recv()
+    keep_early.wait()
+    chain = chain_phases(early_all_ref, up_send, up_recv, down_send, down_recv)
+    first = gather_phases(first_ref, first_all_ref, send_sems, recv_sems, local_sems.at[2], ring)
+    second = gather_phases(
+        second_ref, second_all_ref, send_sems, recv_sems, local_sems.at[3], ring + 9
+    )
+    next(chain)
+    next(first)
+    next(first)
+    next(second)
+    later = exchange_copies(later_ref, later_all_ref.at[me], send_sems, recv_sems, ring + 18)
+    next(chain)
+    next(first)
+    next(chain)
+    next(second)
+    next(first)
+    next(second)
+    for copy in later:
+        copy.wait_recv()
+    next(chain)
+    next(second)
+    for copy in early + later:
+        copy.wait_send()
+    keep_later.wait()
+
+
+def plane_open(first, second, early, later, collective_id):
+    ring, depth = lax.axis_size("seq"), lax.axis_size("dp")
+    rows, columns = first.shape
+    total = 2 * ring + 18
+    return pl.pallas_call(
+        plane_open_kernel,
+        out_shape=[
+            jax.ShapeDtypeStruct((ring, rows, columns), first.dtype),
+            jax.ShapeDtypeStruct((ring, rows, columns), second.dtype),
+            jax.ShapeDtypeStruct((depth, ring * early.shape[1], early.shape[2]), early.dtype),
+            jax.ShapeDtypeStruct(later.shape, later.dtype),
+        ],
+        in_specs=[pl.BlockSpec(memory_space=pl.ANY)] * 4,
+        out_specs=[pl.BlockSpec(memory_space=pl.ANY)] * 4,
+        scratch_shapes=[
+            pltpu.SemaphoreType.DMA((total,)),
+            pltpu.SemaphoreType.DMA((total,)),
+            pltpu.SemaphoreType.DMA((4,)),
+        ]
+        + [pltpu.SemaphoreType.DMA((depth - 1,))] * 4,
+        compiler_params=pltpu.CompilerParams(collective_id=collective_id, has_side_effects=True),
+        name="plane_open",
+    )(first, second, early, later)
+
+
+def plane_gather(own, collective_id):
+    ring = lax.axis_size("seq")
+    rows, columns = own.shape
+    return pl.pallas_call(
+        plane_gather_kernel,
+        out_shape=jax.ShapeDtypeStruct((ring, rows, columns), own.dtype),
+        in_specs=[pl.BlockSpec(memory_space=pl.ANY)],
+        out_specs=pl.BlockSpec(memory_space=pl.ANY),
+        scratch_shapes=[
+            pltpu.SemaphoreType.DMA((9,)),
+            pltpu.SemaphoreType.DMA((9,)),
+            pltpu.SemaphoreType.DMA,
+        ],
+        compiler_params=pltpu.CompilerParams(collective_id=collective_id, has_side_effects=True),
+        name="plane_gather",
+    )(own)
+
+
+def plane_scatter_kernel(
+    part_ref,
+    sum_ref,
+    own_ref,
+    near_ref,
+    far_in_ref,
+    side_in_ref,
+    send_sems,
+    recv_sems,
+    load_sems,
+):
+    me, sibling, across, along = plane_peers()
+    far = along + across - me
+    flip = sibling - me
+    rows = sum_ref.shape[0]
+    half = rows // 2
+    upper, lower = pl.ds(0, half), pl.ds(half, half)
+    greet((sibling, across, along))
+    slabs = (far, across, along, me)
+    loads = []
+    nears = []
+    for k, slab in enumerate(slabs):
+        load = pltpu.make_async_copy(part_ref.at[slab], own_ref.at[k], load_sems.at[k])
+        load.start()
+        loads.append(load)
+        near = send_to(sibling, part_ref.at[slab + flip], near_ref.at[k], send_sems.at[k], recv_sems.at[k])
+        near.start()
+        nears.append(near)
+
+    def send(k, peer, source, target):
+        copy = send_to(peer, source, target, send_sems.at[k], recv_sems.at[k])
+        copy.start()
+        return copy
+
+    step = 32
+
+    def fold(target, other, start, count):
+        @pl.loop(0, count // step)
+        def _(i):
+            at = pl.ds(pl.multiple_of(start + i * step, step), step)
+            target[at] = (target[at].astype(F32) + other[at].astype(F32)).astype(BF16)
+
+    def join(k):
+        loads[k].wait()
+        nears[k].wait_recv()
+
+    join(0)
+    fold(own_ref.at[0], near_ref.at[0], 0, rows)
+    copies = [
+        send(4, across, own_ref.at[0, upper], far_in_ref.at[upper]),
+        send(5, along, own_ref.at[0, lower], far_in_ref.at[lower]),
+    ]
+    join(1)
+    fold(own_ref.at[1], near_ref.at[1], 0, rows)
+    copies.append(send(6, across, own_ref.at[1, upper], side_in_ref.at[0, upper]))
+    join(2)
+    fold(own_ref.at[2], near_ref.at[2], 0, rows)
+    copies.append(send(7, along, own_ref.at[2, lower], side_in_ref.at[1, lower]))
+    copies[0].wait_recv()
+    fold(own_ref.at[2], far_in_ref, 0, half)
+    copies.append(send(8, along, own_ref.at[2, upper], side_in_ref.at[1, upper]))
+    copies[1].wait_recv()
+    fold(own_ref.at[1], far_in_ref, half, half)
+    copies.append(send(9, across, own_ref.at[1, lower], side_in_ref.at[0, lower]))
+    join(3)
+    for copy in copies[2:]:
+        copy.wait_recv()
+
+    @pl.loop(0, rows // step)
+    def _(i):
+        at = pl.ds(pl.multiple_of(i * step, step), step)
+        sum_ref[at] = (
+            own_ref[3, at].astype(F32)
+            + near_ref[3, at].astype(F32)
+            + side_in_ref[0, at].astype(F32)
+            + side_in_ref[1, at].astype(F32)
+        )
+
+    for copy in nears + copies:
+        copy.wait_send()
+
+
+def plane_scatter(part, collective_id):
+    ring, rows, columns = part.shape
+    return pl.pallas_call(
+        plane_scatter_kernel,
+        out_shape=jax.ShapeDtypeStruct((rows, columns), F32),
+        in_specs=[pl.BlockSpec(memory_space=pl.ANY)],
+        out_specs=pl.BlockSpec(memory_space=pltpu.VMEM),
+        scratch_shapes=[
+            pltpu.VMEM((4, rows, columns), BF16),
+            pltpu.VMEM((4, rows, columns), BF16),
+            pltpu.VMEM((rows, columns), BF16),
+            pltpu.VMEM((2, rows, columns), BF16),
+            pltpu.SemaphoreType.DMA((10,)),
+            pltpu.SemaphoreType.DMA((10,)),
+            pltpu.SemaphoreType.DMA((4,)),
+        ],
+        compiler_params=pltpu.CompilerParams(
+            collective_id=collective_id, has_side_effects=True, vmem_limit_bytes=VMEM_LIMIT
+        ),
+        name="plane_scatter",
+    )(part)
+
+
+def small_sum_kernel(own_ref, all_ref, stage_ref, total_ref, send_sems, recv_sems):
+    depth, ring = stage_ref.shape[0], all_ref.shape[0]
+    place, me = lax.axis_index("dp"), lax.axis_index("seq")
+    barrier = pltpu.get_barrier_semaphore()
+    mesh_ids = pl.DeviceIdType.MESH
+    columns = [lax.rem(place + k, depth) for k in range(1, depth)]
+    plane = [lax.rem(me + k, ring) for k in range(1, ring)]
+    for peer in columns:
+        pl.semaphore_signal(barrier, inc=1, device_id={"dp": peer}, device_id_type=mesh_ids)
+    for peer in plane:
+        pl.semaphore_signal(barrier, inc=1, device_id={"seq": peer}, device_id_type=mesh_ids)
+    pl.semaphore_wait(barrier, depth + ring - 2)
+    first = []
+    for k, peer in enumerate(columns):
+        copy = pltpu.make_async_remote_copy(
+            src_ref=own_ref,
+            dst_ref=stage_ref.at[place],
+            send_sem=send_sems.at[k],
+            recv_sem=recv_sems.at[k],
+            device_id={"dp": peer},
+            device_id_type=mesh_ids,
+        )
+        copy.start()
+        first.append(copy)
+    stage_ref[place] = own_ref[...]
+    for copy in first:
+        copy.wait_recv()
+    total = stage_ref[0]
+    for k in range(1, depth):
+        total = total + stage_ref[k]
+    total_ref[...] = total
+    second = []
+    for k, peer in enumerate(plane):
+        copy = pltpu.make_async_remote_copy(
+            src_ref=total_ref,
+            dst_ref=all_ref.at[me],
+            send_sem=send_sems.at[depth - 1 + k],
+            recv_sem=recv_sems.at[depth - 1 + k],
+            device_id={"seq": peer},
+            device_id_type=mesh_ids,
+        )
+        copy.start()
+        second.append(copy)
+    all_ref[me] = total
+    for copy in second:
+        copy.wait_recv()
+    for copy in first + second:
+        copy.wait_send()
+
+
+def small_sum(own, collective_id):
+    depth, ring = lax.axis_size("dp"), lax.axis_size("seq")
+    count = depth + ring - 2
+    return pl.pallas_call(
+        small_sum_kernel,
+        out_shape=jax.ShapeDtypeStruct((ring,) + own.shape, F32),
+        in_specs=[pl.BlockSpec(memory_space=pltpu.VMEM)],
+        out_specs=pl.BlockSpec(memory_space=pltpu.VMEM),
+        scratch_shapes=[
+            pltpu.VMEM((depth,) + own.shape, F32),
+            pltpu.VMEM(own.shape, F32),
+            pltpu.SemaphoreType.DMA((count,)),
+            pltpu.SemaphoreType.DMA((count,)),
+        ],
+        compiler_params=pltpu.CompilerParams(collective_id=collective_id, has_side_effects=True),
+        name="small_sum",
+    )(own)
+
+
+def greet_plane(ring):
+    me = lax.axis_index("seq")
+    greet([lax.rem(me + k, ring) for k in range(1, ring)])
+
+
+def plane_exchange_kernel(count, *refs):
+    cuts, swaps = refs[:count], refs[count : 2 * count]
+    send_sems, recv_sems, local_sems = refs[2 * count :]
+    ring = cuts[0].shape[0]
+    me = lax.axis_index("seq")
+    greet_plane(ring)
+    copies, keeps = [], []
+    for k in range(count):
+        keep = pltpu.make_async_copy(cuts[k].at[me], swaps[k].at[me], local_sems.at[k])
+        keep.start()
+        keeps.append(keep)
+        copies += exchange_copies(cuts[k], swaps[k].at[me], send_sems, recv_sems, k * (ring - 1))
+    for copy in copies:
+        copy.wait_recv()
+    for copy in copies:
+        copy.wait_send()
+    for keep in keeps:
+        keep.wait()
+
+
+def plane_exchange(cuts, collective_id):
+    count = len(cuts)
+    total = count * (cuts[0].shape[0] - 1)
+    return pl.pallas_call(
+        functools.partial(plane_exchange_kernel, count),
+        out_shape=[jax.ShapeDtypeStruct(cut.shape, cut.dtype) for cut in cuts],
+        in_specs=[pl.BlockSpec(memory_space=pl.ANY)] * count,
+        out_specs=[pl.BlockSpec(memory_space=pl.ANY)] * count,
+        scratch_shapes=[
+            pltpu.SemaphoreType.DMA((total,)),
+            pltpu.SemaphoreType.DMA((total,)),
+            pltpu.SemaphoreType.DMA((count,)),
+        ],
+        compiler_params=pltpu.CompilerParams(collective_id=collective_id, has_side_effects=True),
+        name="plane_exchange",
+    )(*cuts)
+
+
+def rms_back(values, gain, grad):
+    scale = lax.rsqrt(jnp.mean(values * values, -1, keepdims=True) + 1e-05)
+    weighted = grad * gain
+    part = scale * weighted - values * (
+        scale * scale * scale * jnp.mean(weighted * values, -1, keepdims=True)
+    )
+    return (part, jnp.sum(grad * values * scale, 0))
+
+
+def low_dot(left, right, dims):
+    return lax.dot_general(left, right, (dims, ((), ())), preferred_element_type=F32)
+
+
+NN = ((1,), (0,))
+NT = ((1,), (1,))
+TN = ((0,), (0,))
+
+
+def split_heads_device(
+    inputs,
+    lengths,
+    first_gain,
+    input_weight,
+    decay_weight,
+    conv_weight,
+    decay_log,
+    decay_bias,
+    head_gain,
+    output_weight,
+    second_gain,
+    gate_up_weight,
+    down_weight,
+    cotangent,
+):
+    micro_count, seq_local, span, model_width = inputs.shape
+    ring = lax.axis_size("seq")
+    depth = lax.axis_size("dp")
+    rank = lax.axis_index("seq")
+    seqs = micro_count * seq_local
+    row_count = seqs * span
+    all_rows = ring * row_count
+    head_count = decay_log.shape[0]
+    heads = head_count // ring
+    head_size = head_gain.shape[0]
+    key_width = head_count * head_size
+    width = heads * head_size
+    own_units = down_weight.shape[0]
+    units = depth * own_units
+    weight_rows = input_weight.shape[0]
+    tap_count = conv_weight.shape[0]
+
+    tokens = inputs.reshape(row_count, model_width).astype(F32)
+    positions = rank * span + lax.broadcasted_iota(jnp.int32, (micro_count, seq_local, span), 2)
+    valid_rows = (positions < lengths[:, :, None]).astype(F32).reshape(row_count, 1)
+    normed_low = rms_norm(tokens, first_gain).astype(BF16)
+
+    in_cut = jnp.transpose(input_weight.reshape(weight_rows, 4, ring, width), (2, 0, 1, 3))
+    gate_up_cut = jnp.transpose(
+        gate_up_weight.reshape(weight_rows, 2, depth, ring, own_units), (3, 1, 0, 2, 4)
+    ).reshape(ring, 2, weight_rows, units)
+    upstream = valid_rows * cotangent.reshape(row_count, model_width).astype(F32)
+    out_err = upstream.astype(BF16)
+    normed_all, out_err_all, in_own, gate_up_cut = plane_open(
+        normed_low,
+        out_err,
+        in_cut.reshape(ring, weight_rows, 4 * width),
+        gate_up_cut.reshape(ring, 2 * weight_rows, units),
+        1,
+    )
+    gate_up_cut = gate_up_cut.reshape(ring, 2, weight_rows, units)
+    normed_all = normed_all.reshape(all_rows, model_width)
+    out_err_all = out_err_all.reshape(all_rows, model_width)
+    in_own = in_own.reshape(model_width, 4 * width)
+    in_own, output_weight, down_weight = lax.optimization_barrier(
+        (in_own, output_weight, down_weight)
+    )
+    turns = [(depth * s + z, ring * z + s) for s in range(ring) for z in range(depth)]
+    out_own = gather_rows(lax.ppermute(output_weight, ("dp", "seq"), turns), "dp")
+    gate_own = gather_rows(gate_up_cut[:, 0].reshape(ring * weight_rows, units), "dp")
+    up_own = gather_rows(gate_up_cut[:, 1].reshape(ring * weight_rows, units), "dp")
+    down_own = gather_rows(down_weight, "dp")
+
+    def own_lanes(pair):
+        rows = pair.shape[0]
+        decay_part = lax.dynamic_slice(pair, (0, rank * heads), (rows, heads))
+        other = pair.shape[1] - head_count
+        if other:
+            strength_part = lax.dynamic_slice(pair, (0, head_count + rank * heads), (rows, heads))
+            decay_part = jnp.concatenate([decay_part, strength_part], 1)
+        return jnp.pad(decay_part, ((0, 0), (0, 128 - decay_part.shape[1])))
+
+    decay_own = own_lanes(decay_weight)
+    params = jnp.pad(own_lanes(jnp.stack([decay_log, decay_bias])), ((0, 6), (0, 0)))
+    taps = lax.dynamic_slice(
+        conv_weight.reshape(tap_count, 3, key_width), (0, 0, rank * width), (tap_count, 3, width)
+    ).reshape(tap_count, 3 * width)
+    gain = head_gain.reshape(1, head_size)
+
+    def chunks(value):
+        return value.reshape(ring, seqs, span, value.shape[-1])
+
+    mixed = chunks(low_dot(normed_all, in_own[:, : 3 * width], NN).astype(BF16))
+    gate_raw = chunks(low_dot(normed_all, in_own[:, 3 * width :], NN))
+    logits = chunks(low_dot(normed_all, decay_own, NN))
+    gated, memory, inverse, fresh, mixer_out = run_forward(
+        mixed, gate_raw, logits, taps, params, gain, heads
+    )
+    gated_rows = gated.reshape(all_rows, width)
+    hidden_part = low_dot(gated_rows, out_own, NN).astype(BF16)
+    hidden = tokens + plane_scatter(hidden_part.reshape(ring, row_count, model_width), 2)
+    second_low = rms_norm(hidden, second_gain).astype(BF16)
+    second_all = plane_gather(second_low, 3).reshape(all_rows, model_width)
+    gate_part = low_dot(second_all, gate_own, NN)
+    up_part = low_dot(second_all, up_own, NN)
+    gate_open = jax.nn.sigmoid(gate_part)
+    activated = (gate_part * gate_open * up_part).astype(BF16)
+    down_part = low_dot(activated, down_own, NN).astype(BF16)
+
+    down_term = low_dot(activated, out_err_all, TN).astype(BF16)
+    down_term, out_err_all = lax.optimization_barrier((down_term, out_err_all))
+    activated_grad = low_dot(out_err_all, down_own, NT)
+    gate_err = (
+        activated_grad * up_part * gate_open * (1.0 + gate_part * (1.0 - gate_open))
+    ).astype(BF16)
+    up_err = (activated_grad * gate_part * gate_open).astype(BF16)
+    gate_term = low_dot(second_all, gate_err, TN).astype(BF16)
+    up_term = low_dot(second_all, up_err, TN).astype(BF16)
+    gate_term, up_term, gate_err, up_err = lax.optimization_barrier(
+        (gate_term, up_term, gate_err, up_err)
+    )
+    second_part = (low_dot(gate_err, gate_own, NT) + low_dot(up_err, up_own, NT)).astype(BF16)
+    second_grad = plane_scatter(second_part.reshape(ring, row_count, model_width), 4)
+    down_share = scatter_rows(down_term, "dp").astype(F32)
+    result = valid_rows * (hidden + plane_scatter(down_part.reshape(ring, row_count, model_width), 5))
+    gate_share = scatter_rows(gate_term, "dp")
+    up_share = scatter_rows(up_term, "dp")
+    hidden_part, second_gain_grad = rms_back(hidden, second_gain, second_grad)
+    hidden_grad = upstream + hidden_part
+    branch_err = hidden_grad.astype(BF16)
+    branch_all = plane_gather(branch_err, 11).reshape(all_rows, model_width)
+    output_term = low_dot(gated_rows, branch_all, TN).astype(BF16)
+    gated_grad = low_dot(branch_all, out_own, NT).astype(BF16)
+    output_term, gated_grad = lax.optimization_barrier((output_term, gated_grad))
+    output_term, down_share, gate_share, up_share = lax.optimization_barrier(
+        (output_term, down_share, gate_share, up_share)
+    )
+    output_share = lax.ppermute(
+        scatter_rows(output_term, "dp"), ("dp", "seq"), [(b, a) for a, b in turns]
+    ).astype(F32)
+    gate_share, up_share = plane_exchange(
+        [
+            gate_share.reshape(ring, weight_rows, units),
+            up_share.reshape(ring, weight_rows, units),
+        ],
+        9,
+    )
+    gate_up_share = jnp.stack([gate_share, up_share], 1)
+    gate_up_share = jnp.transpose(
+        gate_up_share.reshape(ring, 2, weight_rows, depth, own_units), (2, 1, 3, 0, 4)
+    )
+    gate_up_share = gate_up_share.reshape(weight_rows, -1).astype(F32)
+
+    in_err, logit_grad, taps_grad, param_grad, gain_grad = run_backward(
+        mixed,
+        gate_raw,
+        logits,
+        taps,
+        params,
+        gain,
+        memory,
+        inverse,
+        fresh,
+        mixer_out,
+        gated_grad.reshape(ring, seqs, span, width),
+    )
+    in_err = in_err.reshape(all_rows, 4 * width)
+    logit_grad = logit_grad.reshape(all_rows, -1)
+    input_term = low_dot(normed_all, in_err, TN).astype(BF16)
+    input_term, in_err, logit_grad = lax.optimization_barrier((input_term, in_err, logit_grad))
+    (input_share,) = plane_exchange(
+        [scatter_rows(input_term, "dp").reshape(ring, weight_rows, 4 * width)], 10
+    )
+    input_share = jnp.transpose(
+        input_share.reshape(ring, weight_rows, 4, width), (1, 2, 0, 3)
+    )
+    input_share = input_share.reshape(weight_rows, -1).astype(F32)
+    logit_top, logit_rest = parts(logit_grad)
+    normed_part = (
+        low_dot(in_err, in_own, NT)
+        + low_dot(logit_top, decay_own, NT)
+        + low_dot(logit_rest, decay_own, NT)
+    ).astype(BF16)
+    normed_grad = plane_scatter(normed_part.reshape(ring, row_count, model_width), 6)
+    token_part, first_gain_grad = rms_back(tokens, first_gain, normed_grad)
+    inputs_grad = hidden_grad + token_part
+    decay_term = (low_dot(normed_all, logit_top, TN) + low_dot(normed_all, logit_rest, TN))[
+        :, : 2 * heads
+    ]
+
+    pieces = [
+        jnp.transpose(decay_term),
+        taps_grad[:tap_count],
+        param_grad[:2, : 2 * heads],
+        first_gain_grad,
+        second_gain_grad,
+        gain_grad[0],
+    ]
+    sizes = [piece.size for piece in pieces]
+    packed = jnp.concatenate([piece.reshape(-1) for piece in pieces])
+    packed = jnp.pad(packed, (0, -packed.size % 1024)).reshape(-1, 128)
+    summed = small_sum(packed, 7).reshape(ring, -1)
+    parted = []
+    start = 0
+    for size in sizes:
+        parted.append(summed[:, start : start + size])
+        start += size
+    decay_sum, taps_sum, param_sum = parted[:3]
+    first_gain_grad, second_gain_grad, gain_grad = [part.sum(0) for part in parted[3:]]
+    decay_sum = decay_sum.reshape(ring, 2, heads, model_width)
+    decay_weight_grad = jnp.transpose(decay_sum, (3, 1, 0, 2)).reshape(model_width, 2 * head_count)
+    taps_sum = jnp.transpose(taps_sum.reshape(ring, tap_count, 3, width), (1, 2, 0, 3))
+    param_sum = jnp.transpose(param_sum.reshape(ring, 2, 2 * heads)[..., :heads], (1, 0, 2))
+    param_sum = param_sum.reshape(2, head_count)
+    return (
+        result.reshape(inputs.shape),
+        inputs_grad.reshape(inputs.shape),
+        first_gain_grad,
+        input_share,
+        decay_weight_grad,
+        taps_sum.reshape(tap_count, 3 * key_width),
+        param_sum[0],
+        param_sum[1],
+        gain_grad,
+        output_share,
+        second_gain_grad,
         gate_up_share,
         down_share,
     )
@@ -348,6 +1512,12 @@
         P(("dp", "seq"), None),
         P(("dp", "seq"), None),
     )
+    ring = mesh.shape["seq"]
+
+    def whole_device(*arrays):
+        heads_divide = ring == 8 and arrays[6].shape[0] % ring == 0
+        return (split_heads_device if heads_divide else per_device)(*arrays)
+
     return jax.shard_map(
-        per_device, mesh=mesh, in_specs=in_specs, out_specs=out_specs, check_vma=False
-    )
+        whole_device, mesh=mesh, in_specs=in_specs, out_specs=out_specs, check_vma=False
+    )

time: 3820 us -> 874 us (0.23)
  waiting for transfers between devices: 2740 us -> 7.83 us
  Pallas kernels: 0 us -> 548 us
  matrix products: 617 us -> 207 us
  other arithmetic: 146 us -> 21.7 us
  local copies, waits for them, and re-layouts: 155 us -> 60.5 us
  blocking collectives: 51.1 us -> 0 us
  loops' own time: 44.9 us -> 0 us
  starting transfers between devices: 45.5 us -> 4.61 us
    reduce_scatter x4 -> x5, waiting for transfers between devices: 2280 us -> 0.03 us  [scatter_rows(): return lax.psum_scatter(value, axis, scatter_dimension=0, tiled=True)]
    pallas_call x0 -> x12, Pallas kernels: none -> 548 us  [the longest x4 170 us: plane_scatter(): pl.pallas_call(plane_scatter_kernel, out_shape=jax.ShapeDtypeStruct((rows...]
    dot_general x165 -> x21, matrix products: 617 us -> 207 us  [low_dot(): lax.dot_general(left, right, (dims, ((), ())), preferred_element_type=F32)]
    ppermute x16 -> x2, waiting for transfers between devices: 266 us -> 5.77 us  [the longest x1 5.76 us: split_heads_device(): lax.ppermute(output_weight, ('dp', 'seq'), turns)]
    all_gather x4, waiting for transfers between devices: 190 us -> 0.04 us  [gather_rows(): return lax.all_gather(value, axis, axis=0, tiled=True)]
    while x367 -> x0, local copies, waits for them, and re-layouts: 56.3 us -> none
    psum x1 -> x0, blocking collectives: 51.1 us -> none  [per_device(): lax.psum((first_gain_grad, decay_weight_grad, conv_grad, decay_log_grad,...]
    another operation x5 -> x0, loops' own time: 44.9 us -> none  [the longest x3 44.8 us: delta_local(): memory, outputs = lax.scan(span_step, memory, pieces)]
  transfers between devices with their start and end apart: 25 -> 11, of which waited for: 20 -> 1; matrix products, arithmetic and copies ran while one was open for 13% -> 29% of each run, Pallas kernels for 0% -> 49%
where the time goes in v1:
time: 874 us; the launch traced here: 865 us
  Pallas kernels  548 us (63%)
  matrix products  207 us (24%)
  local copies, waits for them, and re-layouts  60.5 us (7%)
  other arithmetic  21.7 us (2%)
  between operations  14.8 us (2%)
    dot_general x21, matrix products, low_dot(): lax.dot_general(left, right, (dims, ((), ())), preferred_element_type=F32)  207 us
    pallas_call x4, Pallas kernels, plane_scatter(): pl.pallas_call(plane_scatter_kernel, out_shape=jax.ShapeDtypeStruct((rows...  170 us
    pallas_call x1, Pallas kernels, plane_open(): pl.pallas_call(plane_open_kernel, out_shape=[jax.ShapeDtypeStruct((ring,...  109 us
    pallas_call x2, Pallas kernels, plane_gather(): pl.pallas_call(plane_gather_kernel, out_shape=jax.ShapeDtypeStruct((ring,...  83.6 us
    pallas_call x1, Pallas kernels, run_forward(): pl.pallas_call(mixer_forward, grid=(steps,), in_specs=[rows(3 * width), r...  75.4 us
    pallas_call x1, Pallas kernels, run_backward(): pl.pallas_call(mixer_backward, grid=(steps,), in_specs=[rows(3 * width),...  53 us
    pallas_call x2, Pallas kernels, plane_exchange(): pl.pallas_call(functools.partial(plane_exchange_kernel, count), out_shape...  40.8 us
  transfers between devices with their start and end apart: 11, of which 1 were waited for; matrix products, arithmetic and copies ran while one was open for 29% of the time, Pallas kernels for 49%

profile of v1, /device:TPU:1, one launch (start us, length us, event | category | flops | bytes accessed | tf_op | source)
XLA Modules:
  0.0 864.8 jit_solution(11807223245043907493)
XLA Ops:
  7.3 1.5 fusion.3
  9.3 1.6 copy.71
  11.3 1.5 reshape.246.early_ref
  12.9 5.0 reshape.247
  17.9 2.7 copy.80
  20.6 2.7 reshape_reshape.3.later_ref
  23.4 2.9 fusion.2
  26.3 109.3 %plane_open.1 = (bf16[8,256,2048]{2,1,0:T(8,128)(2,1)}, bf16[8,256,2048]{2,1,0:T(8,128)(2,1)}, bf16[4,512,1024]{2,1,0:T(8,128)(2,1)}, bf16[8,128,704]{2,1,0:T(8,128)(2,1)}) custom-call(bf16[256,2048]{1,0:T(8,128)(2,1)} %get-tuple-element.142.first_ref, bf16[256,2048]{1,0:T(8,128)(2,1)} %get-tuple-element.141.second_ref, ...), custom_call_target="tpu_custom_call" | custom-call | tf_op jit(solution)/shard_map/plane_open/pallas_call | solution.py:987
  135.7 1.9 collective-permute-start
  137.6 5.8 collective-permute-done
  144.2 2.7 fusion.32
  149.4 5.9 fusion.14.logit_ref
  155.4 7.4 fusion.11.gate_ref
  162.8 8.2 convolution_convert_fusion.3
  171.8 75.4 %mixer_forward.1 = (bf16[8,2,128,256]{3,2,1,0:T(8,128)(2,1)S(1)}, f32[8,2,2,128,128]{4,3,2,1,0:T(8,128)S(1)}, f32[8,2,2,128,128]{4,3,2,1,0:T(8,128)}, f32[8,2,128,256]{3,2,1,0:T(8,128)}, f32[8,2,128,256]{3,2,1,0:T(8,128)}) custom-call(bf16[8,2,128,768]{3,2,1,0:T(8,128)(2,1)} %bitcast.220, f32[8,2,128,256]{3,2,1,0:T(8,128)} %fusion.11.gate_ref, ...), custom_call_target="tpu_custom_call" | custom-call | flops 8053063680 | bytes 15728640 | tf_op jit(solution)/shard_map/mixer_forward/pallas_call | solution.py:687
  247.7 1.3 copy-done.11
  249.1 7.2 convolution_convert_fusion.1
  256.3 48.4 %plane_scatter.4 = f32[256,2048]{1,0:T(8,128)S(1)} custom-call(bf16[8,256,2048]{2,1,0:T(8,128)(2,1)} %bitcast.165), custom_call_target="tpu_custom_call" | custom-call | tf_op jit(solution)/shard_map/plane_scatter/pallas_call | solution.py:1110
  305.4 1.2 multiply_convert_fusion.3.own_ref
  306.6 42.9 %plane_gather.2 = bf16[8,256,2048]{2,1,0:T(8,128)(2,1)} custom-call(bf16[256,2048]{1,0:T(8,128)(2,1)} %multiply_convert_fusion.3.own_ref), custom_call_target="tpu_custom_call" | custom-call | tf_op jit(solution)/shard_map/plane_gather/pallas_call | solution.py:1011
  349.6 11.5 %fusion.34 = f32[2048,704]{0,1:T(8,128)} fusion(bf16[2048,2048]{1,0:T(8,128)(2,1)} %bitcast.177, bf16[2048,704]{1,0:T(8,128)(2,1)} %all-gather.7.cloned.1.call-done), kind=kOutput, calls=%fused_computation.85 | convolution fusion | flops 5905580032 | bytes 17039360 | tf_op jit(solution)/shard_map/dot_general | solution.py:1253
  361.1 12.8 %multiply_convert_fusion.2 = (bf16[2048,704]{0,1:T(8,128)(2,1)S(1)}, f32[2048,704]{0,1:T(8,128)}) fusion(f32[2048,704]{0,1:T(8,128)} %fusion.34, bf16[2048,2048]{1,0:T(8,128)(2,1)} %bitcast.178, bf16[2048,704]{1,0:T(8,128)(2,1)} %all-gather.9.cloned.1.call-done), kind=kOutput, calls=%fused_computation.6 | convolution fusion | flops 5914230784 | bytes 25690112 | tf_op jit(solution)/shard_map/dot_general | solution.py:1253
  373.9 1.5 copy-done.42
  375.5 10.8 %convolution_convert_fusion.6 = bf16[704,2048]{1,0:T(8,128)(2,1)} fusion(bf16[2048,704]{0,1:T(8,128)(2,1)S(1)} %get-tuple-element.139, bf16[2048,2048]{1,0:T(8,128)(2,1)} %bitcast.213), kind=kOutput, calls=%fused_computation.13 | convolution fusion | flops 5907021824 | bytes 14155776 | tf_op jit(solution)/shard_map/dot_general | solution.py:1253
  386.4 15.5 %multiply_convert_fusion = (bf16[2048,704]{0,1:T(8,128)(2,1)S(1)}, bf16[2048,704]{0,1:T(8,128)(2,1)}) fusion(f32[2048,704]{0,1:T(8,128)} %fusion.34, f32[2048,704]{0,1:T(8,128)} %get-tuple-element.140, bf16[2048,2048]{1,0:T(8,128)(2,1)} %bitcast.214, bf16[704,2048]{1,0:T(8,128)(2,1)} %all-gather.11.cloned.1.call-done), kind=kOutput, calls=%fused_computation.4 | convolution fusion | flops 5924323328 | bytes 28573696 | tf_op jit(solution)/shard_map/dot_general | solution.py:1253
  401.9 1.6 copy-done.40
  403.5 10.9 %convolution_convert_fusion.4 = bf16[2048,704]{0,1:T(8,128)(2,1)} fusion(bf16[2048,704]{0,1:T(8,128)(2,1)S(1)} %get-tuple-element.57, bf16[2048,2048]{1,0:T(8,128)(2,1)} %bitcast.179), kind=kOutput, calls=%fused_computation.11 | convolution fusion | flops 5907021824 | bytes 14155776 | tf_op jit(solution)/shard_map/dot_general | solution.py:1253
  414.4 10.6 %convolution_convert_fusion.5 = bf16[2048,704]{0,1:T(8,128)(2,1)} fusion(bf16[2048,704]{0,1:T(8,128)(2,1)} %get-tuple-element.56, bf16[2048,2048]{1,0:T(8,128)(2,1)} %bitcast.180), kind=kOutput, calls=%fused_computation.12 | convolution fusion | flops 5907021824 | bytes 14155776 | tf_op jit(solution)/shard_map/dot_general | solution.py:1253
  425.8 13.1 %fusion.35 = f32[2048,2048]{1,0:T(8,128)} fusion(bf16[2048,704]{0,1:T(8,128)(2,1)} %get-tuple-element.56, bf16[2048,704]{1,0:T(8,128)(2,1)} %all-gather.7.cloned.1.call-done), kind=kOutput, calls=%fused_computation.86 | convolution fusion | flops 5905580032 | bytes 22544384 | tf_op jit(solution)/shard_map/dot_general | solution.py:1253
  438.9 9.1 %convolution_convert_fusion = bf16[2048,2048]{1,0:T(8,128)(2,1)} fusion(bf16[2048,704]{0,1:T(8,128)(2,1)S(1)} %copy-done.43, bf16[704,2048]{1,0:T(8,128)(2,1)S(1)} %copy-done.37), kind=kOutput, calls=%fused_computation.2 | convolution fusion | flops 5909774336 | bytes 14155776 | tf_op jit(solution)/shard_map/dot_general | solution.py:1253
  448.0 40.0 %plane_scatter.5 = f32[256,2048]{1,0:T(8,128)S(1)} custom-call(bf16[8,256,2048]{2,1,0:T(8,128)(2,1)} %bitcast.176), custom_call_target="tpu_custom_call" | custom-call | tf_op jit(solution)/shard_map/plane_scatter/pallas_call | solution.py:1110
  488.1 12.6 %add_convert_fusion.1 = bf16[2048,2048]{1,0:T(8,128)(2,1)} fusion(f32[2048,2048]{1,0:T(8,128)} %fusion.35, bf16[2048,704]{0,1:T(8,128)(2,1)S(1)} %copy-done.41, bf16[2048,704]{1,0:T(8,128)(2,1)S(1)} %copy-done.36), kind=kOutput, calls=%fused_computation.1 | convolution fusion | flops 5913968640 | bytes 30932992 | tf_op jit(solution)/shard_map/dot_general | solution.py:1253
  500.7 41.0 %plane_scatter.6 = f32[256,2048]{1,0:T(8,128)S(1)} custom-call(bf16[8,256,2048]{2,1,0:T(8,128)(2,1)} %bitcast.175), custom_call_target="tpu_custom_call" | custom-call | tf_op jit(solution)/shard_map/plane_scatter/pallas_call | solution.py:1110
  542.9 3.2 fusion.30
  546.2 40.7 %plane_gather.3 = bf16[8,256,2048]{2,1,0:T(8,128)(2,1)} custom-call(bf16[256,2048]{1,0:T(8,128)(2,1)} %get-tuple-element.126.own_ref), custom_call_target="tpu_custom_call" | custom-call | tf_op jit(solution)/shard_map/plane_gather/pallas_call | solution.py:1011
  586.9 6.7 convolution_convert_fusion.8
  593.6 6.0 convolution_convert_fusion.7
  599.6 2.4 convert_element_type.157
  602.1 1.6 copy-done.10
  603.7 53.0 %mixer_backward.1 = (bf16[8,2,128,1024]{3,2,1,0:T(8,128)(2,1)}, f32[8,2,128,128]{3,2,1,0:T(8,128)S(1)}, f32[8,768]{1,0:T(8,128)S(1)}, f32[8,128]{1,0:T(8,128)S(1)}, f32[8,128]{1,0:T(8,128)S(1)}) custom-call(bf16[8,2,128,768]{3,2,1,0:T(8,128)(2,1)} %bitcast.221, bf16[8,2,128,768]{3,2,1,0:T(8,128)(2,1)} %bitcast.222, f32[8,2,128,256]{3,2,1,0:T(8,128)S(1)} %copy-done.10, ...), custom_call_target="tpu_custom_call" | custom-call | flops 8053063680 | bytes 20971520 | tf_op jit(solution)/shard_map/mixer_backward/pallas_call | solution.py:741
  656.8 14.2 %convolution_convert_fusion.2 = bf16[2048,1024]{1,0:T(8,128)(2,1)} fusion(bf16[2048,2048]{1,0:T(8,128)(2,1)} %bitcast.168, bf16[2048,1024]{1,0:T(8,128)(2,1)} %bitcast.218), kind=kOutput, calls=%fused_computation.9 | convolution fusion | flops 8592031744 | bytes 16777216 | tf_op jit(solution)/shard_map/dot_general | solution.py:1253
  671.1 4.7 fusion.23
  675.8 4.8 fusion.26
  680.6 8.1 fusion.17
  688.7 11.7 %fusion.36 = f32[2048,2048]{1,0:T(8,128)} fusion(bf16[2048,1024]{1,0:T(8,128)(2,1)S(1)} %bitcast.219, bf16[2048,1024]{1,0:T(8,128)(2,1)S(1)} %bitcast.217), kind=kOutput, calls=%fused_computation.87 | convolution fusion | flops 8589934592 | bytes 25165824 | tf_op jit(solution)/shard_map/dot_general | solution.py:1253
  700.4 15.5 %add_convert_fusion = bf16[2048,2048]{1,0:T(8,128)(2,1)} fusion(f32[2048,2048]{1,0:T(8,128)} %fusion.36, f32[2048,2048]{1,0:T(8,128)} %fusion.17, bf16[2048,4]{1,0:T(8,128)(2,1)S(1)} %copy-done.16, f32[2048,128]{1,0:T(8,128)S(1)} %bitcast.155), kind=kOutput, calls=%fused_computation | convolution fusion | flops 1087373312 | bytes 43008000 | tf_op jit(solution)/shard_map/dot_general | solution.py:1253
  715.9 40.6 %plane_scatter.7 = f32[256,2048]{1,0:T(8,128)S(1)} custom-call(bf16[8,256,2048]{2,1,0:T(8,128)(2,1)} %bitcast.174), custom_call_target="tpu_custom_call" | custom-call | tf_op jit(solution)/shard_map/plane_scatter/pallas_call | solution.py:1110
  757.9 15.8 %small_sum.1 = f32[8,128,128]{2,1,0:T(8,128)} custom-call(f32[128,128]{1,0:T(8,128)} %pad_bitcast_fusion.own_ref), custom_call_target="tpu_custom_call" | custom-call | tf_op jit(solution)/shard_map/small_sum/pallas_call | solution.py:1184
  773.7 1.4 copy.82
  775.9 1.7 slice_reduce_fusion
  777.6 3.4 fusion.8
  781.0 2.3 collective-permute-start.1
  783.4 1.3 slice_reduce_fusion.2
  789.7 2.3 copy.63
  793.1 25.8 %plane_exchange.3 = (bf16[8,64,704]{2,1,0:T(8,128)(2,1)}, bf16[8,64,704]{2,1,0:T(8,128)(2,1)}) custom-call(bf16[8,64,704]{2,1,0:T(8,128)(2,1)} %bitcast.186, bf16[8,64,704]{2,1,0:T(8,128)(2,1)} %bitcast.187), custom_call_target="tpu_custom_call" | custom-call | tf_op jit(solution)/shard_map/plane_exchange/pallas_call | solution.py:1228
  818.9 3.2 stack.21
  822.1 3.0 stack.22
  825.1 1.5 convert_bitcast_fusion
  826.6 4.4 copy.65
  831.0 5.5 reshape.285
  837.3 15.0 %plane_exchange.2 = bf16[8,64,1024]{2,1,0:T(8,128)(2,1)} custom-call(bf16[8,64,1024]{2,1,0:T(8,128)(2,1)} %bitcast.201), custom_call_target="tpu_custom_call" | custom-call | tf_op jit(solution)/shard_map/plane_exchange/pallas_call | solution.py:1228
  852.3 2.0 reshape.286
  854.3 1.2 copy.58
  855.5 2.5 copy.74
  (158 shorter events, 17.9 us)
Async XLA Ops:
  7.2 164.0 %copy-start = (f32[4,6144]{1,0:T(4,128)S(1)}, f32[4,6144]{1,0:T(4,128)}, u32[]{:S(2)}) copy-start(f32[4,6144]{1,0:T(4,128)} %param.19) | copy-start | bytes 294916
  7.2 241.9 %all-gather.5.cloned.1.call-start = ((), (), s32[]{:S(2)}) async-start(), calls=%async_computation.5 | async-start | bytes 1310720 | tf_op jit(solution)/shard_map/all_gather | solution.py:787
  8.8 0.5 copy-start.27
  9.3 14.1 %copy-start.25 = (f32[256]{0:T(256)}, f32[256]{0:T(256)S(1)}, u32[]{:S(2)}) copy-start(f32[256]{0:T(256)S(1)} %rsqrt_bitcast_fusion) | copy-start | bytes 3076
  9.3 3.6 copy-start.19
  17.9 5.4 copy-start.31
  17.9 5.5 copy-start.12
  17.9 5.5 copy-start.23
  23.4 112.3 %copy-start.29 = (f32[2,1,1,128]{3,2,1,0:T(1,128)}, f32[2,1,1,128]{3,2,1,0:T(1,128)S(1)}, u32[]{:S(2)}) copy-start(f32[2,1,1,128]{3,2,1,0:T(1,128)S(1)} %compare_convert_fusion) | copy-start | bytes 3076
  26.3 109.3 %copy-start.38 = (bf16[64,2048]{1,0:T(8,128)(2,1)S(1)}, bf16[64,2048]{1,0:T(8,128)(2,1)}, u32[]{:S(2)}) copy-start(bf16[64,2048]{1,0:T(8,128)(2,1)} %param.23) | copy-start | bytes 786436
  135.7 7.7 collective-permute-start
  143.4 0.7 copy-start.21
  144.1 205.5 %all-gather.7.cloned.1.call-start = ((), (), s32[]{:S(2)}) async-start(), calls=%async_computation.6 | async-start | bytes 3932160 | tf_op jit(solution)/shard_map/all_gather | solution.py:787
  146.8 214.3 %all-gather.9.cloned.1.call-start = ((), (), s32[]{:S(2)}) async-start(), calls=%async_computation.7 | async-start | bytes 3932160 | tf_op jit(solution)/shard_map/all_gather | solution.py:787
  147.6 238.8 %all-gather.11.cloned.1.call-start = ((), (), s32[]{:S(2)}) async-start(), calls=%async_computation.8 | async-start | bytes 3604480 | tf_op jit(solution)/shard_map/all_gather | solution.py:787
  148.1 451.5 %reduce-scatter.8.cloned.1.call-start = ((), (), s32[]{:S(2)}) async-start(), calls=%async_computation.10 | async-start | bytes 3604480 | tf_op jit(solution)/shard_map/reduce_scatter | solution.py:791
  149.4 6.0 copy-start.15
  149.4 6.0 copy-start.34
  149.4 13.4 %slice-start = ((s8[8388608]{0:T(1024)(128)(4,1)}), s8[4194304]{0:T(1024)(128)(4,1)S(1)}, s32[]{:S(2)}) async-start(s8[8388608]{0:T(1024)(128)(4,1)} %bitcast.171), calls=%async_computation.14 | async-start | bytes 8388608
  155.4 7.4 slice-start.1
  162.8 8.3 copy-start.32
  162.8 8.3 copy-start.33
  162.8 8.9 %copy-start.8 = (f32[128]{0:T(128)S(1)}, f32[128]{0:T(128)}, u32[]{:S(2)}) copy-start(f32[128]{0:T(128)} %param.22) | copy-start | bytes 1540
  171.2 0.6 copy-start.6
  247.1 0.6 copy-start.4
  247.7 1.3 copy-start.11
  249.1 7.2 copy-start.2
  256.3 48.4 %copy-start.13 = (bf16[2,1,128,2048]{3,2,1,0:T(8,128)(2,1)S(1)}, bf16[2,1,128,2048]{3,2,1,0:T(8,128)(2,1)}, u32[]{:S(2)}) copy-start(bf16[2,1,128,2048]{3,2,1,0:T(8,128)(2,1)} %param.14) | copy-start | bytes 3145732
  304.7 0.7 copy-start.22
  373.9 1.5 copy-start.42
  386.3 215.7 %reduce-scatter.10.cloned.1.call-start = ((), (), s32[]{:S(2)}) async-start(), calls=%async_computation.11 | async-start | bytes 3604480 | tf_op jit(solution)/shard_map/reduce_scatter | solution.py:791
  401.9 1.6 copy-start.40
  425.0 177.0 %reduce-scatter.12.cloned.1.call-start = ((), (), s32[]{:S(2)}) async-start(), calls=%async_computation.12 | async-start | bytes 3604480 | tf_op jit(solution)/shard_map/reduce_scatter | solution.py:791
  425.7 355.3 %reduce-scatter.14.cloned.1.call-start = ((), (), s32[]{:S(2)}) async-start(), calls=%async_computation.13 | async-start | bytes 1310720 | tf_op jit(solution)/shard_map/reduce_scatter | solution.py:791
  425.8 13.1 %copy-start.37 = (bf16[704,2048]{1,0:T(8,128)(2,1)S(1)}, bf16[704,2048]{1,0:T(8,128)(2,1)}, u32[]{:S(2)}) copy-start(bf16[704,2048]{1,0:T(8,128)(2,1)} %all-gather.11.cloned.1.call-done) | copy-start | bytes 8650756
  425.8 13.1 %copy-start.43 = (bf16[2048,704]{0,1:T(8,128)(2,1)S(1)}, bf16[2048,704]{0,1:T(8,128)(2,1)}, u32[]{:S(2)}) copy-start(bf16[2048,704]{0,1:T(8,128)(2,1)} %copy-done.42) | copy-start | bytes 8650756
  448.0 40.1 %copy-start.36 = (bf16[2048,704]{1,0:T(8,128)(2,1)S(1)}, bf16[2048,704]{1,0:T(8,128)(2,1)}, u32[]{:S(2)}) copy-start(bf16[2048,704]{1,0:T(8,128)(2,1)} %all-gather.9.cloned.1.call-done) | copy-start | bytes 8650756
  448.0 40.1 %copy-start.41 = (bf16[2048,704]{0,1:T(8,128)(2,1)S(1)}, bf16[2048,704]{0,1:T(8,128)(2,1)}, u32[]{:S(2)}) copy-start(bf16[2048,704]{0,1:T(8,128)(2,1)} %copy-done.40) | copy-start | bytes 8650756
  541.7 1.2 copy-start.17
  541.7 1.2 copy-start.30
  546.2 40.7 %copy-start.3 = (bf16[8,2,128,256]{3,2,1,0:T(8,128)(2,1)S(1)}, bf16[8,2,128,256]{3,2,1,0:T(8,128)(2,1)}, u32[]{:S(2)}) copy-start(bf16[8,2,128,256]{3,2,1,0:T(8,128)(2,1)} %copy-done.2) | copy-start | bytes 3145732
  599.6 2.5 copy-start.5
  599.6 2.5 copy-start.7
  599.6 2.5 copy-start.9
  602.0 235.2 %reduce-scatter.6.cloned.1.call-start = ((), (), s32[]{:S(2)}) async-start(), calls=%async_computation.9 | async-start | bytes 5242880 | tf_op jit(solution)/shard_map/reduce_scatter | solution.py:791
  602.1 1.6 copy-start.10
  675.8 4.8 copy-start.16
  680.6 8.1 copy-start.35
  680.6 8.1 copy-start.39
  715.9 40.6 %copy-start.14 = (bf16[2,1,128,2048]{3,2,1,0:T(8,128)(2,1)S(1)}, bf16[2,1,128,2048]{3,2,1,0:T(8,128)(2,1)}, u32[]{:S(2)}) copy-start(bf16[2,1,128,2048]{3,2,1,0:T(8,128)(2,1)} %param.14) | copy-start | bytes 3145732
  715.9 40.7 %copy-start.24 = (f32[2048]{0:T(1024)S(1)}, f32[2048]{0:T(1024)}, u32[]{:S(2)}) copy-start(f32[2048]{0:T(1024)} %param.16) | copy-start | bytes 24580
  715.9 40.7 %copy-start.26 = (f32[256]{0:T(256)S(1)}, f32[256]{0:T(256)}, u32[]{:S(2)}) copy-start(f32[256]{0:T(256)} %copy-done.25) | copy-start | bytes 3076
  756.5 21.0 %copy-start.28 = (f32[2,128]{1,0:T(2,128)S(1)}, f32[2,128]{1,0:T(2,128)}, u32[]{:S(2)}) copy-start(f32[2,128]{1,0:T(2,128)} %copy-done.27) | copy-start | bytes 3076
  775.0 0.8 copy-start.18
  781.0 10.9 %copy-start.20 = (bf16[512,704]{0,1:T(8,128)(2,1)S(1)}, bf16[512,704]{0,1:T(8,128)(2,1)}, u32[]{:S(2)}) copy-start(bf16[512,704]{0,1:T(8,128)(2,1)} %reduce-scatter.12.cloned.1.call-done) | copy-start | bytes 2162692
  781.0 55.4 %collective-permute-start.1 = (bf16[64,2048]{1,0:T(8,128)(2,1)}, bf16[64,2048]{1,0:T(8,128)(2,1)S(1)}, u32[]{:S(2)}, u32[]{:S(2)}) collective-permute-start(bf16[64,2048]{1,0:T(8,128)(2,1)} %reduce-scatter.14.cloned.1.call-done), channel_id=1, source_target_pairs={{0,0},{8,1},{16,2},{24,3},{1,4},{9,5},{17,6},{25,7},{2,8},{10,9},{... | collective-permute-start | bytes 786440 | tf_op jit(solution)/shard_map/ppermute | solution.py:1389
  854.3 3.8 copy-start.1
Sparse Core Ops, SparseCore 0:
  144.2 33.8 all-gather.4
  180.3 63.2 all-gather.6
  245.7 62.1 all-gather.8
  309.3 57.7 all-gather.10
  386.4 52.7 reduce-scatter.7
  441.4 56.0 reduce-scatter.9
  499.7 56.0 reduce-scatter.11
  602.2 24.0 reduce-scatter.13
  671.1 73.9 reduce-scatter.5

commit v2 on v1

--- a/solution.py
+++ b/solution.py
@@ -8,7 +8,7 @@
 from jax.sharding import PartitionSpec as P
 
 SPAN = 64
-VMEM_LIMIT = 48 * 1024 * 1024
+VMEM_LIMIT = 56 * 1024 * 1024
 
 
 HIGH = lax.Precision.HIGHEST
@@ -319,6 +319,10 @@
 BF16 = jnp.bfloat16
 
 
+def lasting(microseconds):
+    return pl.CostEstimate(flops=0, bytes_accessed=int(microseconds * 3.5e6), transcendentals=0)
+
+
 def parts(value):
     top = value.astype(BF16)
     return (top, (value - top.astype(F32)).astype(BF16))
@@ -413,16 +417,22 @@
     taps_ref,
     param_ref,
     gain_ref,
+    own_ref,
     gated_ref,
     memory_ref,
     inverse_ref,
     fresh_ref,
     out_ref,
+    all_ref,
     state_ref,
     halo_ref,
+    send_sems,
+    recv_sems,
+    local_sem,
 ):
     seqs, span, _ = mixed_ref.shape
     heads, head_size = memory_ref.shape[1], memory_ref.shape[2]
+    gather_in_steps(own_ref, all_ref, send_sems, recv_sems, local_sem)
 
     @pl.when(pl.program_id(0) == 0)
     def _():
@@ -495,17 +505,21 @@
     fresh_ref,
     out_ref,
     grad_ref,
+    part_ref,
     error_ref,
     logit_grad_ref,
     taps_grad_ref,
     param_grad_ref,
     gain_grad_ref,
+    sum_ref,
     state_ref,
     halo_ref,
+    *scatter_refs,
 ):
     seqs, span, _ = mixed_ref.shape
     heads, head_size = memory_ref.shape[1], memory_ref.shape[2]
     step = pl.program_id(0)
+    scatter_in_steps(part_ref, sum_ref, *scatter_refs)
 
     @pl.when(step == 0)
     def _():
@@ -646,7 +660,10 @@
             shifted_grad,
             jnp.where(col_index < 2 * heads, terms * strengths * (1.0 - strengths), 0.0),
         )
-        logit_grad_ref[m] = logit_grad
+        logit_top, logit_rest = parts(logit_grad)
+        logit_grad_ref[m] = (
+            logit_top.astype(F32) + pltpu.roll(logit_rest.astype(F32), span // 2, 1)
+        ).astype(BF16)
         decay_lane = col_index[0:1] < heads
         param_grad_ref[0:1, :] += jnp.sum(
             jnp.where(decay_lane, decay_grad * decays, 0.0), 0, keepdims=True
@@ -667,8 +684,9 @@
         error_ref[m] = jnp.concatenate([mixed_grad] + gate_grads, 1).astype(BF16)
 
 
-def run_forward(mixed, gate, logits, taps, params, gain, heads):
+def run_forward(mixed, gate, logits, taps, params, gain, heads, own, collective_id):
     steps, seqs, span, _ = mixed.shape
+    anywhere = pl.BlockSpec(memory_space=pl.ANY)
     head_size = gain.shape[1]
     width = heads * head_size
 
@@ -694,31 +712,37 @@
             whole(taps),
             whole(params),
             whole(gain),
+            anywhere,
         ],
-        out_specs=[rows(width), squares(), squares(), rows(width), rows(width)],
+        out_specs=[rows(width), squares(), squares(), rows(width), rows(width), anywhere],
         out_shape=[
             jax.ShapeDtypeStruct((steps, seqs, span, width), BF16),
             square,
             lower,
             flat,
             flat,
+            jax.ShapeDtypeStruct((steps,) + own.shape, own.dtype),
         ],
         scratch_shapes=[
             pltpu.VMEM((seqs, heads, head_size, head_size), F32),
             pltpu.VMEM((seqs, 8, 3 * width), F32),
+            pltpu.SemaphoreType.DMA((9,)),
+            pltpu.SemaphoreType.DMA((9,)),
+            pltpu.SemaphoreType.DMA,
         ],
-        compiler_params=pltpu.CompilerParams(vmem_limit_bytes=VMEM_LIMIT),
-        cost_estimate=pl.CostEstimate(
-            flops=steps * seqs * heads * 120 * span**3,
-            bytes_accessed=steps * seqs * span * width * 30,
-            transcendentals=0,
+        compiler_params=pltpu.CompilerParams(
+            collective_id=collective_id, has_side_effects=True, vmem_limit_bytes=VMEM_LIMIT
         ),
+        cost_estimate=lasting(75),
         name="mixer_forward",
-    )(mixed, gate, logits, taps, params, gain)
-
-
-def run_backward(mixed, gate, logits, taps, params, gain, memory, inverse, fresh, out, grad):
+    )(mixed, gate, logits, taps, params, gain, own)
+
+
+def run_backward(
+    mixed, gate, logits, taps, params, gain, memory, inverse, fresh, out, grad, part, collective_id
+):
     steps, seqs, span, _ = mixed.shape
+    _, part_rows, columns = part.shape
     heads, head_size = memory.shape[2], memory.shape[3]
     width = heads * head_size
     edge = 16
@@ -754,6 +778,7 @@
             rows(width),
             rows(width),
             rows(width),
+            pl.BlockSpec(memory_space=pl.ANY),
         ],
         out_specs=[
             rows(4 * width),
@@ -761,26 +786,33 @@
             whole((8, 3 * width)),
             whole((8, logits.shape[-1])),
             whole((8, head_size)),
+            whole((part_rows, columns)),
         ],
         out_shape=[
             jax.ShapeDtypeStruct((steps, seqs, span, 4 * width), BF16),
-            jax.ShapeDtypeStruct(logits.shape, F32),
+            jax.ShapeDtypeStruct(logits.shape, BF16),
             jax.ShapeDtypeStruct((8, 3 * width), F32),
             jax.ShapeDtypeStruct((8, logits.shape[-1]), F32),
             jax.ShapeDtypeStruct((8, head_size), F32),
+            jax.ShapeDtypeStruct((part_rows, columns), F32),
         ],
         scratch_shapes=[
             pltpu.VMEM((seqs, heads, head_size, head_size), F32),
             pltpu.VMEM((seqs, 8, 3 * width), F32),
+            pltpu.VMEM((4, part_rows, columns), BF16),
+            pltpu.VMEM((4, part_rows, columns), BF16),
+            pltpu.VMEM((part_rows, columns), BF16),
+            pltpu.VMEM((2, part_rows, columns), BF16),
+            pltpu.SemaphoreType.DMA((10,)),
+            pltpu.SemaphoreType.DMA((10,)),
+            pltpu.SemaphoreType.DMA((4,)),
         ],
-        compiler_params=pltpu.CompilerParams(vmem_limit_bytes=VMEM_LIMIT),
-        cost_estimate=pl.CostEstimate(
-            flops=steps * seqs * heads * 120 * span**3,
-            bytes_accessed=steps * seqs * span * width * 40,
-            transcendentals=0,
+        compiler_params=pltpu.CompilerParams(
+            collective_id=collective_id, has_side_effects=True, vmem_limit_bytes=VMEM_LIMIT
         ),
+        cost_estimate=lasting(55),
         name="mixer_backward",
-    )(mixed, mixed, gate, logits, taps, params, gain, memory, inverse, fresh, out, grad)
+    )(mixed, mixed, gate, logits, taps, params, gain, memory, inverse, fresh, out, grad, part)
 
 
 def gather_rows(value, axis):
@@ -858,12 +890,6 @@
     yield
 
 
-def plane_gather_kernel(own_ref, all_ref, send_sems, recv_sems, local_sem):
-    greet(plane_peers()[1:])
-    for _ in gather_phases(own_ref, all_ref, send_sems, recv_sems, local_sem, 0):
-        pass
-
-
 def chain_phases(all_ref, up_send, up_recv, down_send, down_recv):
     depth = all_ref.shape[0]
     place = lax.axis_index("dp")
@@ -912,11 +938,9 @@
 
 def plane_open_kernel(
     first_ref,
-    second_ref,
     early_ref,
     later_ref,
     first_all_ref,
-    second_all_ref,
     early_all_ref,
     later_all_ref,
     send_sems,
@@ -957,73 +981,101 @@
     keep_early.wait()
     chain = chain_phases(early_all_ref, up_send, up_recv, down_send, down_recv)
     first = gather_phases(first_ref, first_all_ref, send_sems, recv_sems, local_sems.at[2], ring)
-    second = gather_phases(
-        second_ref, second_all_ref, send_sems, recv_sems, local_sems.at[3], ring + 9
-    )
+    next(chain)
+    next(first)
+    later = exchange_copies(later_ref, later_all_ref.at[me], send_sems, recv_sems, ring + 9)
+    next(chain)
+    next(first)
     next(chain)
     next(first)
     next(first)
-    next(second)
-    later = exchange_copies(later_ref, later_all_ref.at[me], send_sems, recv_sems, ring + 18)
-    next(chain)
-    next(first)
-    next(chain)
-    next(second)
-    next(first)
-    next(second)
     for copy in later:
         copy.wait_recv()
     next(chain)
-    next(second)
     for copy in early + later:
         copy.wait_send()
     keep_later.wait()
 
 
-def plane_open(first, second, early, later, collective_id):
+def plane_open(first, early, later, collective_id):
     ring, depth = lax.axis_size("seq"), lax.axis_size("dp")
     rows, columns = first.shape
-    total = 2 * ring + 18
+    total = 2 * ring + 9
     return pl.pallas_call(
         plane_open_kernel,
         out_shape=[
             jax.ShapeDtypeStruct((ring, rows, columns), first.dtype),
-            jax.ShapeDtypeStruct((ring, rows, columns), second.dtype),
             jax.ShapeDtypeStruct((depth, ring * early.shape[1], early.shape[2]), early.dtype),
             jax.ShapeDtypeStruct(later.shape, later.dtype),
         ],
-        in_specs=[pl.BlockSpec(memory_space=pl.ANY)] * 4,
-        out_specs=[pl.BlockSpec(memory_space=pl.ANY)] * 4,
+        in_specs=[pl.BlockSpec(memory_space=pl.ANY)] * 3,
+        out_specs=[pl.BlockSpec(memory_space=pl.ANY)] * 3,
         scratch_shapes=[
             pltpu.SemaphoreType.DMA((total,)),
             pltpu.SemaphoreType.DMA((total,)),
-            pltpu.SemaphoreType.DMA((4,)),
+            pltpu.SemaphoreType.DMA((3,)),
         ]
         + [pltpu.SemaphoreType.DMA((depth - 1,))] * 4,
         compiler_params=pltpu.CompilerParams(collective_id=collective_id, has_side_effects=True),
+        cost_estimate=lasting(90),
         name="plane_open",
-    )(first, second, early, later)
-
-
-def plane_gather(own, collective_id):
-    ring = lax.axis_size("seq")
-    rows, columns = own.shape
-    return pl.pallas_call(
-        plane_gather_kernel,
-        out_shape=jax.ShapeDtypeStruct((ring, rows, columns), own.dtype),
-        in_specs=[pl.BlockSpec(memory_space=pl.ANY)],
-        out_specs=pl.BlockSpec(memory_space=pl.ANY),
-        scratch_shapes=[
-            pltpu.SemaphoreType.DMA((9,)),
-            pltpu.SemaphoreType.DMA((9,)),
-            pltpu.SemaphoreType.DMA,
-        ],
-        compiler_params=pltpu.CompilerParams(collective_id=collective_id, has_side_effects=True),
-        name="plane_gather",
-    )(own)
-
-
-def plane_scatter_kernel(
+    )(first, early, later)
+
+
+def gather_in_steps(own_ref, all_ref, send_sems, recv_sems, local_sem):
+    me, sibling, across, along = plane_peers()
+    far = along + across - me
+    half = own_ref.shape[0] // 2
+    upper, lower = pl.ds(0, half), pl.ds(half, half)
+    keep = pltpu.make_async_copy(own_ref, all_ref.at[me], local_sem)
+    plan = [
+        (across, own_ref, all_ref.at[me]),
+        (along, own_ref, all_ref.at[me]),
+        (sibling, own_ref, all_ref.at[me]),
+        (along, all_ref.at[across, upper], all_ref.at[across, upper]),
+        (across, all_ref.at[along, lower], all_ref.at[along, lower]),
+        (sibling, all_ref.at[across], all_ref.at[across]),
+        (sibling, all_ref.at[along], all_ref.at[along]),
+        (sibling, all_ref.at[far, upper], all_ref.at[far, upper]),
+        (sibling, all_ref.at[far, lower], all_ref.at[far, lower]),
+    ]
+    copies = [
+        send_to(peer, source, target, send_sems.at[k], recv_sems.at[k])
+        for k, (peer, source, target) in enumerate(plan)
+    ]
+    step, steps = pl.program_id(0), pl.num_programs(0)
+
+    @pl.when(step == 0)
+    def _():
+        greet((sibling, across, along))
+        keep.start()
+        for k in (0, 1, 2):
+            copies[k].start()
+
+    @pl.when(step == 3)
+    def _():
+        copies[0].wait_recv()
+        copies[1].wait_recv()
+        for k in (3, 4, 5, 6):
+            copies[k].start()
+
+    @pl.when(step == 5)
+    def _():
+        copies[3].wait_recv()
+        copies[4].wait_recv()
+        for k in (7, 8):
+            copies[k].start()
+
+    @pl.when(step == steps - 1)
+    def _():
+        for k in (2, 5, 6, 7, 8):
+            copies[k].wait_recv()
+        for copy in copies:
+            copy.wait_send()
+        keep.wait()
+
+
+def scatter_in_steps(
     part_ref,
     sum_ref,
     own_ref,
@@ -1040,95 +1092,88 @@
     rows = sum_ref.shape[0]
     half = rows // 2
     upper, lower = pl.ds(0, half), pl.ds(half, half)
-    greet((sibling, across, along))
     slabs = (far, across, along, me)
-    loads = []
-    nears = []
-    for k, slab in enumerate(slabs):
-        load = pltpu.make_async_copy(part_ref.at[slab], own_ref.at[k], load_sems.at[k])
-        load.start()
-        loads.append(load)
-        near = send_to(sibling, part_ref.at[slab + flip], near_ref.at[k], send_sems.at[k], recv_sems.at[k])
-        near.start()
-        nears.append(near)
-
-    def send(k, peer, source, target):
-        copy = send_to(peer, source, target, send_sems.at[k], recv_sems.at[k])
-        copy.start()
-        return copy
-
-    step = 32
-
-    def fold(target, other, start, count):
-        @pl.loop(0, count // step)
+    loads = [
+        pltpu.make_async_copy(part_ref.at[slab], own_ref.at[k], load_sems.at[k])
+        for k, slab in enumerate(slabs)
+    ]
+    plan = [(sibling, part_ref.at[slab + flip], near_ref.at[k]) for k, slab in enumerate(slabs)]
+    plan += [
+        (across, own_ref.at[0, upper], far_in_ref.at[upper]),
+        (along, own_ref.at[0, lower], far_in_ref.at[lower]),
+        (across, own_ref.at[1, upper], side_in_ref.at[0, upper]),
+        (along, own_ref.at[2, lower], side_in_ref.at[1, lower]),
+        (along, own_ref.at[2, upper], side_in_ref.at[1, upper]),
+        (across, own_ref.at[1, lower], side_in_ref.at[0, lower]),
+    ]
+    copies = [
+        send_to(peer, source, target, send_sems.at[k], recv_sems.at[k])
+        for k, (peer, source, target) in enumerate(plan)
+    ]
+    step, steps = pl.program_id(0), pl.num_programs(0)
+    tall = 32
+
+    def fold(target, other, start, size):
+        @pl.loop(0, size // tall)
         def _(i):
-            at = pl.ds(pl.multiple_of(start + i * step, step), step)
+            at = pl.ds(pl.multiple_of(start + i * tall, tall), tall)
             target[at] = (target[at].astype(F32) + other[at].astype(F32)).astype(BF16)
 
     def join(k):
         loads[k].wait()
-        nears[k].wait_recv()
-
-    join(0)
-    fold(own_ref.at[0], near_ref.at[0], 0, rows)
-    copies = [
-        send(4, across, own_ref.at[0, upper], far_in_ref.at[upper]),
-        send(5, along, own_ref.at[0, lower], far_in_ref.at[lower]),
-    ]
-    join(1)
-    fold(own_ref.at[1], near_ref.at[1], 0, rows)
-    copies.append(send(6, across, own_ref.at[1, upper], side_in_ref.at[0, upper]))
-    join(2)
-    fold(own_ref.at[2], near_ref.at[2], 0, rows)
-    copies.append(send(7, along, own_ref.at[2, lower], side_in_ref.at[1, lower]))
-    copies[0].wait_recv()
-    fold(own_ref.at[2], far_in_ref, 0, half)
-    copies.append(send(8, along, own_ref.at[2, upper], side_in_ref.at[1, upper]))
-    copies[1].wait_recv()
-    fold(own_ref.at[1], far_in_ref, half, half)
-    copies.append(send(9, across, own_ref.at[1, lower], side_in_ref.at[0, lower]))
-    join(3)
-    for copy in copies[2:]:
-        copy.wait_recv()
-
-    @pl.loop(0, rows // step)
-    def _(i):
-        at = pl.ds(pl.multiple_of(i * step, step), step)
-        sum_ref[at] = (
-            own_ref[3, at].astype(F32)
-            + near_ref[3, at].astype(F32)
-            + side_in_ref[0, at].astype(F32)
-            + side_in_ref[1, at].astype(F32)
-        )
-
-    for copy in nears + copies:
-        copy.wait_send()
-
-
-def plane_scatter(part, collective_id):
-    ring, rows, columns = part.shape
-    return pl.pallas_call(
-        plane_scatter_kernel,
-        out_shape=jax.ShapeDtypeStruct((rows, columns), F32),
-        in_specs=[pl.BlockSpec(memory_space=pl.ANY)],
-        out_specs=pl.BlockSpec(memory_space=pltpu.VMEM),
-        scratch_shapes=[
-            pltpu.VMEM((4, rows, columns), BF16),
-            pltpu.VMEM((4, rows, columns), BF16),
-            pltpu.VMEM((rows, columns), BF16),
-            pltpu.VMEM((2, rows, columns), BF16),
-            pltpu.SemaphoreType.DMA((10,)),
-            pltpu.SemaphoreType.DMA((10,)),
-            pltpu.SemaphoreType.DMA((4,)),
-        ],
-        compiler_params=pltpu.CompilerParams(
-            collective_id=collective_id, has_side_effects=True, vmem_limit_bytes=VMEM_LIMIT
-        ),
-        name="plane_scatter",
-    )(part)
-
-
-def small_sum_kernel(own_ref, all_ref, stage_ref, total_ref, send_sems, recv_sems):
+        copies[k].wait_recv()
+        fold(own_ref.at[k], near_ref.at[k], 0, rows)
+
+    @pl.when(step == 0)
+    def _():
+        greet((sibling, across, along))
+        for k in range(4):
+            loads[k].start()
+            copies[k].start()
+
+    @pl.when(step == 1)
+    def _():
+        join(0)
+        copies[4].start()
+        copies[5].start()
+        join(1)
+        copies[6].start()
+        join(2)
+        copies[7].start()
+
+    @pl.when(step == 3)
+    def _():
+        copies[4].wait_recv()
+        fold(own_ref.at[2], far_in_ref, 0, half)
+        copies[8].start()
+        copies[5].wait_recv()
+        fold(own_ref.at[1], far_in_ref, half, half)
+        copies[9].start()
+
+    @pl.when(step == steps - 1)
+    def _():
+        loads[3].wait()
+        copies[3].wait_recv()
+        for copy in copies[6:]:
+            copy.wait_recv()
+
+        @pl.loop(0, rows // tall)
+        def _(i):
+            at = pl.ds(pl.multiple_of(i * tall, tall), tall)
+            sum_ref[at] = (
+                own_ref[3, at].astype(F32)
+                + near_ref[3, at].astype(F32)
+                + side_in_ref[0, at].astype(F32)
+                + side_in_ref[1, at].astype(F32)
+            )
+
+        for copy in copies:
+            copy.wait_send()
+
+
+def small_sum_kernel(
+    own_ref, cut_ref, all_ref, swapped_ref, stage_ref, total_ref, send_sems, recv_sems, local_sem
+):
     depth, ring = stage_ref.shape[0], all_ref.shape[0]
     place, me = lax.axis_index("dp"), lax.axis_index("seq")
     barrier = pltpu.get_barrier_semaphore()
@@ -1140,6 +1185,8 @@
     for peer in plane:
         pl.semaphore_signal(barrier, inc=1, device_id={"seq": peer}, device_id_type=mesh_ids)
     pl.semaphore_wait(barrier, depth + ring - 2)
+    keep = pltpu.make_async_copy(cut_ref.at[me], swapped_ref.at[me], local_sem)
+    keep.start()
     first = []
     for k, peer in enumerate(columns):
         copy = pltpu.make_async_remote_copy(
@@ -1152,6 +1199,9 @@
         )
         copy.start()
         first.append(copy)
+    swaps = exchange_copies(
+        cut_ref, swapped_ref.at[me], send_sems, recv_sems, depth + ring - 2
+    )
     stage_ref[place] = own_ref[...]
     for copy in first:
         copy.wait_recv()
@@ -1172,29 +1222,36 @@
         copy.start()
         second.append(copy)
     all_ref[me] = total
-    for copy in second:
+    for copy in second + swaps:
         copy.wait_recv()
-    for copy in first + second:
+    for copy in first + second + swaps:
         copy.wait_send()
-
-
-def small_sum(own, collective_id):
+    keep.wait()
+
+
+def small_sum(own, cut, collective_id):
     depth, ring = lax.axis_size("dp"), lax.axis_size("seq")
-    count = depth + ring - 2
+    count = depth + 2 * ring - 3
+    vmem, anywhere = pl.BlockSpec(memory_space=pltpu.VMEM), pl.BlockSpec(memory_space=pl.ANY)
     return pl.pallas_call(
         small_sum_kernel,
-        out_shape=jax.ShapeDtypeStruct((ring,) + own.shape, F32),
-        in_specs=[pl.BlockSpec(memory_space=pltpu.VMEM)],
-        out_specs=pl.BlockSpec(memory_space=pltpu.VMEM),
+        out_shape=[
+            jax.ShapeDtypeStruct((ring,) + own.shape, F32),
+            jax.ShapeDtypeStruct(cut.shape, cut.dtype),
+        ],
+        in_specs=[vmem, anywhere],
+        out_specs=[vmem, anywhere],
         scratch_shapes=[
             pltpu.VMEM((depth,) + own.shape, F32),
             pltpu.VMEM(own.shape, F32),
             pltpu.SemaphoreType.DMA((count,)),
             pltpu.SemaphoreType.DMA((count,)),
+            pltpu.SemaphoreType.DMA,
         ],
         compiler_params=pltpu.CompilerParams(collective_id=collective_id, has_side_effects=True),
+        cost_estimate=lasting(20),
         name="small_sum",
-    )(own)
+    )(own, cut)
 
 
 def greet_plane(ring):
@@ -1202,42 +1259,471 @@
     greet([lax.rem(me + k, ring) for k in range(1, ring)])
 
 
-def plane_exchange_kernel(count, *refs):
-    cuts, swaps = refs[:count], refs[count : 2 * count]
-    send_sems, recv_sems, local_sems = refs[2 * count :]
-    ring = cuts[0].shape[0]
-    me = lax.axis_index("seq")
-    greet_plane(ring)
-    copies, keeps = [], []
+def plane_scatter_dot_kernel(count, dims, fill, swaps, *refs):
+    refs = list(refs)
+
+    def take(size):
+        taken = refs[:size]
+        del refs[:size]
+        return taken
+
+    left_hbm, right_hbm, fill_hbm = take(count), take(count), take(int(fill))
+    cut_refs = take(swaps)
+    (sum_ref,) = take(1)
+    terms = take(count if fill else 0)
+    swapped_refs = take(swaps)
+    lefts, rights, fill_refs = take(count), take(count), take(int(fill))
+    out_ref, own_ref, near_ref, far_in_ref, side_in_ref = take(5)
+    send_sems, recv_sems, load_sems = refs
+    loads = []
     for k in range(count):
-        keep = pltpu.make_async_copy(cuts[k].at[me], swaps[k].at[me], local_sems.at[k])
-        keep.start()
-        keeps.append(keep)
-        copies += exchange_copies(cuts[k], swaps[k].at[me], send_sems, recv_sems, k * (ring - 1))
-    for copy in copies:
+        for source, target in ((left_hbm[k], lefts[k]), (right_hbm[k], rights[k])):
+            load = pltpu.make_async_copy(source, target, load_sems.at[len(loads)])
+            load.start()
+            loads.append(load)
+    if fill:
+        fill_load = pltpu.make_async_copy(fill_hbm[0], fill_refs[0], load_sems.at[2 * count])
+        fill_load.start()
+    me, sibling, across, along = plane_peers()
+    far = along + across - me
+    flip = sibling - me
+    rows, columns = sum_ref.shape
+    half = rows // 2
+    upper, lower = pl.ds(0, half), pl.ds(half, half)
+    swapped, keeps = [], []
+    if swaps:
+        ring = cut_refs[0].shape[0]
+        greet_plane(ring)
+        for k in range(swaps):
+            keep = pltpu.make_async_copy(
+                cut_refs[k].at[me], swapped_refs[k].at[me], load_sems.at[2 * count + k]
+            )
+            keep.start()
+            keeps.append(keep)
+            swapped += exchange_copies(
+                cut_refs[k], swapped_refs[k].at[me], send_sems, recv_sems, 10 + k * (ring - 1)
+            )
+    else:
+        greet((sibling, across, along))
+    for load in loads:
+        load.wait()
+    wide = 512
+
+    def slab_dot(slab, target):
+        @pl.loop(0, columns // wide)
+        def _(i):
+            at = pl.ds(pl.multiple_of(i * wide, wide), wide)
+            total = None
+            for k in range(count):
+                right = rights[k][:, at] if dims[1] == (0,) else rights[k][at, :]
+                term = low_dot(lefts[k][slab], right, dims)
+                total = term if total is None else total + term
+            target[:, at] = total.astype(BF16)
+
+    def send(k, peer, source, target):
+        copy = send_to(peer, source, target, send_sems.at[k], recv_sems.at[k])
+        copy.start()
+        return copy
+
+    step = 32
+
+    def fold(target, other, start, size):
+        @pl.loop(0, size // step)
+        def _(i):
+            at = pl.ds(pl.multiple_of(start + i * step, step), step)
+            target[at] = (target[at].astype(F32) + other[at].astype(F32)).astype(BF16)
+
+    nears = []
+
+    def near_slab(k, slab):
+        slab_dot(slab + flip, out_ref.at[k])
+        nears.append(send(k, sibling, out_ref.at[k], near_ref.at[k]))
+
+    near_slab(0, far)
+    slab_dot(far, own_ref.at[0])
+    near_slab(1, across)
+    nears[0].wait_recv()
+    fold(own_ref.at[0], near_ref.at[0], 0, rows)
+    copies = [
+        send(4, across, own_ref.at[0, upper], far_in_ref.at[upper]),
+        send(5, along, own_ref.at[0, lower], far_in_ref.at[lower]),
+    ]
+    slab_dot(across, own_ref.at[1])
+    near_slab(2, along)
+    nears[1].wait_recv()
+    fold(own_ref.at[1], near_ref.at[1], 0, rows)
+    copies.append(send(6, across, own_ref.at[1, upper], side_in_ref.at[0, upper]))
+    slab_dot(along, own_ref.at[2])
+    near_slab(3, me)
+    nears[2].wait_recv()
+    fold(own_ref.at[2], near_ref.at[2], 0, rows)
+    copies.append(send(7, along, own_ref.at[2, lower], side_in_ref.at[1, lower]))
+    slab_dot(me, own_ref.at[3])
+    copies[0].wait_recv()
+    fold(own_ref.at[2], far_in_ref, 0, half)
+    copies.append(send(8, along, own_ref.at[2, upper], side_in_ref.at[1, upper]))
+    copies[1].wait_recv()
+    fold(own_ref.at[1], far_in_ref, half, half)
+    copies.append(send(9, across, own_ref.at[1, lower], side_in_ref.at[0, lower]))
+    if fill:
+        fill_load.wait()
+        tall = 256
+
+        @pl.loop(0, terms[0].shape[0] // tall)
+        def _(i):
+            at = pl.ds(pl.multiple_of(i * tall, tall), tall)
+            turned = fill_refs[0][:, at]
+            for k in range(count):
+                wide_left = lefts[k][...].reshape(-1, lefts[k].shape[2])
+                terms[k][at, :] = low_dot(turned, wide_left, TN).astype(BF16)
+
+    nears[3].wait_recv()
+
+    def finish(a, start):
+        @pl.loop(0, half // step)
+        def _(i):
+            at = pl.ds(pl.multiple_of(start + i * step, step), step)
+            sum_ref[at] = (
+                own_ref[3, at].astype(F32)
+                + near_ref[3, at].astype(F32)
+                + side_in_ref[0, at].astype(F32)
+                + side_in_ref[1, at].astype(F32)
+            )
+
+    for copy in copies[2:]:
         copy.wait_recv()
-    for copy in copies:
+    finish(0, 0)
+    finish(1, half)
+    for copy in swapped:
+        copy.wait_recv()
+    for copy in nears + copies + swapped:
         copy.wait_send()
     for keep in keeps:
         keep.wait()
 
 
-def plane_exchange(cuts, collective_id):
-    count = len(cuts)
-    total = count * (cuts[0].shape[0] - 1)
+def plane_scatter_dot(lefts, rights, dims, collective_id, fill=None, cuts=()):
+    count = len(lefts)
+    ring, rows, _ = lefts[0].shape
+    columns = rights[0].shape[1 - dims[1][0]]
+    filled = fill is not None
+    fills = [fill] if filled else []
+    vmem, anywhere = pl.BlockSpec(memory_space=pltpu.VMEM), pl.BlockSpec(memory_space=pl.ANY)
+    total = 10 + len(cuts) * (ring - 1)
+    term_shapes = [
+        jax.ShapeDtypeStruct((fill.shape[1], left.shape[2]), BF16) for left in lefts if filled
+    ]
     return pl.pallas_call(
-        functools.partial(plane_exchange_kernel, count),
-        out_shape=[jax.ShapeDtypeStruct(cut.shape, cut.dtype) for cut in cuts],
-        in_specs=[pl.BlockSpec(memory_space=pl.ANY)] * count,
-        out_specs=[pl.BlockSpec(memory_space=pl.ANY)] * count,
-        scratch_shapes=[
+        functools.partial(plane_scatter_dot_kernel, count, dims, filled, len(cuts)),
+        out_shape=[jax.ShapeDtypeStruct((rows, columns), F32)]
+        + term_shapes
+        + [jax.ShapeDtypeStruct(cut.shape, cut.dtype) for cut in cuts],
+        in_specs=[anywhere] * (2 * count + len(fills) + len(cuts)),
+        out_specs=[vmem] * (1 + len(term_shapes)) + [anywhere] * len(cuts),
+        scratch_shapes=[pltpu.VMEM(left.shape, BF16) for left in lefts]
+        + [pltpu.VMEM(right.shape, BF16) for right in rights]
+        + [pltpu.VMEM(value.shape, BF16) for value in fills]
+        + [
+            pltpu.VMEM((4, rows, columns), BF16),
+            pltpu.VMEM((4, rows, columns), BF16),
+            pltpu.VMEM((4, rows, columns), BF16),
+            pltpu.VMEM((rows, columns), BF16),
+            pltpu.VMEM((2, rows, columns), BF16),
             pltpu.SemaphoreType.DMA((total,)),
             pltpu.SemaphoreType.DMA((total,)),
-            pltpu.SemaphoreType.DMA((count,)),
+            pltpu.SemaphoreType.DMA((2 * count + len(fills) + len(cuts),)),
         ],
-        compiler_params=pltpu.CompilerParams(collective_id=collective_id, has_side_effects=True),
-        name="plane_exchange",
-    )(*cuts)
+        compiler_params=pltpu.CompilerParams(
+            collective_id=collective_id, has_side_effects=True, vmem_limit_bytes=VMEM_LIMIT
+        ),
+        cost_estimate=lasting(45),
+        name="plane_scatter_dot",
+    )(*lefts, *rights, *fills, *cuts)
+
+
+def gather_in_turn(own_ref, all_ref, send_sems, recv_sems, use):
+    me, sibling, across, along = plane_peers()
+    far = along + across - me
+    flip = sibling - me
+    half = own_ref.shape[0] // 2
+    upper, lower = pl.ds(0, half), pl.ds(half, half)
+    copies = []
+
+    def send(peer, source, target):
+        k = len(copies)
+        copy = send_to(peer, source, target, send_sems.at[k], recv_sems.at[k])
+        copy.start()
+        copies.append(copy)
+
+    send(across, own_ref, all_ref.at[me])
+    send(along, own_ref, all_ref.at[me])
+    send(sibling, own_ref, all_ref.at[me])
+    all_ref[me] = own_ref[...]
+    use(me)
+    copies[2].wait_recv()
+    use(sibling)
+    copies[0].wait_recv()
+    send(along, all_ref.at[across, upper], all_ref.at[across, upper])
+    copies[1].wait_recv()
+    send(across, all_ref.at[along, lower], all_ref.at[along, lower])
+    send(sibling, all_ref.at[across], all_ref.at[across])
+    send(sibling, all_ref.at[along], all_ref.at[along])
+    use(across)
+    use(along)
+    copies[5].wait_recv()
+    use(across + flip)
+    copies[6].wait_recv()
+    use(along + flip)
+    copies[3].wait_recv()
+    send(sibling, all_ref.at[far, upper], all_ref.at[far, upper])
+    copies[4].wait_recv()
+    send(sibling, all_ref.at[far, lower], all_ref.at[far, lower])
+    use(far)
+    copies[7].wait_recv()
+    copies[8].wait_recv()
+    use(far + flip)
+    for copy in copies:
+        copy.wait_send()
+
+
+def gather_feed_kernel(
+    own_hbm,
+    gate_hbm,
+    up_hbm,
+    down_hbm,
+    error_hbm,
+    all_hbm,
+    activated_hbm,
+    gate_err_hbm,
+    up_err_hbm,
+    down_term_ref,
+    own_ref,
+    gate_ref,
+    up_ref,
+    down_ref,
+    error_ref,
+    all_ref,
+    activated_out,
+    gate_out,
+    up_out,
+    total_ref,
+    send_sems,
+    recv_sems,
+    load_sems,
+    save_sems,
+):
+    loads = []
+    for source, target in (
+        (own_hbm, own_ref),
+        (gate_hbm, gate_ref),
+        (up_hbm, up_ref),
+        (down_hbm, down_ref),
+        (error_hbm, error_ref),
+    ):
+        load = pltpu.make_async_copy(source, target, load_sems.at[len(loads)])
+        load.start()
+        loads.append(load)
+    greet(plane_peers()[1:])
+    loads[0].wait()
+    waiting = loads[1:]
+    saves = []
+    tall = 128
+    wide = 512
+    rows, columns = own_ref.shape
+
+    def use(slab):
+        first = bool(waiting)
+        while waiting:
+            waiting.pop().wait()
+        turn = len(saves) % 2
+        if len(saves) > 1:
+            for save in saves[-2]:
+                save.wait()
+
+        @pl.loop(0, rows // tall)
+        def _(i):
+            at = pl.ds(pl.multiple_of(i * tall, tall), tall)
+            values = all_ref[slab, at, :]
+            gate = low_dot(values, gate_ref[...], NN)
+            up = low_dot(values, up_ref[...], NN)
+            grad = low_dot(error_ref[slab, at, :], down_ref[...], NT)
+            opening = sigmoid(gate)
+            gate_open = gate * opening
+            activated_out[turn, at, :] = (gate_open * up).astype(BF16)
+            gate_out[turn, at, :] = (
+                grad * up * (opening * (1.0 + gate * (1.0 - opening)))
+            ).astype(BF16)
+            up_out[turn, at, :] = (grad * gate_open).astype(BF16)
+
+        batch = []
+        for k, (source, target) in enumerate(
+            (
+                (activated_out.at[turn], activated_hbm.at[slab]),
+                (gate_out.at[turn], gate_err_hbm.at[slab]),
+                (up_out.at[turn], up_err_hbm.at[slab]),
+                (all_ref.at[slab], all_hbm.at[slab]),
+            )
+        ):
+            save = pltpu.make_async_copy(source, target, save_sems.at[turn, k])
+            save.start()
+            batch.append(save)
+        saves.append(batch)
+
+        @pl.loop(0, columns // wide)
+        def _(i):
+            at = pl.ds(pl.multiple_of(i * wide, wide), wide)
+            term = low_dot(activated_out[turn], error_ref[slab, :, at], TN)
+            if first:
+                total_ref[:, at] = term
+            else:
+                total_ref[:, at] += term
+
+    gather_in_turn(own_ref, all_ref, send_sems, recv_sems, use)
+    down_term_ref[...] = total_ref[...].astype(BF16)
+    for batch in saves[-2:]:
+        for save in batch:
+            save.wait()
+
+
+def gather_feed(own, gate_own, up_own, down_own, error_all, collective_id):
+    ring = lax.axis_size("seq")
+    rows, columns = own.shape
+    units = gate_own.shape[1]
+    anywhere = pl.BlockSpec(memory_space=pl.ANY)
+    parted = jax.ShapeDtypeStruct((ring, rows, units), BF16)
+    return pl.pallas_call(
+        gather_feed_kernel,
+        out_shape=[
+            jax.ShapeDtypeStruct((ring, rows, columns), BF16),
+            parted,
+            parted,
+            parted,
+            jax.ShapeDtypeStruct(down_own.shape, BF16),
+        ],
+        in_specs=[anywhere] * 5,
+        out_specs=[anywhere] * 4 + [pl.BlockSpec(memory_space=pltpu.VMEM)],
+        scratch_shapes=[
+            pltpu.VMEM((rows, columns), BF16),
+            pltpu.VMEM(gate_own.shape, BF16),
+            pltpu.VMEM(up_own.shape, BF16),
+            pltpu.VMEM(down_own.shape, BF16),
+            pltpu.VMEM((ring, rows, columns), BF16),
+            pltpu.VMEM((ring, rows, columns), BF16),
+            pltpu.VMEM((2, rows, units), BF16),
+            pltpu.VMEM((2, rows, units), BF16),
+            pltpu.VMEM((2, rows, units), BF16),
+            pltpu.VMEM(down_own.shape, F32),
+            pltpu.SemaphoreType.DMA((9,)),
+            pltpu.SemaphoreType.DMA((9,)),
+            pltpu.SemaphoreType.DMA((5,)),
+            pltpu.SemaphoreType.DMA((2, 4)),
+        ],
+        compiler_params=pltpu.CompilerParams(
+            collective_id=collective_id, has_side_effects=True, vmem_limit_bytes=VMEM_LIMIT
+        ),
+        cost_estimate=lasting(60),
+        name="gather_feed",
+    )(own, gate_own, up_own, down_own, error_all)
+
+
+def gather_branch_kernel(
+    own_hbm,
+    gated_hbm,
+    weight_hbm,
+    activated_hbm,
+    down_hbm,
+    grad_ref,
+    term_ref,
+    part_hbm,
+    own_ref,
+    gated_ref,
+    weight_ref,
+    activated_ref,
+    down_ref,
+    all_ref,
+    total_ref,
+    part_out,
+    send_sems,
+    recv_sems,
+    load_sems,
+    save_sems,
+):
+    loads = []
+    for source, target in (
+        (own_hbm, own_ref),
+        (gated_hbm, gated_ref),
+        (weight_hbm, weight_ref),
+        (activated_hbm, activated_ref),
+        (down_hbm, down_ref),
+    ):
+        load = pltpu.make_async_copy(source, target, load_sems.at[len(loads)])
+        load.start()
+        loads.append(load)
+    greet(plane_peers()[1:])
+    loads[0].wait()
+    waiting = loads[1:]
+    total_ref[...] = jnp.zeros_like(total_ref)
+    wide = 512
+    saves = []
+
+    def use(slab):
+        while waiting:
+            waiting.pop().wait()
+        turn = len(saves) % 2
+        if len(saves) > 1:
+            saves[-2].wait()
+        grad_ref[slab] = low_dot(all_ref[slab], weight_ref[...], NT).astype(BF16)
+
+        @pl.loop(0, total_ref.shape[1] // wide)
+        def _(i):
+            at = pl.ds(pl.multiple_of(i * wide, wide), wide)
+            total_ref[:, at] += low_dot(gated_ref[slab], all_ref[slab, :, at], TN)
+            part_out[turn, :, at] = low_dot(activated_ref[slab], down_ref[:, at], NN).astype(BF16)
+
+        save = pltpu.make_async_copy(part_out.at[turn], part_hbm.at[slab], save_sems.at[turn])
+        save.start()
+        saves.append(save)
+
+    gather_in_turn(own_ref, all_ref, send_sems, recv_sems, use)
+    term_ref[...] = total_ref[...].astype(BF16)
+    for save in saves[-2:]:
+        save.wait()
+
+
+def gather_branch(own, gated, weight, activated, down_own, collective_id):
+    ring, rows, width = gated.shape
+    columns = own.shape[1]
+    vmem = pl.BlockSpec(memory_space=pltpu.VMEM)
+    anywhere = pl.BlockSpec(memory_space=pl.ANY)
+    return pl.pallas_call(
+        gather_branch_kernel,
+        out_shape=[
+            jax.ShapeDtypeStruct((ring, rows, width), BF16),
+            jax.ShapeDtypeStruct((width, columns), BF16),
+            jax.ShapeDtypeStruct((ring, rows, columns), BF16),
+        ],
+        in_specs=[anywhere] * 5,
+        out_specs=[vmem, vmem, anywhere],
+        scratch_shapes=[
+            pltpu.VMEM(own.shape, BF16),
+            pltpu.VMEM(gated.shape, BF16),
+            pltpu.VMEM(weight.shape, BF16),
+            pltpu.VMEM(activated.shape, BF16),
+            pltpu.VMEM(down_own.shape, BF16),
+            pltpu.VMEM((ring, rows, columns), BF16),
+            pltpu.VMEM((width, columns), F32),
+            pltpu.VMEM((2, rows, columns), BF16),
+            pltpu.SemaphoreType.DMA((9,)),
+            pltpu.SemaphoreType.DMA((9,)),
+            pltpu.SemaphoreType.DMA((5,)),
+            pltpu.SemaphoreType.DMA((2,)),
+        ],
+        compiler_params=pltpu.CompilerParams(
+            collective_id=collective_id, has_side_effects=True, vmem_limit_bytes=VMEM_LIMIT
+        ),
+        cost_estimate=lasting(45),
+        name="gather_branch",
+    )(own, gated, weight, activated, down_own)
 
 
 def rms_back(values, gain, grad):
@@ -1302,25 +1788,22 @@
     ).reshape(ring, 2, weight_rows, units)
     upstream = valid_rows * cotangent.reshape(row_count, model_width).astype(F32)
     out_err = upstream.astype(BF16)
-    normed_all, out_err_all, in_own, gate_up_cut = plane_open(
+    turns = [(depth * s + z, ring * z + s) for s in range(ring) for z in range(depth)]
+    down_own = gather_rows(down_weight, "dp")
+    out_cut = lax.ppermute(output_weight, ("dp", "seq"), turns)
+    normed_all, in_own, gate_up_cut = plane_open(
         normed_low,
-        out_err,
         in_cut.reshape(ring, weight_rows, 4 * width),
         gate_up_cut.reshape(ring, 2 * weight_rows, units),
         1,
     )
     gate_up_cut = gate_up_cut.reshape(ring, 2, weight_rows, units)
     normed_all = normed_all.reshape(all_rows, model_width)
-    out_err_all = out_err_all.reshape(all_rows, model_width)
     in_own = in_own.reshape(model_width, 4 * width)
-    in_own, output_weight, down_weight = lax.optimization_barrier(
-        (in_own, output_weight, down_weight)
-    )
-    turns = [(depth * s + z, ring * z + s) for s in range(ring) for z in range(depth)]
-    out_own = gather_rows(lax.ppermute(output_weight, ("dp", "seq"), turns), "dp")
+    in_own, out_cut, down_own = lax.optimization_barrier((in_own, out_cut, down_own))
+    out_own = gather_rows(out_cut, "dp")
     gate_own = gather_rows(gate_up_cut[:, 0].reshape(ring * weight_rows, units), "dp")
     up_own = gather_rows(gate_up_cut[:, 1].reshape(ring * weight_rows, units), "dp")
-    down_own = gather_rows(down_weight, "dp")
 
     def own_lanes(pair):
         rows = pair.shape[0]
@@ -1344,65 +1827,32 @@
     mixed = chunks(low_dot(normed_all, in_own[:, : 3 * width], NN).astype(BF16))
     gate_raw = chunks(low_dot(normed_all, in_own[:, 3 * width :], NN))
     logits = chunks(low_dot(normed_all, decay_own, NN))
-    gated, memory, inverse, fresh, mixer_out = run_forward(
-        mixed, gate_raw, logits, taps, params, gain, heads
-    )
-    gated_rows = gated.reshape(all_rows, width)
-    hidden_part = low_dot(gated_rows, out_own, NN).astype(BF16)
-    hidden = tokens + plane_scatter(hidden_part.reshape(ring, row_count, model_width), 2)
+    gated, memory, inverse, fresh, mixer_out, out_err_all = run_forward(
+        mixed, gate_raw, logits, taps, params, gain, heads, out_err, 5
+    )
+    gated = gated.reshape(ring, row_count, width)
+    hidden = tokens + plane_scatter_dot([gated], [out_own], NN, 2)[0]
     second_low = rms_norm(hidden, second_gain).astype(BF16)
-    second_all = plane_gather(second_low, 3).reshape(all_rows, model_width)
-    gate_part = low_dot(second_all, gate_own, NN)
-    up_part = low_dot(second_all, up_own, NN)
-    gate_open = jax.nn.sigmoid(gate_part)
-    activated = (gate_part * gate_open * up_part).astype(BF16)
-    down_part = low_dot(activated, down_own, NN).astype(BF16)
-
-    down_term = low_dot(activated, out_err_all, TN).astype(BF16)
-    down_term, out_err_all = lax.optimization_barrier((down_term, out_err_all))
-    activated_grad = low_dot(out_err_all, down_own, NT)
-    gate_err = (
-        activated_grad * up_part * gate_open * (1.0 + gate_part * (1.0 - gate_open))
-    ).astype(BF16)
-    up_err = (activated_grad * gate_part * gate_open).astype(BF16)
-    gate_term = low_dot(second_all, gate_err, TN).astype(BF16)
-    up_term = low_dot(second_all, up_err, TN).astype(BF16)
-    gate_term, up_term, gate_err, up_err = lax.optimization_barrier(
-        (gate_term, up_term, gate_err, up_err)
-    )
-    second_part = (low_dot(gate_err, gate_own, NT) + low_dot(up_err, up_own, NT)).astype(BF16)
-    second_grad = plane_scatter(second_part.reshape(ring, row_count, model_width), 4)
+    second_all, activated, gate_err, up_err, down_term = gather_feed(
+        second_low, gate_own, up_own, down_own, out_err_all, 3
+    )
     down_share = scatter_rows(down_term, "dp").astype(F32)
-    result = valid_rows * (hidden + plane_scatter(down_part.reshape(ring, row_count, model_width), 5))
+    second_grad, gate_term, up_term = plane_scatter_dot(
+        [gate_err, up_err],
+        [gate_own, up_own],
+        NT,
+        4,
+        second_all.reshape(all_rows, model_width),
+    )
     gate_share = scatter_rows(gate_term, "dp")
     up_share = scatter_rows(up_term, "dp")
     hidden_part, second_gain_grad = rms_back(hidden, second_gain, second_grad)
     hidden_grad = upstream + hidden_part
     branch_err = hidden_grad.astype(BF16)
-    branch_all = plane_gather(branch_err, 11).reshape(all_rows, model_width)
-    output_term = low_dot(gated_rows, branch_all, TN).astype(BF16)
-    gated_grad = low_dot(branch_all, out_own, NT).astype(BF16)
-    output_term, gated_grad = lax.optimization_barrier((output_term, gated_grad))
-    output_term, down_share, gate_share, up_share = lax.optimization_barrier(
-        (output_term, down_share, gate_share, up_share)
-    )
-    output_share = lax.ppermute(
-        scatter_rows(output_term, "dp"), ("dp", "seq"), [(b, a) for a, b in turns]
-    ).astype(F32)
-    gate_share, up_share = plane_exchange(
-        [
-            gate_share.reshape(ring, weight_rows, units),
-            up_share.reshape(ring, weight_rows, units),
-        ],
-        9,
-    )
-    gate_up_share = jnp.stack([gate_share, up_share], 1)
-    gate_up_share = jnp.transpose(
-        gate_up_share.reshape(ring, 2, weight_rows, depth, own_units), (2, 1, 3, 0, 4)
-    )
-    gate_up_share = gate_up_share.reshape(weight_rows, -1).astype(F32)
-
-    in_err, logit_grad, taps_grad, param_grad, gain_grad = run_backward(
+    gated_grad, output_term, down_part = gather_branch(
+        branch_err, gated, out_own, activated, down_own, 11
+    )
+    in_err, logit_grad, taps_grad, param_grad, gain_grad, final_part = run_backward(
         mixed,
         gate_raw,
         logits,
@@ -1414,31 +1864,45 @@
         fresh,
         mixer_out,
         gated_grad.reshape(ring, seqs, span, width),
-    )
-    in_err = in_err.reshape(all_rows, 4 * width)
-    logit_grad = logit_grad.reshape(all_rows, -1)
-    input_term = low_dot(normed_all, in_err, TN).astype(BF16)
-    input_term, in_err, logit_grad = lax.optimization_barrier((input_term, in_err, logit_grad))
-    (input_share,) = plane_exchange(
-        [scatter_rows(input_term, "dp").reshape(ring, weight_rows, 4 * width)], 10
-    )
-    input_share = jnp.transpose(
-        input_share.reshape(ring, weight_rows, 4, width), (1, 2, 0, 3)
-    )
-    input_share = input_share.reshape(weight_rows, -1).astype(F32)
-    logit_top, logit_rest = parts(logit_grad)
-    normed_part = (
-        low_dot(in_err, in_own, NT)
-        + low_dot(logit_top, decay_own, NT)
-        + low_dot(logit_rest, decay_own, NT)
-    ).astype(BF16)
-    normed_grad = plane_scatter(normed_part.reshape(ring, row_count, model_width), 6)
+        down_part,
+        12,
+    )
+    result = valid_rows * (hidden + final_part)
+    input_term = low_dot(normed_all, in_err.reshape(all_rows, 4 * width), TN).astype(BF16)
+    input_term, in_err, logit_grad, down_share, gate_share, up_share = lax.optimization_barrier(
+        (input_term, in_err, logit_grad, down_share, gate_share, up_share)
+    )
+    input_cut = scatter_rows(input_term, "dp")
+    lanes = logit_grad.shape[-1]
+    decay_twice = decay_own + jnp.roll(decay_own, lanes // 2, 1)
+    normed_grad, gate_share, up_share = plane_scatter_dot(
+        [
+            in_err.reshape(ring, row_count, 4 * width),
+            logit_grad.reshape(ring, row_count, lanes),
+        ],
+        [in_own, decay_twice],
+        NT,
+        6,
+        cuts=[
+            gate_share.reshape(ring, weight_rows, units),
+            up_share.reshape(ring, weight_rows, units),
+        ],
+    )
+    output_term, input_cut, normed_grad = lax.optimization_barrier(
+        (output_term, input_cut, normed_grad)
+    )
+    output_share = lax.ppermute(
+        scatter_rows(output_term, "dp"), ("dp", "seq"), [(b, a) for a, b in turns]
+    ).astype(F32)
+    gate_up_share = jnp.stack([gate_share, up_share], 1)
+    gate_up_share = jnp.transpose(
+        gate_up_share.reshape(ring, 2, weight_rows, depth, own_units), (2, 1, 3, 0, 4)
+    )
+    gate_up_share = gate_up_share.reshape(weight_rows, -1).astype(F32)
     token_part, first_gain_grad = rms_back(tokens, first_gain, normed_grad)
     inputs_grad = hidden_grad + token_part
-    decay_term = (low_dot(normed_all, logit_top, TN) + low_dot(normed_all, logit_rest, TN))[
-        :, : 2 * heads
-    ]
-
+    decay_term = low_dot(normed_all, logit_grad.reshape(all_rows, lanes), TN)
+    decay_term = decay_term[:, : 2 * heads] + decay_term[:, lanes // 2 : lanes // 2 + 2 * heads]
     pieces = [
         jnp.transpose(decay_term),
         taps_grad[:tap_count],
@@ -1450,7 +1914,10 @@
     sizes = [piece.size for piece in pieces]
     packed = jnp.concatenate([piece.reshape(-1) for piece in pieces])
     packed = jnp.pad(packed, (0, -packed.size % 1024)).reshape(-1, 128)
-    summed = small_sum(packed, 7).reshape(ring, -1)
+    summed, input_share = small_sum(packed, input_cut.reshape(ring, weight_rows, 4 * width), 7)
+    input_share = jnp.transpose(input_share.reshape(ring, weight_rows, 4, width), (1, 2, 0, 3))
+    input_share = input_share.reshape(weight_rows, -1).astype(F32)
+    summed = summed.reshape(ring, -1)
     parted = []
     start = 0
     for size in sizes:

time: 874 us -> 710 us (0.81)
  matrix products: 207 us -> 41.7 us
  waiting for transfers between devices: 7.83 us -> 26.7 us
  Pallas kernels: 548 us -> 533 us
  local copies, waits for them, and re-layouts: 60.5 us -> 49.1 us
    dot_general x21 -> x5, matrix products: 207 us -> 41.7 us  [low_dot(): lax.dot_general(left, right, (dims, ((), ())), preferred_element_type=F32)]
    pallas_call x9 -> x6, Pallas kernels: 310 us -> 282 us  [the longest x3 154 us: plane_scatter_dot(): pl.pallas_call(functools.partial(plane_scatter_dot_kernel, count, dims, f...]
    reduce_scatter x5, waiting for transfers between devices: 0.03 us -> 17.7 us  [scatter_rows(): return lax.psum_scatter(value, axis, scatter_dimension=0, tiled=True)]
  transfers between devices with their start and end apart: 11 -> 11, of which waited for: 1 -> 4; matrix products, arithmetic and copies ran while one was open for 29% -> 17% of each run, Pallas kernels for 49% -> 68%
where the time goes in v2:
time: 710 us; the launch traced here: 701 us
  Pallas kernels  533 us (75%)
  local copies, waits for them, and re-layouts  49.1 us (7%)
  matrix products  41.7 us (6%)
  other arithmetic  27.7 us (4%)
  waiting for transfers between devices  26.7 us (4%)
  between operations  14.8 us (2%)
  starting transfers between devices  8.05 us (1%)
    pallas_call x3, Pallas kernels, plane_scatter_dot(): pl.pallas_call(functools.partial(plane_scatter_dot_kernel, count, dims, f...  154 us
    pallas_call x1, Pallas kernels, plane_open(): pl.pallas_call(plane_open_kernel, out_shape=[jax.ShapeDtypeStruct((ring,...  116 us
    pallas_call x1, Pallas kernels, run_forward(): pl.pallas_call(mixer_forward, grid=(steps,), in_specs=[rows(3 * width), r...  79.5 us
    pallas_call x1, Pallas kernels, gather_feed(): pl.pallas_call(gather_feed_kernel, out_shape=[jax.ShapeDtypeStruct((ring,...  59.4 us
    pallas_call x1, Pallas kernels, run_backward(): pl.pallas_call(mixer_backward, grid=(steps,), in_specs=[rows(3 * width),...  56.1 us
    pallas_call x1, Pallas kernels, gather_branch(): pl.pallas_call(gather_branch_kernel, out_shape=[jax.ShapeDtypeStruct((rin...  45.1 us
    dot_general x5, matrix products, low_dot(): lax.dot_general(left, right, (dims, ((), ())), preferred_element_type=F32)  41.7 us
    pallas_call x1, Pallas kernels, small_sum(): pl.pallas_call(small_sum_kernel, out_shape=[jax.ShapeDtypeStruct((ring,)...  23.9 us
  transfers between devices with their start and end apart: 11, of which 4 were waited for; matrix products, arithmetic and copies ran while one was open for 17% of the time, Pallas kernels for 68%

profile of v2, /device:TPU:1, one launch (start us, length us, event | category | flops | bytes accessed | tf_op | source)
XLA Modules:
  0.0 701.3 jit_solution(3443003564306582433)
XLA Ops:
  7.2 0.7 all-gather.5.cloned.1.call-update
  8.0 4.6 collective-permute-start
  12.6 1.5 copy.73
  14.5 1.5 reshape.234.early_ref
  16.0 5.0 reshape.235
  21.1 2.7 copy.82
  23.8 2.7 reshape_reshape.3.later_ref
  26.8 1.3 fusion.5.first_ref
  28.1 115.7 %plane_open.1 = (bf16[8,256,2048]{2,1,0:T(8,128)(2,1)}, bf16[4,512,1024]{2,1,0:T(8,128)(2,1)}, bf16[8,128,704]{2,1,0:T(8,128)(2,1)}) custom-call(bf16[256,2048]{1,0:T(8,128)(2,1)} %fusion.5.first_ref, bf16[8,64,1024]{2,1,0:T(8,128)(2,1)} %reshape.234.early_ref, bf16[8,128,704]{2,1,0:T(8,128)(2,1)} %reshape_reshape.3.later_ref), custom_call_target="tpu_custom_call" | custom-call | bytes 315000000 | tf_op jit(solution)/shard_map/plane_open/pallas_call | solution.py:1004
  143.8 0.7 copy-done.14
  144.6 2.7 fusion.23
  148.0 0.8 constant_dynamic-slice_fusion.3
  149.2 1.2 fusion.2.own_ref
  150.5 7.1 %fusion.14.logit_ref = f32[8,2,128,128]{3,2,1,0:T(8,128)} fusion(bf16[8,2,128,2048]{3,2,1,0:T(8,128)(2,1)} %bitcast.129, bf16[2048,4]{1,0:T(8,128)(2,1)S(1)} %copy.57), kind=kOutput, calls=%fused_computation.32 | convolution fusion | flops 1073741824 | bytes 9453568 | tf_op jit(solution)/shard_map/dot_general | solution.py:1739
  157.7 0.6 pad.27.param_ref
  158.3 0.6 constant_dynamic-slice_fusion.1
  158.9 7.3 %fusion.11.gate_ref = f32[8,2,128,256]{3,2,1,0:T(8,128)} fusion(bf16[8,2,128,2048]{3,2,1,0:T(8,128)(2,1)} %bitcast.130, bf16[2048,1024]{1,0:T(8,128)(2,1)S(1)} %bitcast.141), kind=kOutput, calls=%fused_computation.27 | convolution fusion | flops 2147483648 | bytes 11534336 | tf_op jit(solution)/shard_map/dot_general | solution.py:1739
  166.2 8.2 %convolution_convert_fusion.1 = bf16[2048,768]{1,0:T(8,128)(2,1)} fusion(bf16[2048,2048]{1,0:T(8,128)(2,1)S(1)} %bitcast.135, bf16[2048,1024]{1,0:T(8,128)(2,1)S(1)} %bitcast.142), kind=kOutput, calls=%fused_computation.2 | convolution fusion | flops 6444023808 | bytes 14680064 | tf_op jit(solution)/shard_map/dot_general | solution.py:1739
  174.4 79.5 %mixer_forward.1 = (bf16[8,2,128,256]{3,2,1,0:T(8,128)(2,1)}, f32[8,2,2,128,128]{4,3,2,1,0:T(8,128)}, f32[8,2,2,128,128]{4,3,2,1,0:T(8,128)}, f32[8,2,128,256]{3...) custom-call(bf16[8,2,128,768]{3,2,1,0:T(8,128)(2,1)} %bitcast.126, ...), custom_call_target="tpu_custom_call" | custom-call | bytes 262500000 | tf_op jit(solution)/shard_map/mixer_forward/pallas_call | solution.py:705
  253.9 43.8 %plane_scatter_dot.3 = f32[256,2048]{1,0:T(8,128)} custom-call(bf16[8,256,256]{2,1,0:T(8,128)(2,1)} %bitcast.145, bf16[256,2048]{1,0:T(8,128)(2,1)} %all-gather.7.cloned.1.call-done.refs_1_.weight_hbm), custom_call_target="tpu_custom_call" | custom-call | bytes 157500000 | tf_op jit(solution)/shard_map/plane_scatter_dot/pallas_call | solution.py:1416
  297.8 2.0 multiply_reduce_fusion.2
  299.7 1.2 multiply_convert_fusion.own_hbm
  300.9 0.9 all-gather.11.cloned.1.call-done.up_hbm.refs_3_
  301.9 59.4 %gather_feed.1 = (bf16[8,256,2048]{2,1,0:T(8,128)(2,1)}, bf16[8,256,704]{2,1,0:T(8,128)(2,1)}, bf16[8,256,704]{2,1,0:T(8,128)(2,1)}, bf16[8,256,704]{2,1,0:T(8,128)(2,1)}, bf16[704,2048]{1,0:T(8,128)(2,1)}) custom-call(bf16[256,2048]{1,0:T(8,128)(2,1)} %multiply_convert_fusion.own_hbm, bf16[2048,704]{1,0:T(8,128)(2,1)} %all-gather.9.cloned.1.call-done.gate_hbm.refs_2_, ...), custom_call_target="tpu_custom_call" | custom-call | bytes 210000000 | tf_op jit(solution)/shard_map/gather_feed/pallas_call | solution.py:1594
  361.4 52.1 %plane_scatter_dot.4 = (f32[256,2048]{1,0:T(8,128)}, bf16[2048,704]{1,0:T(8,128)(2,1)}, bf16[2048,704]{1,0:T(8,128)(2,1)}) custom-call(bf16[8,256,704]{2,1,0:T(8,128)(2,1)} %get-tuple-element.68.refs_0_, bf16[8,256,704]{2,1,0:T(8,128)(2,1)} %get-tuple-element.69.refs_1_, bf16[2048,704]{1,0:T(8,128)(2,1)} %all-gather.9.cloned.1.call-done.gate_hbm.refs_2_, ...), custom_call_target="tpu_custom_call" | custom-call | bytes 157500000 | tf_op jit(solution)/shard_map/plane_scatter_dot/pallas_call | solution.py:1416
  413.6 0.7 reduce-scatter.10.cloned.1.call-update
  414.3 2.3 multiply_reduce_fusion
  416.8 2.4 fusion.21
  419.2 45.1 %gather_branch.1 = (bf16[8,256,256]{2,1,0:T(8,128)(2,1)}, bf16[256,2048]{1,0:T(8,128)(2,1)}, bf16[8,256,2048]{2,1,0:T(8,128)(2,1)}) custom-call(bf16[256,2048]{1,0:T(8,128)(2,1)} %get-tuple-element.144.own_hbm, bf16[8,256,256]{2,1,0:T(8,128)(2,1)} %bitcast.146, bf16[256,2048]{1,0:T(8,128)(2,1)} %all-gather.7.cloned.1.call-done.refs_1_.weight_hbm, ...), custom_call_target="tpu_custom_call" | custom-call | bytes 157500000 | tf_op jit(solution)/shard_map/gather_branch/pallas_call | solution.py:1698
  464.3 56.1 %mixer_backward.1 = (bf16[8,2,128,1024]{3,2,1,0:T(8,128)(2,1)}, bf16[8,2,128,128]{3,2,1,0:T(8,128)(2,1)}, f32[8,768]{1,0:T(8,128)}, f32[8,128]{1,0:T(8,128)}, f32[8,128]{1,0:T(8,128)}, /*index=5*/f32[256,2048]{1,0:T(8,128)}) custom-call(bf16[8,2,128,768]{3,2,1,0:T(8,128)(2,1)} %bitcast.127, bf16[8,2,128,768]{3,2,1,0:T(8,128)(2,1)} %bitcast.128, ...), custom_call_target="tpu_custom_call" | custom-call | bytes 192500000 | tf_op jit(solution)/shard_map/mixer_backward/pallas_call | solution.py:765
  520.5 14.4 %convolution_convert_fusion = bf16[2048,1024]{1,0:T(8,128)(2,1)} fusion(bf16[2048,2048]{1,0:T(8,128)(2,1)} %bitcast.131, bf16[2048,1024]{1,0:T(8,128)(2,1)} %bitcast.143), kind=kOutput, calls=%fused_computation.1 | convolution fusion | flops 8592031744 | bytes 16777216 | tf_op jit(solution)/shard_map/dot_general | solution.py:1739
  534.8 2.4 convert_element_type.93
  537.2 4.0 reduce-scatter.10.cloned.1.call-done
  541.3 1.1 pad_slice_fusion
  542.4 2.1 pad_add_fusion.refs_3_
  544.5 0.7 slice.70
  545.3 0.7 slice_bitcast_fusion.1
  546.0 3.2 add_multiply_fusion
  549.2 57.6 %plane_scatter_dot.5 = (f32[256,2048]{1,0:T(8,128)}, bf16[8,64,704]{2,1,0:T(8,128)(2,1)}, bf16[8,64,704]{2,1,0:T(8,128)(2,1)}) custom-call(bf16[8,256,1024]{2,1,0:T(8,128)(2,1)} %bitcast.144, bf16[8,256,128]{2,1,0:T(8,128)(2,1)} %bitcast.168, bf16[2048,1024]{1,0:T(8,128)(2,1)} %bitcast.140, bf16[2048,128]{1,0:T(8,128)(2,1)} %pad_add_fusion.refs_3_, ...), custom_call_target="tpu_custom_call" | custom-call | bytes 157500000 | tf_op jit(solution)/shard_map/plane_scatter_dot/pallas_call | solution.py:1416
  606.8 13.7 %reduce-scatter.12.cloned.1.call-done = bf16[512,1024]{1,0:T(8,128)(2,1)} async-done(((bf16[2048,1024]{1,0:T(8,128)(2,1)}), bf16[512,1024]{1,0:T(8,128)(2,1)}) %reduce-scatter.12.cloned.1.call-update) | async-done | bytes 1048592 | tf_op jit(solution)/shard_map/reduce_scatter | solution.py:823
  620.6 4.8 fusion.25
  625.4 0.8 stack.21
  626.2 3.0 stack.22
  629.2 1.5 convert_bitcast_fusion
  630.6 4.4 copy.65
  635.0 5.8 reshape.269
  641.5 0.6 pad_bitcast_fusion.own_ref
  642.2 23.9 %small_sum.1 = (f32[8,128,128]{2,1,0:T(8,128)}, bf16[8,64,1024]{2,1,0:T(8,128)(2,1)}) custom-call(f32[128,128]{1,0:T(8,128)} %pad_bitcast_fusion.own_ref, bf16[8,64,1024]{2,1,0:T(8,128)(2,1)} %bitcast.161), custom_call_target="tpu_custom_call" | custom-call | bytes 70000000 | tf_op jit(solution)/shard_map/small_sum/pallas_call | solution.py:1236
  666.1 1.4 copy.84
  667.4 0.8 copy-done.9
  668.3 3.4 fusion.8
  671.7 3.1 collective-permute-start.1
  674.8 0.9 slice.87
  675.7 1.0 slice.86
  676.8 0.6 squeeze.11
  678.3 0.9 reshape.261
  679.2 0.7 copy.77
  679.8 0.9 reshape.270
  680.8 1.2 copy.60
  682.0 2.5 copy.76
  684.6 1.3 slice_reduce_fusion.2
  685.8 1.7 slice_reduce_fusion
  687.5 5.9 collective-permute-done.1
  693.4 0.8 convert_element_type.98
  (95 shorter events, 4.4 us)
Async XLA Ops:
  7.2 151.1 %copy-start = (f32[4,6144]{1,0:T(4,128)S(1)}, f32[4,6144]{1,0:T(4,128)}, u32[]{:S(2)}) copy-start(f32[4,6144]{1,0:T(4,128)} %param.19) | copy-start | bytes 294916
  7.2 136.6 %all-gather.5.cloned.1.call-start = ((), (), s32[]{:S(2)}) async-start(), calls=%async_computation.5 | async-start | bytes 3604480 | tf_op jit(solution)/shard_map/all_gather | solution.py:819
  7.9 246.0 %all-gather.7.cloned.1.call-start = ((), (), s32[]{:S(2)}) async-start(), calls=%async_computation.6 | async-start | bytes 1310720 | tf_op jit(solution)/shard_map/all_gather | solution.py:819
  8.0 135.8 %collective-permute-start = (bf16[64,2048]{1,0:T(8,128)(2,1)}, bf16[64,2048]{1,0:T(8,128)(2,1)S(1)}, u32[]{:S(2)}, u32[]{:S(2)}) collective-permute-start(bf16[64,2048]{1,0:T(8,128)(2,1)} %param.23), channel_id=1, source_target_pairs={{0,0},{1,8},{2,16},{3,24},{4,1},{5,9},{6,17},{7,25},{8,2},{9,10},{... | collective-permute-start | bytes 786440 | tf_op jit(solution)/shard_map/ppermute | solution.py:1793
  14.1 2.0 copy-start.10
  23.7 2.7 copy-start.2
  23.7 3.0 copy-start.15
  143.8 0.7 copy-start.14
  144.5 156.4 %all-gather.9.cloned.1.call-start = ((), (), s32[]{:S(2)}) async-start(), calls=%async_computation.7 | async-start | bytes 3932160 | tf_op jit(solution)/shard_map/all_gather | solution.py:819
  144.6 4.6 copy-start.18
  144.6 4.7 copy-start.7
  147.4 154.5 %all-gather.11.cloned.1.call-start = ((), (), s32[]{:S(2)}) async-start(), calls=%async_computation.8 | async-start | bytes 3932160 | tf_op jit(solution)/shard_map/all_gather | solution.py:819
  147.9 386.9 %reduce-scatter.6.cloned.1.call-start = ((), (), s32[]{:S(2)}) async-start(), calls=%async_computation.9 | async-start | bytes 3604480 | tf_op jit(solution)/shard_map/reduce_scatter | solution.py:823
  149.1 8.5 %copy-start.4 = (bf16[2048,4]{1,0:T(8,128)(2,1)}, bf16[2048,4]{1,0:T(8,128)(2,1)S(1)}, u32[]{:S(2)}) copy-start(bf16[2048,4]{1,0:T(8,128)(2,1)S(1)} %copy.57) | copy-start | bytes 49156
  150.5 7.1 %copy-start.19 = (f32[16]{0:T(128)S(1)}, f32[16]{0:T(128)}, u32[]{:S(2)}) copy-start(f32[16]{0:T(128)} %param.21) | copy-start | bytes 196
  150.5 7.1 %copy-start.20 = (f32[16]{0:T(128)S(1)}, f32[16]{0:T(128)}, u32[]{:S(2)}) copy-start(f32[16]{0:T(128)} %param.20) | copy-start | bytes 196
  150.5 8.4 %copy-start.6 = (bf16[4,512,1024]{2,1,0:T(8,128)(2,1)S(1)}, bf16[4,512,1024]{2,1,0:T(8,128)(2,1)}, u32[]{:S(2)}) copy-start(bf16[4,512,1024]{2,1,0:T(8,128)(2,1)} %get-tuple-element.57) | copy-start | bytes 12582916
  150.5 15.7 %slice-start = ((s8[8388608]{0:T(1024)(128)(4,1)}), s8[4194304]{0:T(1024)(128)(4,1)S(1)}, s32[]{:S(2)}) async-start(s8[8388608]{0:T(1024)(128)(4,1)} %bitcast.133), calls=%async_computation.14 | async-start | bytes 8388608
  158.9 7.3 %slice-start.1 = ((s8[8388608]{0:T(1024)(128)(4,1)}), s8[4194304]{0:T(1024)(128)(4,1)S(1)}, s32[]{:S(2)}) async-start(s8[8388608]{0:T(1024)(128)(4,1)} %bitcast.133), calls=%async_computation.15 | async-start | bytes 8388608
  297.8 2.0 copy-start.16
  361.4 175.8 %reduce-scatter.8.cloned.1.call-start = ((), (), s32[]{:S(2)}) async-start(), calls=%async_computation.10 | async-start | bytes 3932160 | tf_op jit(solution)/shard_map/reduce_scatter | solution.py:823
  413.5 127.7 %reduce-scatter.10.cloned.1.call-start = ((), (), s32[]{:S(2)}) async-start(), calls=%async_computation.11 | async-start | bytes 3932160 | tf_op jit(solution)/shard_map/reduce_scatter | solution.py:823
  414.3 206.3 %reduce-scatter.12.cloned.1.call-start = ((), (), s32[]{:S(2)}) async-start(), calls=%async_computation.12 | async-start | bytes 5242880 | tf_op jit(solution)/shard_map/reduce_scatter | solution.py:823
  414.3 2.3 copy-start.5
  414.3 2.5 copy-start.8
  541.2 4.1 copy-start.17
  541.2 130.5 %reduce-scatter.14.cloned.1.call-start = ((), (), s32[]{:S(2)}) async-start(), calls=%async_computation.13 | async-start | bytes 1310720 | tf_op jit(solution)/shard_map/reduce_scatter | solution.py:823
  549.2 71.4 %copy-start.13 = (bf16[8,2,128,128]{3,2,1,0:T(8,128)(2,1)S(1)}, bf16[8,2,128,128]{3,2,1,0:T(8,128)(2,1)}, u32[]{:S(2)}) copy-start(bf16[8,2,128,128]{3,2,1,0:T(8,128)(2,1)} %get-tuple-element.84) | copy-start | bytes 1572868
  620.6 4.8 copy-start.12
  635.0 5.8 copy-start.3
  667.4 0.8 copy-start.9
  671.7 8.1 %copy-start.11 = (bf16[8,64,1024]{2,1,0:T(8,128)(2,1)S(1)}, bf16[8,64,1024]{2,1,0:T(8,128)(2,1)}, u32[]{:S(2)}) copy-start(bf16[8,64,1024]{2,1,0:T(8,128)(2,1)} %get-tuple-element.94) | copy-start | bytes 3145732
  671.7 21.7 %collective-permute-start.1 = (bf16[64,2048]{1,0:T(8,128)(2,1)}, bf16[64,2048]{1,0:T(8,128)(2,1)S(1)}, u32[]{:S(2)}, u32[]{:S(2)}) collective-permute-start(bf16[64,2048]{1,0:T(8,128)(2,1)} %reduce-scatter.14.cloned.1.call-done), channel_id=1, source_target_pairs={{0,0},{8,1},{16,2},{24,3},{1,4},{9,5},{17,6},{25,7},{2,8},{10,9},{... | collective-permute-start | bytes 786440 | tf_op jit(solution)/shard_map/ppermute | solution.py:1894
  682.0 12.3 %copy-start.1 = (f32[4,6144]{1,0:T(4,128)S(1)}, f32[4,6144]{1,0:T(4,128)}, u32[]{:S(2)}) copy-start(f32[4,6144]{1,0:T(4,128)} %param.19) | copy-start | bytes 294916
Sparse Core Ops, SparseCore 0:
  9.6 78.6 all-gather.4
  144.6 27.6 all-gather.6
  174.5 63.1 all-gather.8
  239.7 62.1 all-gather.10
  361.5 54.7 reduce-scatter.5
  418.4 60.1 reduce-scatter.7
  480.9 60.2 reduce-scatter.9
  543.5 76.9 reduce-scatter.11
  622.9 27.4 reduce-scatter.13

commit v3 on v2

--- a/solution.py
+++ b/solution.py
@@ -354,21 +354,28 @@
     )
 
 
-def lower_inverse(strict_lower, row_index, col_index):
-    extent = strict_lower.shape[0]
+def lower_inverses(strict_lowers, row_index, col_index):
+    extent = row_index.shape[0]
 
     def below(width):
         same = (row_index // (2 * width)) == (col_index // (2 * width))
         return same & ((row_index // width) % 2 == 1) & ((col_index // width) % 2 == 0)
 
-    inverse = jnp.where(row_index == col_index, 1.0, 0.0) - jnp.where(below(1), strict_lower, 0.0)
+    mask = below(1)
+    identity = jnp.where(row_index == col_index, 1.0, 0.0)
+    inverses = [identity - jnp.where(mask, strict, 0.0) for strict in strict_lowers]
     width = 2
     while width < extent:
-        block = jnp.where(below(width), strict_lower, 0.0)
-        split = parts(inverse)
-        inverse = inverse - mm(parts(mm(split, parts(block))), split)
+        mask = below(width)
+        splits = [parts(inverse) for inverse in inverses]
+        blocks = [parts(jnp.where(mask, strict, 0.0)) for strict in strict_lowers]
+        halves = [mm(split, block) for split, block in zip(splits, blocks)]
+        inverses = [
+            inverse - mm(parts(half), split)
+            for inverse, half, split in zip(inverses, halves, splits)
+        ]
         width *= 2
-    return inverse
+    return inverses
 
 
 def active_rows(before, rows, taps):
@@ -444,52 +451,68 @@
     ones = jnp.where(col_index <= row_index, 1.0, 0.0).astype(BF16)
     taps = taps_ref[...]
     width = heads * head_size
+    pairs = [(m, h) for m in range(seqs) for h in range(heads)]
+    active, decay_parts = [], []
     for m in range(seqs):
         rows = mixed_ref[m].astype(F32)
         convolved, _ = active_rows(halo_ref[m], rows, taps)
         halo_ref[m] = rows[span - 8 :]
-        active = convolved * sigmoid(convolved)
-        _, decays, strengths, running = decay_terms(logit_ref[m], param_ref, heads, ones)
-        running_rows = jnp.transpose(running)
-        strength_rows = jnp.transpose(strengths)
-        for h in range(heads):
-            own = slice(h * head_size, (h + 1) * head_size)
-            queries = unit(active[:, own])[0] * head_size ** (-0.5)
-            probes = unit(active[:, width + h * head_size : width + (h + 1) * head_size])[0]
-            writes = active[:, 2 * width + h * head_size : 2 * width + (h + 1) * head_size]
-            run = running[:, h : h + 1]
-            last = running[span - 1 : span, h : h + 1]
-            weight_row = strength_rows[heads + h : heads + h + 1, :]
-            weight_col = strengths[:, heads + h : heads + h + 1]
-            faded = jnp.exp(jnp.minimum(run - running_rows[h : h + 1, :], 0.0)) * weight_row
-            probe_parts = parts(probes)
-            query_parts = parts(queries)
-            strict = jnp.where(col_index < row_index, faded * mm_nt(probe_parts, probe_parts), 0.0)
-            mixing = jnp.where(col_index <= row_index, faded * mm_nt(query_parts, probe_parts), 0.0)
-            inverse = lower_inverse(strict, row_index, col_index)
-            scale_in = jnp.exp(run)
-            both = mm(
-                parts(inverse), parts(jnp.concatenate([writes, scale_in * probes], 1))
-            )
-            memory = state_ref[m, h]
-            memory_parts = parts(memory)
-            reads = mm(
-                parts(jnp.concatenate([both[:, head_size:], scale_in * queries], 0)), memory_parts
-            )
-            fresh = both[:, :head_size] - reads[:span]
-            fresh_parts = parts(fresh)
-            mixer_out = reads[span:] + mm(parts(mixing), fresh_parts)
-            kept = jnp.transpose(jnp.exp(last - run) * weight_col * probes)
-            state_ref[m, h] = jnp.exp(last) * memory + mm(parts(kept), fresh_parts)
-            memory_ref[m, h] = memory
-            inverse_ref[m, h] = inverse
-            fresh_ref[m, :, own] = fresh
-            out_ref[m, :, own] = mixer_out
-            scale = lax.rsqrt(jnp.mean(mixer_out * mixer_out, -1, keepdims=True) + 1e-05)
-            gate = gate_ref[m, :, own]
-            gated_ref[m, :, own] = (
-                mixer_out * scale * gain_ref[...] * (gate * sigmoid(gate))
-            ).astype(BF16)
+        active.append(convolved * sigmoid(convolved))
+        _, _, strengths, running = decay_terms(logit_ref[m], param_ref, heads, ones)
+        decay_parts.append((strengths, running, jnp.transpose(strengths), jnp.transpose(running)))
+
+    def columns(m, h, block):
+        start = block * width + h * head_size
+        return active[m][:, start : start + head_size]
+
+    queries = [unit(columns(m, h, 0))[0] * head_size ** (-0.5) for m, h in pairs]
+    probes = [unit(columns(m, h, 1))[0] for m, h in pairs]
+    products = [
+        mm_nt(parts(jnp.concatenate([query, probe], 0)), parts(probe))
+        for query, probe in zip(queries, probes)
+    ]
+    stricts, mixings, scales, kepts, lasts = [], [], [], [], []
+    for (m, h), probe, product in zip(pairs, probes, products):
+        strengths, running, strength_rows, running_rows = decay_parts[m]
+        run = running[:, h : h + 1]
+        last = running[span - 1 : span, h : h + 1]
+        weight_row = strength_rows[heads + h : heads + h + 1, :]
+        weight_col = strengths[:, heads + h : heads + h + 1]
+        faded = jnp.exp(jnp.minimum(run - running_rows[h : h + 1, :], 0.0)) * weight_row
+        mixings.append(jnp.where(col_index <= row_index, faded * product[:span], 0.0))
+        stricts.append(jnp.where(col_index < row_index, faded * product[span:], 0.0))
+        scales.append(jnp.exp(run))
+        kepts.append(jnp.transpose(jnp.exp(last - run) * weight_col * probe))
+        lasts.append(jnp.exp(last))
+    inverses = lower_inverses(stricts, row_index, col_index)
+    boths = [
+        mm(parts(inverse), parts(jnp.concatenate([columns(m, h, 2), scale * probe], 1)))
+        for (m, h), inverse, scale, probe in zip(pairs, inverses, scales, probes)
+    ]
+    memories = [state_ref[m, h] for m, h in pairs]
+    reads = [
+        mm(parts(jnp.concatenate([both[:, head_size:], scale * query], 0)), parts(memory))
+        for both, scale, query, memory in zip(boths, scales, queries, memories)
+    ]
+    freshes = [both[:, :head_size] - read[:span] for both, read in zip(boths, reads)]
+    fresh_parts = [parts(fresh) for fresh in freshes]
+    for (m, h), last, memory, kept, fresh in zip(pairs, lasts, memories, kepts, fresh_parts):
+        state_ref[m, h] = last * memory + mm(parts(kept), fresh)
+    outs = [
+        read[span:] + mm(parts(mixing), fresh)
+        for read, mixing, fresh in zip(reads, mixings, fresh_parts)
+    ]
+    for (m, h), memory, inverse, fresh, mixer_out in zip(pairs, memories, inverses, freshes, outs):
+        own = slice(h * head_size, (h + 1) * head_size)
+        memory_ref[m, h] = memory
+        inverse_ref[m, h] = inverse
+        fresh_ref[m, :, own] = fresh
+        out_ref[m, :, own] = mixer_out
+        scale = lax.rsqrt(jnp.mean(mixer_out * mixer_out, -1, keepdims=True) + 1e-05)
+        gate = gate_ref[m, :, own]
+        gated_ref[m, :, own] = (
+            mixer_out * scale * gain_ref[...] * (gate * sigmoid(gate))
+        ).astype(BF16)
 
 
 def mixer_backward(
@@ -539,120 +562,166 @@
     width = heads * head_size
     gain = gain_ref[...]
     edge = before_ref.shape[1]
+    pairs = [(m, h) for m in range(seqs) for h in range(heads)]
+    everyone = range(len(pairs))
+    active, openings, curves, shifts, decay_parts = [], [], [], [], []
     for m in range(seqs):
         rows = mixed_ref[m].astype(F32)
         before = jnp.where(first, 0.0, before_ref[m].astype(F32))[edge - 8 :]
-        convolved, shifts = active_rows(before, rows, taps)
+        convolved, moved = active_rows(before, rows, taps)
         opening = sigmoid(convolved)
-        active = convolved * opening
-        logit = logit_ref[m]
-        shifted_logit, decays, strengths, running = decay_terms(logit, param_ref, heads, ones)
-        running_rows = jnp.transpose(running)
-        strength_rows = jnp.transpose(strengths)
-        active_grads = [None] * (3 * heads)
-        gate_grads = [None] * heads
-        col_terms = jnp.zeros((span, span), F32)
-        row_terms = jnp.zeros((span, span), F32)
-        for h in range(heads):
-            own = slice(h * head_size, (h + 1) * head_size)
-            raw_queries = active[:, own]
-            raw_probes = active[:, width + h * head_size : width + (h + 1) * head_size]
-            queries, query_scale = unit(raw_queries)
-            queries = queries * head_size ** (-0.5)
-            probes, probe_scale = unit(raw_probes)
-            mixer_out = out_ref[m, :, own]
-            gate = gate_ref[m, :, own]
-            gated_grad = grad_ref[m, :, own].astype(F32)
-            scale = lax.rsqrt(jnp.mean(mixer_out * mixer_out, -1, keepdims=True) + 1e-05)
-            gate_open = sigmoid(gate)
-            normal = mixer_out * scale
-            gate_grads[h] = gated_grad * normal * gain * (gate_open * (1.0 + gate * (1.0 - gate_open)))
-            normal_grad = gated_grad * (gate * gate_open)
-            gain_grad_ref[0:1, :] += jnp.sum(normal_grad * normal, 0, keepdims=True)
-            weighted = normal_grad * gain
-            out_grad = scale * (
-                weighted - normal * jnp.mean(weighted * normal, -1, keepdims=True)
+        active.append(convolved * opening)
+        curves.append(convolved)
+        openings.append(opening)
+        shifts.append(moved)
+        shifted_logit, decays, strengths, running = decay_terms(
+            logit_ref[m], param_ref, heads, ones
+        )
+        decay_parts.append(
+            (
+                shifted_logit,
+                decays,
+                strengths,
+                running,
+                jnp.transpose(strengths),
+                jnp.transpose(running),
             )
-
-            run = running[:, h : h + 1]
-            last = running[span - 1 : span, h : h + 1]
-            weight_row = strength_rows[heads + h : heads + h + 1, :]
-            weight_col = strengths[:, heads + h : heads + h + 1]
-            faded = jnp.exp(jnp.minimum(run - running_rows[h : h + 1, :], 0.0))
-            scale_in = jnp.exp(run)
-            end_scale = jnp.exp(last)
-            remaining = jnp.exp(last - run)
-            kept = remaining * weight_col
-
-            memory = memory_ref[m, h]
-            fresh = fresh_ref[m, :, own]
-            state_grad = state_ref[m, h]
-            probe_parts = parts(probes)
-            query_parts = parts(queries)
-            fresh_parts = parts(fresh)
-            memory_parts = parts(memory)
-            state_grad_parts = parts(state_grad)
-            products = mm_nt(parts(jnp.concatenate([queries, probes], 0)), probe_parts)
-            fade_query = jnp.where(col_index <= row_index, faded * products[:span], 0.0)
-            fade_probe = jnp.where(col_index < row_index, faded * products[span:], 0.0)
-            out_grad_parts = parts(out_grad)
-            probe_state = mm(probe_parts, state_grad_parts)
-            fresh_grad = (
-                mm(parts(jnp.transpose(fade_query * weight_row)), out_grad_parts)
-                + kept * probe_state
-            )
-            solved = mm(parts(jnp.transpose(inverse_ref[m, h])), parts(fresh_grad))
-            turned_queries = parts(jnp.transpose(queries))
-            turned_probes = parts(jnp.transpose(probes))
-            state_ref[m, h] = (
-                end_scale * state_grad
-                + mm(turned_queries, parts(scale_in * out_grad))
-                - mm(turned_probes, parts(scale_in * solved))
-            )
-            joined = parts(jnp.concatenate([out_grad, solved], 0))
-            outer = mm_nt(joined, fresh_parts)
-            mixing_grad = jnp.where(col_index <= row_index, outer[:span], 0.0)
-            strict_grad = jnp.where(col_index < row_index, -outer[span:], 0.0)
-            through = mm_nt(joined, memory_parts)
-            out_state = scale_in * through[:span]
-            solved_state = scale_in * through[span:]
-            spread = faded * weight_row
-            mix_fade = mixing_grad * spread
-            strict_fade = strict_grad * spread
-            on_probes = mm(parts(jnp.concatenate([mix_fade, strict_fade], 0)), probe_parts)
-            query_grad = out_state + on_probes[:span]
-            probe_grad = (
-                kept * mm_nt(fresh_parts, state_grad_parts)
-                - solved_state
-                + on_probes[span:]
-                + mm(parts(jnp.transpose(mix_fade)), query_parts)
-                + mm(parts(jnp.transpose(strict_fade)), probe_parts)
-            )
-            pairs = mixing_grad * fade_query + strict_grad * fade_probe
-            weighted_pairs = pairs * weight_row
-            probe_fresh = jnp.sum(probe_state * fresh, -1, keepdims=True)
-            run_col = (
-                jnp.sum(out_state * queries - solved_state * probes, -1, keepdims=True)
-                + jnp.sum(weighted_pairs, -1, keepdims=True)
-                - kept * probe_fresh
-            )
-            last_grad = jnp.sum(kept * probe_fresh, 0, keepdims=True) + end_scale * jnp.sum(
-                jnp.sum(state_grad * memory, -1, keepdims=True), 0, keepdims=True
-            )
-            run_col = run_col + jnp.where(row_index[:, 0:1] == span - 1, last_grad, 0.0)
-            col_terms = jnp.where(col_index == h, run_col, col_terms)
-            col_terms = jnp.where(col_index == heads + h, remaining * probe_fresh, col_terms)
-            row_terms = jnp.where(
-                row_index == h, -jnp.sum(weighted_pairs, 0, keepdims=True), row_terms
-            )
-            row_terms = jnp.where(
-                row_index == heads + h, jnp.sum(pairs, 0, keepdims=True), row_terms
-            )
-            active_grads[h] = unit_back(raw_queries, query_scale, query_grad) * head_size ** (-0.5)
-            active_grads[heads + h] = unit_back(raw_probes, probe_scale, probe_grad)
-            active_grads[2 * heads + h] = solved
-
-        terms = col_terms + jnp.transpose(row_terms)
+        )
+
+    def columns(m, h, block):
+        start = block * width + h * head_size
+        return active[m][:, start : start + head_size]
+
+    raw_queries = [columns(m, h, 0) for m, h in pairs]
+    raw_probes = [columns(m, h, 1) for m, h in pairs]
+    query_units = [unit(value) for value in raw_queries]
+    probe_units = [unit(value) for value in raw_probes]
+    queries = [value * head_size ** (-0.5) for value, _ in query_units]
+    probes = [value for value, _ in probe_units]
+    gate_grads, out_grads = [], []
+    for m, h in pairs:
+        own = slice(h * head_size, (h + 1) * head_size)
+        mixer_out = out_ref[m, :, own]
+        gate = gate_ref[m, :, own]
+        gated_grad = grad_ref[m, :, own].astype(F32)
+        scale = lax.rsqrt(jnp.mean(mixer_out * mixer_out, -1, keepdims=True) + 1e-05)
+        gate_open = sigmoid(gate)
+        normal = mixer_out * scale
+        gate_grads.append(
+            gated_grad * normal * gain * (gate_open * (1.0 + gate * (1.0 - gate_open)))
+        )
+        normal_grad = gated_grad * (gate * gate_open)
+        gain_grad_ref[0:1, :] += jnp.sum(normal_grad * normal, 0, keepdims=True)
+        weighted = normal_grad * gain
+        out_grads.append(
+            scale * (weighted - normal * jnp.mean(weighted * normal, -1, keepdims=True))
+        )
+
+    probe_parts = [parts(value) for value in probes]
+    query_parts = [parts(value) for value in queries]
+    out_grad_parts = [parts(value) for value in out_grads]
+    state_grads = [state_ref[m, h] for m, h in pairs]
+    state_grad_parts = [parts(value) for value in state_grads]
+    products = [
+        mm_nt(parts(jnp.concatenate([query, probe], 0)), probe_part)
+        for query, probe, probe_part in zip(queries, probes, probe_parts)
+    ]
+    probe_states = [mm(left, right) for left, right in zip(probe_parts, state_grad_parts)]
+    weight_rows, spreads, fade_queries, fade_probes = [], [], [], []
+    scales, end_scales, remainings, kepts = [], [], [], []
+    for (m, h), product in zip(pairs, products):
+        _, _, strengths, running, strength_rows, running_rows = decay_parts[m]
+        run = running[:, h : h + 1]
+        last = running[span - 1 : span, h : h + 1]
+        weight_row = strength_rows[heads + h : heads + h + 1, :]
+        weight_rows.append(weight_row)
+        faded = jnp.exp(jnp.minimum(run - running_rows[h : h + 1, :], 0.0))
+        spreads.append(faded * weight_row)
+        fade_queries.append(jnp.where(col_index <= row_index, faded * product[:span], 0.0))
+        fade_probes.append(jnp.where(col_index < row_index, faded * product[span:], 0.0))
+        scales.append(jnp.exp(run))
+        end_scales.append(jnp.exp(last))
+        remaining = jnp.exp(last - run)
+        remainings.append(remaining)
+        kepts.append(remaining * strengths[:, heads + h : heads + h + 1])
+    fresh_grads = [
+        mm(parts(jnp.transpose(fade * weight_row)), out_grad) + kept * probe_state
+        for fade, weight_row, out_grad, kept, probe_state in zip(
+            fade_queries, weight_rows, out_grad_parts, kepts, probe_states
+        )
+    ]
+    solves = [
+        mm(parts(jnp.transpose(inverse_ref[m, h])), parts(fresh_grad))
+        for (m, h), fresh_grad in zip(pairs, fresh_grads)
+    ]
+    for k in everyone:
+        m, h = pairs[k]
+        state_ref[m, h] = (
+            end_scales[k] * state_grads[k]
+            + mm(parts(jnp.transpose(queries[k])), parts(scales[k] * out_grads[k]))
+            - mm(parts(jnp.transpose(probes[k])), parts(scales[k] * solves[k]))
+        )
+    freshes = [fresh_ref[m, :, h * head_size : (h + 1) * head_size] for m, h in pairs]
+    memories = [memory_ref[m, h] for m, h in pairs]
+    fresh_parts = [parts(value) for value in freshes]
+    joined = [
+        parts(jnp.concatenate([out_grad, solved], 0)) for out_grad, solved in zip(out_grads, solves)
+    ]
+    outers = [mm_nt(both, fresh) for both, fresh in zip(joined, fresh_parts)]
+    throughs = [mm_nt(both, parts(memory)) for both, memory in zip(joined, memories)]
+    mixing_grads = [jnp.where(col_index <= row_index, outer[:span], 0.0) for outer in outers]
+    strict_grads = [jnp.where(col_index < row_index, -outer[span:], 0.0) for outer in outers]
+    mix_fades = [grad * spread for grad, spread in zip(mixing_grads, spreads)]
+    strict_fades = [grad * spread for grad, spread in zip(strict_grads, spreads)]
+    on_probes = [
+        mm(parts(jnp.concatenate([mix, strict], 0)), probe)
+        for mix, strict, probe in zip(mix_fades, strict_fades, probe_parts)
+    ]
+    fresh_states = [mm_nt(fresh, grad) for fresh, grad in zip(fresh_parts, state_grad_parts)]
+    turned = [
+        mm(parts(jnp.transpose(mix)), query) + mm(parts(jnp.transpose(strict)), probe)
+        for mix, strict, query, probe in zip(mix_fades, strict_fades, query_parts, probe_parts)
+    ]
+    active_grads = [[None] * (3 * heads) for _ in range(seqs)]
+    col_terms = [jnp.zeros((span, span), F32)] * seqs
+    row_terms = [jnp.zeros((span, span), F32)] * seqs
+    for k in everyone:
+        m, h = pairs[k]
+        out_state = scales[k] * throughs[k][:span]
+        solved_state = scales[k] * throughs[k][span:]
+        query_grad = out_state + on_probes[k][:span]
+        probe_grad = kepts[k] * fresh_states[k] - solved_state + on_probes[k][span:] + turned[k]
+        pair_terms = mixing_grads[k] * fade_queries[k] + strict_grads[k] * fade_probes[k]
+        weighted_pairs = pair_terms * weight_rows[k]
+        probe_fresh = jnp.sum(probe_states[k] * freshes[k], -1, keepdims=True)
+        run_col = (
+            jnp.sum(out_state * queries[k] - solved_state * probes[k], -1, keepdims=True)
+            + jnp.sum(weighted_pairs, -1, keepdims=True)
+            - kepts[k] * probe_fresh
+        )
+        last_grad = jnp.sum(kepts[k] * probe_fresh, 0, keepdims=True) + end_scales[k] * jnp.sum(
+            jnp.sum(state_grads[k] * memories[k], -1, keepdims=True), 0, keepdims=True
+        )
+        run_col = run_col + jnp.where(row_index[:, 0:1] == span - 1, last_grad, 0.0)
+        col_terms[m] = jnp.where(col_index == h, run_col, col_terms[m])
+        col_terms[m] = jnp.where(
+            col_index == heads + h, remainings[k] * probe_fresh, col_terms[m]
+        )
+        row_terms[m] = jnp.where(
+            row_index == h, -jnp.sum(weighted_pairs, 0, keepdims=True), row_terms[m]
+        )
+        row_terms[m] = jnp.where(
+            row_index == heads + h, jnp.sum(pair_terms, 0, keepdims=True), row_terms[m]
+        )
+        active_grads[m][h] = unit_back(
+            raw_queries[k], query_units[k][1], query_grad
+        ) * head_size ** (-0.5)
+        active_grads[m][heads + h] = unit_back(raw_probes[k], probe_units[k][1], probe_grad)
+        active_grads[m][2 * heads + h] = solves[k]
+
+    for m in range(seqs):
+        shifted_logit, decays, strengths = decay_parts[m][:3]
+        terms = col_terms[m] + jnp.transpose(row_terms[m])
         decay_grad = ones_dot(ones_back, terms)
         shifted_grad = decay_grad * -jnp.exp(param_ref[0:1, :]) * sigmoid(shifted_logit)
         logit_grad = jnp.where(
@@ -671,8 +740,8 @@
         param_grad_ref[1:2, :] += jnp.sum(
             jnp.where(decay_lane, shifted_grad, 0.0), 0, keepdims=True
         )
-        conv_grad = jnp.concatenate(active_grads, 1) * (
-            opening * (1.0 + convolved * (1.0 - opening))
+        conv_grad = jnp.concatenate(active_grads[m], 1) * (
+            openings[m] * (1.0 + curves[m] * (1.0 - openings[m]))
         )
         extended = jnp.concatenate([conv_grad, halo_ref[m]], 0)
         halo_ref[m] = conv_grad[:8]
@@ -680,8 +749,10 @@
         for j in range(tap_count):
             reach = tap_count - 1 - j
             mixed_grad = mixed_grad + taps[j : j + 1] * extended[reach : reach + span]
-            taps_grad_ref[j : j + 1, :] += jnp.sum(conv_grad * shifts[j], 0, keepdims=True)
-        error_ref[m] = jnp.concatenate([mixed_grad] + gate_grads, 1).astype(BF16)
+            taps_grad_ref[j : j + 1, :] += jnp.sum(conv_grad * shifts[m][j], 0, keepdims=True)
+        error_ref[m] = jnp.concatenate(
+            [mixed_grad] + gate_grads[m * heads : (m + 1) * heads], 1
+        ).astype(BF16)
 
 
 def run_forward(mixed, gate, logits, taps, params, gain, heads, own, collective_id):
@@ -733,7 +804,7 @@
         compiler_params=pltpu.CompilerParams(
             collective_id=collective_id, has_side_effects=True, vmem_limit_bytes=VMEM_LIMIT
         ),
-        cost_estimate=lasting(75),
+        cost_estimate=lasting(55),
         name="mixer_forward",
     )(mixed, gate, logits, taps, params, gain, own)
 
@@ -890,7 +961,7 @@
     yield
 
 
-def chain_phases(all_ref, up_send, up_recv, down_send, down_recv):
+def chain_hops(all_ref, up_send, up_recv, down_send, down_recv):
     depth = all_ref.shape[0]
     place = lax.axis_index("dp")
     above, below = lax.rem(place + 1, depth), lax.rem(place + depth - 1, depth)
@@ -905,21 +976,61 @@
             device_id_type=pl.DeviceIdType.MESH,
         )
 
-    ups, downs = [], []
+    hops = []
     for t in range(depth - 1):
         up = hop(lax.rem(place + depth - t, depth), above, up_send.at[t], up_recv.at[t])
         down = hop(lax.rem(place + t, depth), below, down_send.at[t], down_recv.at[t])
-        ups.append(up)
-        downs.append(down)
-        pl.when((place < depth - 1) & (place >= t))(up.start)
-        pl.when((place > 0) & (place + t < depth))(down.start)
-        yield
-        pl.when(place > t)(up.wait_recv)
-        pl.when(place + t + 1 < depth)(down.wait_recv)
-    for t in range(depth - 1):
-        pl.when((place < depth - 1) & (place >= t))(ups[t].wait_send)
-        pl.when((place > 0) & (place + t < depth))(downs[t].wait_send)
-    yield
+        below_slot, above_slot = place + depth - 1 - t, place + 1 + t
+        hops.append(
+            (
+                (up, (place < depth - 1) & (place >= t), place > t, lax.rem(below_slot, depth)),
+                (
+                    down,
+                    (place > 0) & (place + t < depth),
+                    above_slot < depth,
+                    lax.rem(above_slot, depth),
+                ),
+            )
+        )
+    return hops
+
+
+def hop_start(hop):
+    for copy, leaves, _, _ in hop:
+        pl.when(leaves)(copy.start)
+
+
+def hop_arrive(hop):
+    for copy, _, arrives, _ in hop:
+        pl.when(arrives)(copy.wait_recv)
+
+
+def hop_finish(hops):
+    for hop in hops:
+        for copy, leaves, _, _ in hop:
+            pl.when(leaves)(copy.wait_send)
+
+
+def greet_all(ring, depth):
+    me, place = lax.axis_index("seq"), lax.axis_index("dp")
+    barrier = pltpu.get_barrier_semaphore()
+    for axis, index, size in (("seq", me, ring), ("dp", place, depth)):
+        for k in range(1, size):
+            pl.semaphore_signal(
+                barrier,
+                inc=1,
+                device_id={axis: lax.rem(index + k, size)},
+                device_id_type=pl.DeviceIdType.MESH,
+            )
+    pl.semaphore_wait(barrier, ring + depth - 2)
+
+
+def spread_units(piece, target_ref, depth):
+    ring, _, columns = piece.shape
+    own = columns // (2 * depth)
+    for k in range(2 * depth):
+        block = jnp.concatenate([piece[s, :, k * own : (k + 1) * own] for s in range(ring)], 1)
+        target_ref[:, k * ring * own : (k + 1) * ring * own] = block.astype(target_ref.dtype)
 
 
 def exchange_copies(cut_ref, land, send_sems, recv_sems, start):
@@ -938,88 +1049,167 @@
 
 def plane_open_kernel(
     first_ref,
-    early_ref,
-    later_ref,
+    weight_hbm,
+    pair_hbm,
+    lanes_hbm,
+    first_all_hbm,
+    weight_all_hbm,
+    pair_all_ref,
+    mixed_ref,
+    gate_ref,
+    logit_ref,
     first_all_ref,
-    early_all_ref,
-    later_all_ref,
+    weight_all_ref,
+    pair_ref,
+    cut_ref,
+    lanes_ref,
+    total_ref,
     send_sems,
     recv_sems,
     local_sems,
-    up_send,
-    up_recv,
-    down_send,
-    down_recv,
+    *chain_sems,
 ):
     place, me = lax.axis_index("dp"), lax.axis_index("seq")
-    depth, ring = early_all_ref.shape[0], early_ref.shape[0]
-    rows = early_ref.shape[1]
-    barrier = pltpu.get_barrier_semaphore()
-    for k in range(1, ring):
-        pl.semaphore_signal(
-            barrier,
-            inc=1,
-            device_id={"seq": lax.rem(me + k, ring)},
-            device_id_type=pl.DeviceIdType.MESH,
-        )
-    for k in range(1, depth):
-        pl.semaphore_signal(
-            barrier,
-            inc=1,
-            device_id={"dp": lax.rem(place + k, depth)},
-            device_id_type=pl.DeviceIdType.MESH,
-        )
-    pl.semaphore_wait(barrier, ring + depth - 2)
-    spot = early_all_ref.at[place, pl.ds(pl.multiple_of(me * rows, rows), rows)]
-    keep_early = pltpu.make_async_copy(early_ref.at[me], spot, local_sems.at[0])
-    keep_early.start()
-    keep_later = pltpu.make_async_copy(later_ref.at[me], later_all_ref.at[me], local_sems.at[1])
-    keep_later.start()
-    early = exchange_copies(early_ref, spot, send_sems, recv_sems, 0)
+    depth, rows = weight_all_ref.shape[0], weight_hbm.shape[0]
+    ring, units = cut_ref.shape[0], cut_ref.shape[2] // 2
+    width = weight_all_ref.shape[2] // 4
+    load = pltpu.make_async_copy(pair_hbm, pair_ref, local_sems.at[0])
+    load.start()
+    lanes_load = pltpu.make_async_copy(lanes_hbm, lanes_ref, local_sems.at[3])
+    lanes_load.start()
+    greet_all(ring, depth)
+    keeps, early = [], []
+    own_rows = pl.ds(pl.multiple_of(me * rows, rows), rows)
+    for block in range(4):
+        target = weight_all_ref.at[place, own_rows, pl.ds(block * width, width)]
+
+        def source(peer, block=block):
+            start = pl.multiple_of((block * ring + peer) * width, width)
+            return weight_hbm.at[:, pl.ds(start, width)]
+
+        keep = pltpu.make_async_copy(source(me), target, local_sems.at[4 + block])
+        keep.start()
+        keeps.append(keep)
+        for k in range(1, ring):
+            peer = lax.rem(me + k, ring)
+            spot = block * (ring - 1) + k - 1
+            copy = send_to(peer, source(peer), target, send_sems.at[spot], recv_sems.at[spot])
+            copy.start()
+            early.append(copy)
+    load.wait()
+    own = units // depth
+    half = pair_ref.shape[1] // 2
+    for s in range(ring):
+        pieces = []
+        for g in range(2):
+            for z in range(depth):
+                start = g * half + (z * ring + s) * own
+                pieces.append(pair_ref[:, start : start + own])
+        cut_ref[s] = jnp.concatenate(pieces, 1)
     for copy in early:
         copy.wait_recv()
-    keep_early.wait()
-    chain = chain_phases(early_all_ref, up_send, up_recv, down_send, down_recv)
-    first = gather_phases(first_ref, first_all_ref, send_sems, recv_sems, local_sems.at[2], ring)
-    next(chain)
+    for keep in keeps:
+        keep.wait()
+    base = 4 * (ring - 1)
+    hops = chain_hops(weight_all_ref, *chain_sems)
+    first = gather_phases(first_ref, first_all_ref, send_sems, recv_sems, local_sems.at[1], base)
+    hop_start(hops[0])
     next(first)
-    later = exchange_copies(later_ref, later_all_ref.at[me], send_sems, recv_sems, ring + 9)
-    next(chain)
+    pair_keep = pltpu.make_async_copy(cut_ref.at[me], pair_all_ref.at[me], local_sems.at[2])
+    pair_keep.start()
+    later = exchange_copies(cut_ref, pair_all_ref.at[me], send_sems, recv_sems, base + 9)
     next(first)
-    next(chain)
+    hop_arrive(hops[0])
+    hop_start(hops[1])
     next(first)
     next(first)
+    lanes_load.wait()
+    deep = weight_all_ref.shape[1]
+
+    def spread_slot(slot, fresh=False):
+        def run():
+            at = pl.ds(pl.multiple_of(slot * deep, deep), deep)
+
+            @pl.loop(0, ring)
+            def _(r):
+                term = low_dot(first_all_ref[r, :, at], weight_all_ref[slot], NN)
+                total_ref[r] = term if fresh else total_ref[r] + term
+
+        return run
+
+    @pl.loop(0, ring)
+    def _(r):
+        logit_ref[r] = low_dot(first_all_ref[r], lanes_ref[...], NN)
+
+    spread_slot(place, True)()
+    for _, _, arrives, slot in hops[0]:
+        pl.when(arrives)(spread_slot(slot))
+    saves = [pltpu.make_async_copy(first_all_ref, first_all_hbm, local_sems.at[0])]
+    saves[0].start()
+    for t in range(1, depth - 1):
+        hop_arrive(hops[t])
+        if t + 1 < depth - 1:
+            hop_start(hops[t + 1])
+        else:
+            saves.append(pltpu.make_async_copy(weight_all_ref, weight_all_hbm, local_sems.at[1]))
+            saves[1].start()
+        for _, _, arrives, slot in hops[t]:
+            pl.when(arrives)(spread_slot(slot))
+
+    @pl.loop(0, ring)
+    def _(r):
+        mixed_ref[r] = total_ref[r, :, : 3 * width].astype(BF16)
+        gate_ref[r] = total_ref[r, :, 3 * width :]
+
     for copy in later:
         copy.wait_recv()
-    next(chain)
+    hop_finish(hops)
     for copy in early + later:
         copy.wait_send()
-    keep_later.wait()
-
-
-def plane_open(first, early, later, collective_id):
+    pair_keep.wait()
+    for save in saves:
+        save.wait()
+
+
+def plane_open(first, weight, pair, lanes, collective_id):
     ring, depth = lax.axis_size("seq"), lax.axis_size("dp")
     rows, columns = first.shape
-    total = 2 * ring + 9
+    weight_rows = weight.shape[0]
+    width = weight.shape[1] // (4 * ring)
+    total = 5 * (ring - 1) + 9
+    cut = jax.ShapeDtypeStruct((ring, weight_rows, pair.shape[1] // ring), pair.dtype)
+    first_shape, weight_shape = (ring, rows, columns), (depth, ring * weight_rows, 4 * width)
+    vmem, anywhere = pl.BlockSpec(memory_space=pltpu.VMEM), pl.BlockSpec(memory_space=pl.ANY)
     return pl.pallas_call(
         plane_open_kernel,
         out_shape=[
-            jax.ShapeDtypeStruct((ring, rows, columns), first.dtype),
-            jax.ShapeDtypeStruct((depth, ring * early.shape[1], early.shape[2]), early.dtype),
-            jax.ShapeDtypeStruct(later.shape, later.dtype),
+            jax.ShapeDtypeStruct(first_shape, BF16),
+            jax.ShapeDtypeStruct(weight_shape, BF16),
+            cut,
+            jax.ShapeDtypeStruct((ring, rows, 3 * width), BF16),
+            jax.ShapeDtypeStruct((ring, rows, width), F32),
+            jax.ShapeDtypeStruct((ring, rows, lanes.shape[1]), F32),
         ],
-        in_specs=[pl.BlockSpec(memory_space=pl.ANY)] * 3,
-        out_specs=[pl.BlockSpec(memory_space=pl.ANY)] * 3,
+        in_specs=[anywhere] * 4,
+        out_specs=[anywhere] * 3 + [vmem] * 3,
         scratch_shapes=[
+            pltpu.VMEM(first_shape, BF16),
+            pltpu.VMEM(weight_shape, BF16),
+            pltpu.VMEM(pair.shape, BF16),
+            pltpu.VMEM(cut.shape, BF16),
+            pltpu.VMEM(lanes.shape, BF16),
+            pltpu.VMEM((ring, rows, 4 * width), F32),
             pltpu.SemaphoreType.DMA((total,)),
             pltpu.SemaphoreType.DMA((total,)),
-            pltpu.SemaphoreType.DMA((3,)),
+            pltpu.SemaphoreType.DMA((8,)),
         ]
         + [pltpu.SemaphoreType.DMA((depth - 1,))] * 4,
-        compiler_params=pltpu.CompilerParams(collective_id=collective_id, has_side_effects=True),
-        cost_estimate=lasting(90),
+        compiler_params=pltpu.CompilerParams(
+            collective_id=collective_id, has_side_effects=True, vmem_limit_bytes=VMEM_LIMIT
+        ),
+        cost_estimate=lasting(150),
         name="plane_open",
-    )(first, early, later)
+    )(first, weight, pair, lanes)
 
 
 def gather_in_steps(own_ref, all_ref, send_sems, recv_sems, local_sem):
@@ -1172,19 +1362,14 @@
 
 
 def small_sum_kernel(
-    own_ref, cut_ref, all_ref, swapped_ref, stage_ref, total_ref, send_sems, recv_sems, local_sem
+    own_ref, cut_ref, all_ref, joined_ref, swapped_ref, stage_ref, total_ref, send_sems, recv_sems, local_sem
 ):
     depth, ring = stage_ref.shape[0], all_ref.shape[0]
     place, me = lax.axis_index("dp"), lax.axis_index("seq")
-    barrier = pltpu.get_barrier_semaphore()
     mesh_ids = pl.DeviceIdType.MESH
     columns = [lax.rem(place + k, depth) for k in range(1, depth)]
     plane = [lax.rem(me + k, ring) for k in range(1, ring)]
-    for peer in columns:
-        pl.semaphore_signal(barrier, inc=1, device_id={"dp": peer}, device_id_type=mesh_ids)
-    for peer in plane:
-        pl.semaphore_signal(barrier, inc=1, device_id={"seq": peer}, device_id_type=mesh_ids)
-    pl.semaphore_wait(barrier, depth + ring - 2)
+    greet_all(ring, depth)
     keep = pltpu.make_async_copy(cut_ref.at[me], swapped_ref.at[me], local_sem)
     keep.start()
     first = []
@@ -1224,9 +1409,16 @@
     all_ref[me] = total
     for copy in second + swaps:
         copy.wait_recv()
+    keep.wait()
+    width = cut_ref.shape[2] // 4
+    for block in range(4):
+        for s in range(ring):
+            start = (block * ring + s) * width
+            joined_ref[:, start : start + width] = swapped_ref[
+                s, :, block * width : (block + 1) * width
+            ].astype(F32)
     for copy in first + second + swaps:
         copy.wait_send()
-    keep.wait()
 
 
 def small_sum(own, cut, collective_id):
@@ -1237,11 +1429,12 @@
         small_sum_kernel,
         out_shape=[
             jax.ShapeDtypeStruct((ring,) + own.shape, F32),
-            jax.ShapeDtypeStruct(cut.shape, cut.dtype),
+            jax.ShapeDtypeStruct((cut.shape[1], ring * cut.shape[2]), F32),
         ],
         in_specs=[vmem, anywhere],
-        out_specs=[vmem, anywhere],
+        out_specs=[vmem, vmem],
         scratch_shapes=[
+            pltpu.VMEM(cut.shape, cut.dtype),
             pltpu.VMEM((depth,) + own.shape, F32),
             pltpu.VMEM(own.shape, F32),
             pltpu.SemaphoreType.DMA((count,)),
@@ -1271,7 +1464,7 @@
     cut_refs = take(swaps)
     (sum_ref,) = take(1)
     terms = take(count if fill else 0)
-    swapped_refs = take(swaps)
+    spread_refs, swapped_refs = take(swaps), take(swaps)
     lefts, rights, fill_refs = take(count), take(count), take(int(fill))
     out_ref, own_ref, near_ref, far_in_ref, side_in_ref = take(5)
     send_sems, recv_sems, load_sems = refs
@@ -1290,19 +1483,16 @@
     rows, columns = sum_ref.shape
     half = rows // 2
     upper, lower = pl.ds(0, half), pl.ds(half, half)
-    swapped, keeps = [], []
+    swapped = []
     if swaps:
-        ring = cut_refs[0].shape[0]
-        greet_plane(ring)
-        for k in range(swaps):
-            keep = pltpu.make_async_copy(
-                cut_refs[k].at[me], swapped_refs[k].at[me], load_sems.at[2 * count + k]
-            )
-            keep.start()
-            keeps.append(keep)
-            swapped += exchange_copies(
-                cut_refs[k], swapped_refs[k].at[me], send_sems, recv_sems, 10 + k * (ring - 1)
-            )
+        greet_plane(lefts[0].shape[0])
+        keep = pltpu.make_async_copy(
+            cut_refs[0].at[me], swapped_refs[0].at[me], load_sems.at[2 * count]
+        )
+        keep.start()
+        swapped = exchange_copies(
+            cut_refs[0], swapped_refs[0].at[me], send_sems, recv_sems, 10
+        )
     else:
         greet((sibling, across, along))
     for load in loads:
@@ -1365,6 +1555,11 @@
     copies[1].wait_recv()
     fold(own_ref.at[1], far_in_ref, half, half)
     copies.append(send(9, across, own_ref.at[1, lower], side_in_ref.at[0, lower]))
+    if swaps:
+        for copy in swapped:
+            copy.wait_recv()
+        keep.wait()
+        spread_units(swapped_refs[0], spread_refs[0], lax.axis_size("dp"))
     if fill:
         fill_load.wait()
         tall = 256
@@ -1394,21 +1589,18 @@
         copy.wait_recv()
     finish(0, 0)
     finish(1, half)
-    for copy in swapped:
-        copy.wait_recv()
     for copy in nears + copies + swapped:
         copy.wait_send()
-    for keep in keeps:
-        keep.wait()
-
-
-def plane_scatter_dot(lefts, rights, dims, collective_id, fill=None, cuts=()):
+
+
+def plane_scatter_dot(lefts, rights, dims, collective_id, fill=None, cut=None):
     count = len(lefts)
     ring, rows, _ = lefts[0].shape
     columns = rights[0].shape[1 - dims[1][0]]
     filled = fill is not None
     fills = [fill] if filled else []
     vmem, anywhere = pl.BlockSpec(memory_space=pltpu.VMEM), pl.BlockSpec(memory_space=pl.ANY)
+    cuts = [] if cut is None else [cut]
     total = 10 + len(cuts) * (ring - 1)
     term_shapes = [
         jax.ShapeDtypeStruct((fill.shape[1], left.shape[2]), BF16) for left in lefts if filled
@@ -1417,10 +1609,11 @@
         functools.partial(plane_scatter_dot_kernel, count, dims, filled, len(cuts)),
         out_shape=[jax.ShapeDtypeStruct((rows, columns), F32)]
         + term_shapes
-        + [jax.ShapeDtypeStruct(cut.shape, cut.dtype) for cut in cuts],
+        + [jax.ShapeDtypeStruct((cut.shape[1], ring * cut.shape[2]), F32) for cut in cuts],
         in_specs=[anywhere] * (2 * count + len(fills) + len(cuts)),
-        out_specs=[vmem] * (1 + len(term_shapes)) + [anywhere] * len(cuts),
-        scratch_shapes=[pltpu.VMEM(left.shape, BF16) for left in lefts]
+        out_specs=[vmem] * (1 + len(term_shapes) + len(cuts)),
+        scratch_shapes=[pltpu.VMEM(cut.shape, BF16) for cut in cuts]
+        + [pltpu.VMEM(left.shape, BF16) for left in lefts]
         + [pltpu.VMEM(right.shape, BF16) for right in rights]
         + [pltpu.VMEM(value.shape, BF16) for value in fills]
         + [
@@ -1488,24 +1681,20 @@
 
 def gather_feed_kernel(
     own_hbm,
-    gate_hbm,
-    up_hbm,
+    pair_hbm,
     down_hbm,
     error_hbm,
     all_hbm,
     activated_hbm,
-    gate_err_hbm,
-    up_err_hbm,
+    pair_err_hbm,
     down_term_ref,
     own_ref,
-    gate_ref,
-    up_ref,
+    pair_ref,
     down_ref,
     error_ref,
     all_ref,
     activated_out,
-    gate_out,
-    up_out,
+    pair_out,
     total_ref,
     send_sems,
     recv_sems,
@@ -1515,8 +1704,7 @@
     loads = []
     for source, target in (
         (own_hbm, own_ref),
-        (gate_hbm, gate_ref),
-        (up_hbm, up_ref),
+        (pair_hbm, pair_ref),
         (down_hbm, down_ref),
         (error_hbm, error_ref),
     ):
@@ -1527,9 +1715,11 @@
     loads[0].wait()
     waiting = loads[1:]
     saves = []
-    tall = 128
+    tall = 256
     wide = 512
     rows, columns = own_ref.shape
+    units = down_ref.shape[0]
+
 
     def use(slab):
         first = bool(waiting)
@@ -1544,23 +1734,20 @@
         def _(i):
             at = pl.ds(pl.multiple_of(i * tall, tall), tall)
             values = all_ref[slab, at, :]
-            gate = low_dot(values, gate_ref[...], NN)
-            up = low_dot(values, up_ref[...], NN)
+            pair = low_dot(values, pair_ref[...], NN)
+            gate, up = pair[:, :units], pair[:, units:]
             grad = low_dot(error_ref[slab, at, :], down_ref[...], NT)
             opening = sigmoid(gate)
             gate_open = gate * opening
             activated_out[turn, at, :] = (gate_open * up).astype(BF16)
-            gate_out[turn, at, :] = (
-                grad * up * (opening * (1.0 + gate * (1.0 - opening)))
-            ).astype(BF16)
-            up_out[turn, at, :] = (grad * gate_open).astype(BF16)
+            gate_err = grad * up * (opening * (1.0 + gate * (1.0 - opening)))
+            pair_out[turn, at, :] = jnp.concatenate([gate_err, grad * gate_open], 1).astype(BF16)
 
         batch = []
         for k, (source, target) in enumerate(
             (
                 (activated_out.at[turn], activated_hbm.at[slab]),
-                (gate_out.at[turn], gate_err_hbm.at[slab]),
-                (up_out.at[turn], up_err_hbm.at[slab]),
+                (pair_out.at[turn], pair_err_hbm.at[slab]),
                 (all_ref.at[slab], all_hbm.at[slab]),
             )
         ):
@@ -1585,45 +1772,41 @@
             save.wait()
 
 
-def gather_feed(own, gate_own, up_own, down_own, error_all, collective_id):
+def gather_feed(own, pair_own, down_own, error_all, collective_id):
     ring = lax.axis_size("seq")
     rows, columns = own.shape
-    units = gate_own.shape[1]
+    units = down_own.shape[0]
     anywhere = pl.BlockSpec(memory_space=pl.ANY)
-    parted = jax.ShapeDtypeStruct((ring, rows, units), BF16)
     return pl.pallas_call(
         gather_feed_kernel,
         out_shape=[
             jax.ShapeDtypeStruct((ring, rows, columns), BF16),
-            parted,
-            parted,
-            parted,
+            jax.ShapeDtypeStruct((ring, rows, units), BF16),
+            jax.ShapeDtypeStruct((ring, rows, 2 * units), BF16),
             jax.ShapeDtypeStruct(down_own.shape, BF16),
         ],
-        in_specs=[anywhere] * 5,
-        out_specs=[anywhere] * 4 + [pl.BlockSpec(memory_space=pltpu.VMEM)],
+        in_specs=[anywhere] * 4,
+        out_specs=[anywhere] * 3 + [pl.BlockSpec(memory_space=pltpu.VMEM)],
         scratch_shapes=[
             pltpu.VMEM((rows, columns), BF16),
-            pltpu.VMEM(gate_own.shape, BF16),
-            pltpu.VMEM(up_own.shape, BF16),
+            pltpu.VMEM(pair_own.shape, BF16),
             pltpu.VMEM(down_own.shape, BF16),
             pltpu.VMEM((ring, rows, columns), BF16),
             pltpu.VMEM((ring, rows, columns), BF16),
             pltpu.VMEM((2, rows, units), BF16),
-            pltpu.VMEM((2, rows, units), BF16),
-            pltpu.VMEM((2, rows, units), BF16),
+            pltpu.VMEM((2, rows, 2 * units), BF16),
             pltpu.VMEM(down_own.shape, F32),
             pltpu.SemaphoreType.DMA((9,)),
             pltpu.SemaphoreType.DMA((9,)),
-            pltpu.SemaphoreType.DMA((5,)),
-            pltpu.SemaphoreType.DMA((2, 4)),
+            pltpu.SemaphoreType.DMA((4,)),
+            pltpu.SemaphoreType.DMA((2, 3)),
         ],
         compiler_params=pltpu.CompilerParams(
             collective_id=collective_id, has_side_effects=True, vmem_limit_bytes=VMEM_LIMIT
         ),
         cost_estimate=lasting(60),
         name="gather_feed",
-    )(own, gate_own, up_own, down_own, error_all)
+    )(own, pair_own, down_own, error_all)
 
 
 def gather_branch_kernel(
@@ -1782,28 +1965,11 @@
     valid_rows = (positions < lengths[:, :, None]).astype(F32).reshape(row_count, 1)
     normed_low = rms_norm(tokens, first_gain).astype(BF16)
 
-    in_cut = jnp.transpose(input_weight.reshape(weight_rows, 4, ring, width), (2, 0, 1, 3))
-    gate_up_cut = jnp.transpose(
-        gate_up_weight.reshape(weight_rows, 2, depth, ring, own_units), (3, 1, 0, 2, 4)
-    ).reshape(ring, 2, weight_rows, units)
     upstream = valid_rows * cotangent.reshape(row_count, model_width).astype(F32)
     out_err = upstream.astype(BF16)
     turns = [(depth * s + z, ring * z + s) for s in range(ring) for z in range(depth)]
     down_own = gather_rows(down_weight, "dp")
-    out_cut = lax.ppermute(output_weight, ("dp", "seq"), turns)
-    normed_all, in_own, gate_up_cut = plane_open(
-        normed_low,
-        in_cut.reshape(ring, weight_rows, 4 * width),
-        gate_up_cut.reshape(ring, 2 * weight_rows, units),
-        1,
-    )
-    gate_up_cut = gate_up_cut.reshape(ring, 2, weight_rows, units)
-    normed_all = normed_all.reshape(all_rows, model_width)
-    in_own = in_own.reshape(model_width, 4 * width)
-    in_own, out_cut, down_own = lax.optimization_barrier((in_own, out_cut, down_own))
-    out_own = gather_rows(out_cut, "dp")
-    gate_own = gather_rows(gate_up_cut[:, 0].reshape(ring * weight_rows, units), "dp")
-    up_own = gather_rows(gate_up_cut[:, 1].reshape(ring * weight_rows, units), "dp")
+    out_own = gather_rows(lax.ppermute(output_weight, ("dp", "seq"), turns), "dp")
 
     def own_lanes(pair):
         rows = pair.shape[0]
@@ -1824,28 +1990,28 @@
     def chunks(value):
         return value.reshape(ring, seqs, span, value.shape[-1])
 
-    mixed = chunks(low_dot(normed_all, in_own[:, : 3 * width], NN).astype(BF16))
-    gate_raw = chunks(low_dot(normed_all, in_own[:, 3 * width :], NN))
-    logits = chunks(low_dot(normed_all, decay_own, NN))
+    normed_all, in_own, pair_cut, mixed, gate_raw, logits = plane_open(
+        normed_low, input_weight, gate_up_weight, decay_own, 1
+    )
+    normed_all = normed_all.reshape(all_rows, model_width)
+    in_own = in_own.reshape(model_width, 4 * width)
+    pair_own = gather_rows(pair_cut.reshape(ring * weight_rows, 2 * units), "dp")
+    mixed, out_own, down_own = lax.optimization_barrier((mixed, out_own, down_own))
+    mixed, gate_raw, logits = chunks(mixed), chunks(gate_raw), chunks(logits)
     gated, memory, inverse, fresh, mixer_out, out_err_all = run_forward(
         mixed, gate_raw, logits, taps, params, gain, heads, out_err, 5
     )
     gated = gated.reshape(ring, row_count, width)
     hidden = tokens + plane_scatter_dot([gated], [out_own], NN, 2)[0]
     second_low = rms_norm(hidden, second_gain).astype(BF16)
-    second_all, activated, gate_err, up_err, down_term = gather_feed(
-        second_low, gate_own, up_own, down_own, out_err_all, 3
+    second_all, activated, pair_err, down_term = gather_feed(
+        second_low, pair_own, down_own, out_err_all, 3
     )
     down_share = scatter_rows(down_term, "dp").astype(F32)
-    second_grad, gate_term, up_term = plane_scatter_dot(
-        [gate_err, up_err],
-        [gate_own, up_own],
-        NT,
-        4,
-        second_all.reshape(all_rows, model_width),
-    )
-    gate_share = scatter_rows(gate_term, "dp")
-    up_share = scatter_rows(up_term, "dp")
+    second_grad, pair_term = plane_scatter_dot(
+        [pair_err], [pair_own], NT, 4, second_all.reshape(all_rows, model_width)
+    )
+    pair_share = scatter_rows(pair_term, "dp")
     hidden_part, second_gain_grad = rms_back(hidden, second_gain, second_grad)
     hidden_grad = upstream + hidden_part
     branch_err = hidden_grad.astype(BF16)
@@ -1869,13 +2035,13 @@
     )
     result = valid_rows * (hidden + final_part)
     input_term = low_dot(normed_all, in_err.reshape(all_rows, 4 * width), TN).astype(BF16)
-    input_term, in_err, logit_grad, down_share, gate_share, up_share = lax.optimization_barrier(
-        (input_term, in_err, logit_grad, down_share, gate_share, up_share)
+    input_term, in_err, logit_grad, down_share, pair_share = lax.optimization_barrier(
+        (input_term, in_err, logit_grad, down_share, pair_share)
     )
     input_cut = scatter_rows(input_term, "dp")
     lanes = logit_grad.shape[-1]
     decay_twice = decay_own + jnp.roll(decay_own, lanes // 2, 1)
-    normed_grad, gate_share, up_share = plane_scatter_dot(
+    normed_grad, gate_up_share = plane_scatter_dot(
         [
             in_err.reshape(ring, row_count, 4 * width),
             logit_grad.reshape(ring, row_count, lanes),
@@ -1883,10 +2049,7 @@
         [in_own, decay_twice],
         NT,
         6,
-        cuts=[
-            gate_share.reshape(ring, weight_rows, units),
-            up_share.reshape(ring, weight_rows, units),
-        ],
+        cut=pair_share.reshape(ring, weight_rows, 2 * units),
     )
     output_term, input_cut, normed_grad = lax.optimization_barrier(
         (output_term, input_cut, normed_grad)
@@ -1894,11 +2057,6 @@
     output_share = lax.ppermute(
         scatter_rows(output_term, "dp"), ("dp", "seq"), [(b, a) for a, b in turns]
     ).astype(F32)
-    gate_up_share = jnp.stack([gate_share, up_share], 1)
-    gate_up_share = jnp.transpose(
-        gate_up_share.reshape(ring, 2, weight_rows, depth, own_units), (2, 1, 3, 0, 4)
-    )
-    gate_up_share = gate_up_share.reshape(weight_rows, -1).astype(F32)
     token_part, first_gain_grad = rms_back(tokens, first_gain, normed_grad)
     inputs_grad = hidden_grad + token_part
     decay_term = low_dot(normed_all, logit_grad.reshape(all_rows, lanes), TN)
@@ -1915,8 +2073,6 @@
     packed = jnp.concatenate([piece.reshape(-1) for piece in pieces])
     packed = jnp.pad(packed, (0, -packed.size % 1024)).reshape(-1, 128)
     summed, input_share = small_sum(packed, input_cut.reshape(ring, weight_rows, 4 * width), 7)
-    input_share = jnp.transpose(input_share.reshape(ring, weight_rows, 4, width), (1, 2, 0, 3))
-    input_share = input_share.reshape(weight_rows, -1).astype(F32)
     summed = summed.reshape(ring, -1)
     parted = []
     start = 0

time: 710 us -> 657 us (0.925)
  local copies, waits for them, and re-layouts: 49.1 us -> 17 us
  matrix products: 41.7 us -> 19.2 us
  waiting for transfers between devices: 26.7 us -> 36.8 us
    pallas_call x1, Pallas kernels: 116 us -> 154 us  [plane_open(): pl.pallas_call(plane_open_kernel, out_shape=[jax.ShapeDtypeStruct(first_s...]
    pallas_call x1, Pallas kernels: 79.5 us -> 50.6 us  [run_forward(): pl.pallas_call(mixer_forward, grid=(steps,), in_specs=[rows(3 * width), r...]
    dot_general x5 -> x2, matrix products: 41.7 us -> 19.2 us  [low_dot(): lax.dot_general(left, right, (dims, ((), ())), preferred_element_type=F32)]
    convert_element_type x4 -> x0, local copies, waits for them, and re-layouts: 12.4 us -> none  [the longest x2 10.2 us: split_heads_device(): gate_up_share = gate_up_share.reshape(weight_rows, -1).astype(F32)]
    reshape x4 -> x0, local copies, waits for them, and re-layouts: 9.64 us -> none  [the longest x2 7.68 us: split_heads_device(): gate_up_weight.reshape(weight_rows, 2, depth, ring, own_units)]
    reduce_scatter x5 -> x4, waiting for transfers between devices: 17.7 us -> 14.1 us  [scatter_rows(): return lax.psum_scatter(value, axis, scatter_dimension=0, tiled=True)]
  transfers between devices with their start and end apart: 11 -> 9, of which waited for: 4 -> 4; matrix products, arithmetic and copies ran while one was open for 17% -> 8% of each run, Pallas kernels for 68% -> 73%
where the time goes in v3:
time: 657 us; the launch traced here: 652 us
  Pallas kernels  531 us (81%)
  waiting for transfers between devices  36.8 us (6%)
  other arithmetic  25.4 us (4%)
  matrix products  19.2 us (3%)
  local copies, waits for them, and re-layouts  17 us (3%)
  between operations  14.9 us (2%)
  starting transfers between devices  8.12 us (1%)
    pallas_call x1, Pallas kernels, plane_open(): pl.pallas_call(plane_open_kernel, out_shape=[jax.ShapeDtypeStruct(first_s...  154 us
    pallas_call x3, Pallas kernels, plane_scatter_dot(): pl.pallas_call(functools.partial(plane_scatter_dot_kernel, count, dims, f...  151 us
    pallas_call x1, Pallas kernels, gather_feed(): pl.pallas_call(gather_feed_kernel, out_shape=[jax.ShapeDtypeStruct((ring,...  53.2 us
    pallas_call x1, Pallas kernels, run_backward(): pl.pallas_call(mixer_backward, grid=(steps,), in_specs=[rows(3 * width),...  51 us
    pallas_call x1, Pallas kernels, run_forward(): pl.pallas_call(mixer_forward, grid=(steps,), in_specs=[rows(3 * width), r...  50.6 us
    pallas_call x1, Pallas kernels, gather_branch(): pl.pallas_call(gather_branch_kernel, out_shape=[jax.ShapeDtypeStruct((rin...  45 us
    pallas_call x1, Pallas kernels, small_sum(): pl.pallas_call(small_sum_kernel, out_shape=[jax.ShapeDtypeStruct((ring,)...  25.2 us
    dot_general x2, matrix products, low_dot(): lax.dot_general(left, right, (dims, ((), ())), preferred_element_type=F32)  19.2 us
  transfers between devices with their start and end apart: 9, of which 4 were waited for; matrix products, arithmetic and copies ran while one was open for 8% of the time, Pallas kernels for 73%

profile of v3, /device:TPU:1, one launch (start us, length us, event | category | flops | bytes accessed | tf_op | source)
XLA Modules:
  0.0 652.2 jit_solution(13899637590279462869)
XLA Ops:
  7.3 4.7 collective-permute-start
  12.0 4.2 collective-permute-done
  16.2 0.7 copy-done.10
  17.0 0.7 all-gather.6.cloned.1.call-update
  17.7 0.8 constant_dynamic-slice_fusion.3
  18.5 0.3 copy.43
  18.9 0.3 fusion.2
  19.2 0.1 pad_slice_fusion
  19.3 1.3 pad_add_fusion
  20.6 1.3 fusion.4.first_ref
  21.8 154.5 %plane_open.1 = (bf16[8,256,2048]{2,1,0:T(8,128)(2,1)}, bf16[4,512,1024]{2,1,0:T(8,128)(2,1)}, bf16[8,64,1408]{2,1,0:T(8,128)(2,1)}, bf16[8,256,768]{2,1,0:T(8,1...) custom-call(bf16[256,2048]{1,0:T(8,128)(2,1)} %fusion.4.first_ref, bf16[64,8192]{1,0:T(8,128)(2,1)} %weight_hbm.1, ...), custom_call_target="tpu_custom_call" | custom-call | bytes 525000000 | tf_op jit(solution)/shard_map/plane_open/pallas_call | solution.py:1183
  176.4 0.3 reduce-scatter.5.cloned.1.call-start
  176.7 0.1 constant_dynamic-slice_fusion
  176.7 0.6 pad.25.param_ref
  177.3 0.6 constant_dynamic-slice_fusion.1
  177.9 0.1 compare_convert_fusion
  178.0 1.2 fusion.1.own_ref
  179.3 50.6 %mixer_forward.1 = (bf16[8,2,128,256]{3,2,1,0:T(8,128)(2,1)}, f32[8,2,2,128,128]{4,3,2,1,0:T(8,128)}, f32[8,2,2,128,128]{4,3,2,1,0:T(8,128)}, f32[8,2,128,256]{3...) custom-call(bf16[8,2,128,768]{3,2,1,0:T(8,128)(2,1)} %bitcast.90, ...), custom_call_target="tpu_custom_call" | custom-call | bytes 192500000 | tf_op jit(solution)/shard_map/mixer_forward/pallas_call | solution.py:776
  229.8 44.1 %plane_scatter_dot.3 = f32[256,2048]{1,0:T(8,128)} custom-call(bf16[8,256,256]{2,1,0:T(8,128)(2,1)} %bitcast.96, bf16[256,2048]{1,0:T(8,128)(2,1)} %all-gather.4.cloned.1.call-done.refs_1_.weight_hbm), custom_call_target="tpu_custom_call" | custom-call | bytes 157500000 | tf_op jit(solution)/shard_map/plane_scatter_dot/pallas_call | solution.py:1608
  274.0 2.0 multiply_reduce_fusion.2
  276.0 1.2 multiply_convert_fusion.own_hbm
  277.2 5.8 all-gather.8.cloned.1.call-done.pair_hbm.refs_1_
  283.0 53.2 %gather_feed.1 = (bf16[8,256,2048]{2,1,0:T(8,128)(2,1)}, bf16[8,256,704]{2,1,0:T(8,128)(2,1)}, bf16[8,256,1408]{2,1,0:T(8,128)(2,1)}, bf16[704,2048]{1,0:T(8,128)(2,1)}) custom-call(bf16[256,2048]{1,0:T(8,128)(2,1)} %multiply_convert_fusion.own_hbm, bf16[2048,1408]{1,0:T(8,128)(2,1)} %all-gather.8.cloned.1.call-done.pair_hbm.refs_1_, ...), custom_call_target="tpu_custom_call" | custom-call | bytes 210000000 | tf_op jit(solution)/shard_map/gather_feed/pallas_call | solution.py:1780
  336.2 51.5 %plane_scatter_dot.4 = (f32[256,2048]{1,0:T(8,128)}, bf16[2048,1408]{1,0:T(8,128)(2,1)}) custom-call(bf16[8,256,1408]{2,1,0:T(8,128)(2,1)} %get-tuple-element.68.refs_0_, bf16[2048,1408]{1,0:T(8,128)(2,1)} %all-gather.8.cloned.1.call-done.pair_hbm.refs_1_, bf16[2048,2048]{1,0:T(8,128)(2,1)} %bitcast.93), custom_call_target="tpu_custom_call" | custom-call | bytes 157500000 | tf_op jit(solution)/shard_map/plane_scatter_dot/pallas_call | solution.py:1608
  387.7 0.3 reduce-scatter.9.cloned.1.call-start
  388.0 2.3 multiply_reduce_fusion
  390.3 0.2 copy-done.6
  390.5 2.4 fusion.13
  392.9 45.0 %gather_branch.1 = (bf16[8,256,256]{2,1,0:T(8,128)(2,1)}, bf16[256,2048]{1,0:T(8,128)(2,1)}, bf16[8,256,2048]{2,1,0:T(8,128)(2,1)}) custom-call(bf16[256,2048]{1,0:T(8,128)(2,1)} %get-tuple-element.142.own_hbm, bf16[8,256,256]{2,1,0:T(8,128)(2,1)} %bitcast.97, bf16[256,2048]{1,0:T(8,128)(2,1)} %all-gather.4.cloned.1.call-done.refs_1_.weight_hbm, ...), custom_call_target="tpu_custom_call" | custom-call | bytes 157500000 | tf_op jit(solution)/shard_map/gather_branch/pallas_call | solution.py:1881
  437.9 51.0 %mixer_backward.1 = (bf16[8,2,128,1024]{3,2,1,0:T(8,128)(2,1)}, bf16[8,2,128,128]{3,2,1,0:T(8,128)(2,1)}, f32[8,768]{1,0:T(8,128)}, f32[8,128]{1,0:T(8,128)}, f32[8,128]{1,0:T(8,128)}, /*index=5*/f32[256,2048]{1,0:T(8,128)}) custom-call(bf16[8,2,128,768]{3,2,1,0:T(8,128)(2,1)} %bitcast.91, bf16[8,2,128,768]{3,2,1,0:T(8,128)(2,1)} %bitcast.92, ...), custom_call_target="tpu_custom_call" | custom-call | bytes 192500000 | tf_op jit(solution)/shard_map/mixer_backward/pallas_call | solution.py:836
  489.0 14.3 %convolution_convert_fusion = bf16[2048,1024]{1,0:T(8,128)(2,1)} fusion(bf16[2048,2048]{1,0:T(8,128)(2,1)} %bitcast.133, bf16[2048,1024]{1,0:T(8,128)(2,1)} %bitcast.99), kind=kOutput, calls=%fused_computation | convolution fusion | flops 8592031744 | bytes 16777216 | tf_op jit(solution)/shard_map/dot_general | solution.py:1922
  503.3 2.4 convert_element_type.68
  505.7 0.7 slice.54
  506.4 0.1 reshape.228
  506.5 0.7 slice_bitcast_fusion.1
  507.2 3.2 add_multiply_fusion
  510.4 55.8 %plane_scatter_dot.5 = (f32[256,2048]{1,0:T(8,128)}, f32[64,11264]{1,0:T(8,128)}) custom-call(bf16[8,256,1024]{2,1,0:T(8,128)(2,1)} %bitcast.100, bf16[8,256,128]{2,1,0:T(8,128)(2,1)} %bitcast.117, bf16[2048,1024]{1,0:T(8,128)(2,1)} %bitcast.98, bf16[2048,128]{1,0:T(8,128)(2,1)} %get-tuple-element.146.refs_3_, bf16[8,64,1408]{2,1,0:T(8,128)(2,1)} %bitcast.111), custom_call_target="tpu_custom_call" | custom-call | bytes 157500000 | tf_op jit(solution)/shard_map/plane_scatter_dot/pallas_call | solution.py:1608
  566.1 14.1 %reduce-scatter.9.cloned.1.call-done = bf16[512,1024]{1,0:T(8,128)(2,1)} async-done(((bf16[2048,1024]{1,0:T(8,128)(2,1)}), bf16[512,1024]{1,0:T(8,128)(2,1)}) %reduce-scatter.9.cloned.1.call-update) | async-done | bytes 1048592 | tf_op jit(solution)/shard_map/reduce_scatter | solution.py:894
  580.3 4.9 fusion.16
  585.2 0.6 fusion.9
  585.8 0.1 concatenate.12
  585.9 0.6 pad_bitcast_fusion.own_ref
  586.6 25.2 %small_sum.1 = (f32[8,128,128]{2,1,0:T(8,128)}, f32[64,8192]{1,0:T(8,128)}) custom-call(f32[128,128]{1,0:T(8,128)} %pad_bitcast_fusion.own_ref, bf16[8,64,1024]{2,1,0:T(8,128)(2,1)} %bitcast.112), custom_call_target="tpu_custom_call" | custom-call | bytes 70000000 | tf_op jit(solution)/shard_map/small_sum/pallas_call | solution.py:1428
  611.7 1.4 copy.56
  613.1 0.8 copy-done.9
  613.9 0.1 copy.50
  614.0 3.4 fusion.7
  617.4 2.7 collective-permute-start.1
  620.1 0.9 slice.69
  621.0 1.0 slice.68
  622.0 0.1 copy.47
  622.1 0.6 squeeze.11
  622.7 0.1 copy.46
  622.7 0.6 squeeze.10
  623.3 0.2 copy.57
  623.5 0.9 reshape.233
  624.4 0.7 copy.53
  625.1 1.3 slice_reduce_fusion.2
  626.4 1.7 slice_reduce_fusion
  628.1 11.9 %collective-permute-done.1 = bf16[64,2048]{1,0:T(8,128)(2,1)S(1)} collective-permute-done((bf16[64,2048]{1,0:T(8,128)(2,1)}, bf16[64,2048]{1,0:T(8,128)(2,1)S(1)}, u32[]{:S(2)}, u32[]{:S(2)}) %collective-permute-start.1) | collective-permute-done | bytes 262176 | tf_op jit(solution)/shard_map/ppermute | solution.py:2057
  640.0 0.8 convert_element_type.69
  640.8 1.3 copy.60
  642.1 1.2 copy-done.7
  643.4 1.6 copy.61
  (60 shorter events, 0.5 us)
Async XLA Ops:
  7.2 170.2 %copy-start = (f32[4,6144]{1,0:T(4,128)S(1)}, f32[4,6144]{1,0:T(4,128)}, u32[]{:S(2)}) copy-start(f32[4,6144]{1,0:T(4,128)} %param.19) | copy-start | bytes 294916
  7.2 11.7 %copy-start.2 = (bf16[2,1,128,2048]{3,2,1,0:T(8,128)(2,1)S(1)}, bf16[2,1,128,2048]{3,2,1,0:T(8,128)(2,1)}, u32[]{:S(2)}) copy-start(bf16[2,1,128,2048]{3,2,1,0:T(8,128)(2,1)} %param.14) | copy-start | bytes 3145732
  7.2 172.0 %all-gather.4.cloned.1.call-start = ((), (), s32[]{:S(2)}) async-start(), calls=%async_computation.4 | async-start | bytes 1310720 | tf_op jit(solution)/shard_map/all_gather | solution.py:890
  7.3 8.9 %collective-permute-start = (bf16[64,2048]{1,0:T(8,128)(2,1)}, bf16[64,2048]{1,0:T(8,128)(2,1)S(1)}, u32[]{:S(2)}, u32[]{:S(2)}) collective-permute-start(bf16[64,2048]{1,0:T(8,128)(2,1)} %param.23), channel_id=1, source_target_pairs={{0,0},{1,8},{2,16},{3,24},{4,1},{5,9},{6,17},{7,25},{8,2},{9,10},{... | collective-permute-start | bytes 786440 | tf_op jit(solution)/shard_map/ppermute | solution.py:1972
  16.2 0.7 copy-start.10
  16.9 162.3 %all-gather.6.cloned.1.call-start = ((), (), s32[]{:S(2)}) async-start(), calls=%async_computation.5 | async-start | bytes 3604480 | tf_op jit(solution)/shard_map/all_gather | solution.py:890
  17.7 265.3 %all-gather.8.cloned.1.call-start = ((), (), s32[]{:S(2)}) async-start(), calls=%async_computation.6 | async-start | bytes 7208960 | tf_op jit(solution)/shard_map/all_gather | solution.py:890
  18.9 1.7 copy-start.11
  21.8 154.8 %copy-start.14 = (f32[16]{0:T(128)S(1)}, f32[16]{0:T(128)}, u32[]{:S(2)}) copy-start(f32[16]{0:T(128)} %param.21) | copy-start | bytes 196
  21.8 154.8 %copy-start.15 = (f32[16]{0:T(128)S(1)}, f32[16]{0:T(128)}, u32[]{:S(2)}) copy-start(f32[16]{0:T(128)} %param.20) | copy-start | bytes 196
  21.8 156.1 %copy-start.16 = (s32[2,1]{0,1:T(1,128)S(1)}, s32[2,1]{0,1:T(1,128)}, u32[]{:S(2)}) copy-start(s32[2,1]{0,1:T(1,128)} %param.15) | copy-start | bytes 28
  21.8 156.2 %copy-start.5 = (bf16[2,1,128,2048]{3,2,1,0:T(8,128)(2,1)S(1)}, bf16[2,1,128,2048]{3,2,1,0:T(8,128)(2,1)}, u32[]{:S(2)}) copy-start(bf16[2,1,128,2048]{3,2,1,0:T(8,128)(2,1)} %param.27) | copy-start | bytes 3145732
  176.4 326.9 %reduce-scatter.5.cloned.1.call-start = ((), (), s32[]{:S(2)}) async-start(), calls=%async_computation.7 | async-start | bytes 3604480 | tf_op jit(solution)/shard_map/reduce_scatter | solution.py:894
  274.0 2.0 copy-start.12
  336.1 169.5 %reduce-scatter.7.cloned.1.call-start = ((), (), s32[]{:S(2)}) async-start(), calls=%async_computation.8 | async-start | bytes 7208960 | tf_op jit(solution)/shard_map/reduce_scatter | solution.py:894
  387.7 192.5 %reduce-scatter.9.cloned.1.call-start = ((), (), s32[]{:S(2)}) async-start(), calls=%async_computation.9 | async-start | bytes 5242880 | tf_op jit(solution)/shard_map/reduce_scatter | solution.py:894
  388.0 2.3 copy-start.4
  388.0 2.5 copy-start.6
  505.6 0.8 copy-start.13
  505.7 111.7 %reduce-scatter.11.cloned.1.call-start = ((), (), s32[]{:S(2)}) async-start(), calls=%async_computation.10 | async-start | bytes 1310720 | tf_op jit(solution)/shard_map/reduce_scatter | solution.py:894
  580.3 4.9 copy-start.3
  613.1 0.8 copy-start.9
  617.4 23.4 %copy-start.8 = (f32[64,8192]{1,0:T(8,128)S(1)}, f32[64,8192]{1,0:T(8,128)}, u32[]{:S(2)}) copy-start(f32[64,8192]{1,0:T(8,128)} %get-tuple-element.168) | copy-start | bytes 6291460
  617.4 22.6 %collective-permute-start.1 = (bf16[64,2048]{1,0:T(8,128)(2,1)}, bf16[64,2048]{1,0:T(8,128)(2,1)S(1)}, u32[]{:S(2)}, u32[]{:S(2)}) collective-permute-start(bf16[64,2048]{1,0:T(8,128)(2,1)} %reduce-scatter.11.cloned.1.call-done), channel_id=1, source_target_pairs={{0,0},{8,1},{16,2},{24,3},{1,4},{9,5},{17,6},{25,7},{2,8},{10,9},{... | collective-permute-start | bytes 786440 | tf_op jit(solution)/shard_map/ppermute | solution.py:2057
  640.8 2.6 copy-start.7
  640.8 4.2 copy-start.1
Sparse Core Ops, SparseCore 0:
  17.0 38.5 all-gather.3
  57.2 84.5 all-gather.5
  176.5 106.4 all-gather.7
  336.3 53.9 reduce-scatter.4
  392.4 102.2 reduce-scatter.6
  505.8 74.4 reduce-scatter.8
  582.7 31.6 reduce-scatter.10

commit v4 on v3

--- a/solution.py
+++ b/solution.py
@@ -425,21 +425,24 @@
     param_ref,
     gain_ref,
     own_ref,
+    rows_ref,
     gated_ref,
     memory_ref,
     inverse_ref,
     fresh_ref,
     out_ref,
     all_ref,
+    rows_out_ref,
     state_ref,
     halo_ref,
     send_sems,
     recv_sems,
-    local_sem,
+    local_sems,
 ):
     seqs, span, _ = mixed_ref.shape
     heads, head_size = memory_ref.shape[1], memory_ref.shape[2]
-    gather_in_steps(own_ref, all_ref, send_sems, recv_sems, local_sem)
+    gather_in_steps(own_ref, all_ref, send_sems, recv_sems, local_sems.at[0])
+    trade_in_steps(rows_ref, rows_out_ref, send_sems, recv_sems, local_sems, heads)
 
     @pl.when(pl.program_id(0) == 0)
     def _():
@@ -529,12 +532,14 @@
     out_ref,
     grad_ref,
     part_ref,
+    term_ref,
     error_ref,
     logit_grad_ref,
     taps_grad_ref,
     param_grad_ref,
     gain_grad_ref,
     sum_ref,
+    share_ref,
     state_ref,
     halo_ref,
     *scatter_refs,
@@ -542,7 +547,8 @@
     seqs, span, _ = mixed_ref.shape
     heads, head_size = memory_ref.shape[1], memory_ref.shape[2]
     step = pl.program_id(0)
-    scatter_in_steps(part_ref, sum_ref, *scatter_refs)
+    scatter_in_steps(part_ref, sum_ref, *scatter_refs[:7])
+    sums_in_steps(term_ref, share_ref, *scatter_refs[7:])
 
     @pl.when(step == 0)
     def _():
@@ -755,7 +761,7 @@
         ).astype(BF16)
 
 
-def run_forward(mixed, gate, logits, taps, params, gain, heads, own, collective_id):
+def run_forward(mixed, gate, logits, taps, params, gain, heads, own, out_rows, collective_id):
     steps, seqs, span, _ = mixed.shape
     anywhere = pl.BlockSpec(memory_space=pl.ANY)
     head_size = gain.shape[1]
@@ -784,8 +790,9 @@
             whole(params),
             whole(gain),
             anywhere,
+            anywhere,
         ],
-        out_specs=[rows(width), squares(), squares(), rows(width), rows(width), anywhere],
+        out_specs=[rows(width), squares(), squares(), rows(width), rows(width)] + [anywhere] * 2,
         out_shape=[
             jax.ShapeDtypeStruct((steps, seqs, span, width), BF16),
             square,
@@ -793,27 +800,30 @@
             flat,
             flat,
             jax.ShapeDtypeStruct((steps,) + own.shape, own.dtype),
+            jax.ShapeDtypeStruct(out_rows.shape, out_rows.dtype),
         ],
         scratch_shapes=[
             pltpu.VMEM((seqs, heads, head_size, head_size), F32),
             pltpu.VMEM((seqs, 8, 3 * width), F32),
-            pltpu.SemaphoreType.DMA((9,)),
-            pltpu.SemaphoreType.DMA((9,)),
-            pltpu.SemaphoreType.DMA,
+            pltpu.SemaphoreType.DMA((9 + heads,)),
+            pltpu.SemaphoreType.DMA((9 + heads,)),
+            pltpu.SemaphoreType.DMA((1 + heads,)),
         ],
         compiler_params=pltpu.CompilerParams(
             collective_id=collective_id, has_side_effects=True, vmem_limit_bytes=VMEM_LIMIT
         ),
         cost_estimate=lasting(55),
         name="mixer_forward",
-    )(mixed, gate, logits, taps, params, gain, own)
+    )(mixed, gate, logits, taps, params, gain, own, out_rows)
 
 
 def run_backward(
-    mixed, gate, logits, taps, params, gain, memory, inverse, fresh, out, grad, part, collective_id
+    mixed, gate, logits, taps, params, gain, memory, inverse, fresh, out, grad, part, term, collective_id
 ):
     steps, seqs, span, _ = mixed.shape
     _, part_rows, columns = part.shape
+    depth = lax.axis_size("dp")
+    term_rows = term.shape[0] // depth
     heads, head_size = memory.shape[2], memory.shape[3]
     width = heads * head_size
     edge = 16
@@ -850,6 +860,7 @@
             rows(width),
             rows(width),
             pl.BlockSpec(memory_space=pl.ANY),
+            pl.BlockSpec(memory_space=pl.ANY),
         ],
         out_specs=[
             rows(4 * width),
@@ -858,6 +869,7 @@
             whole((8, logits.shape[-1])),
             whole((8, head_size)),
             whole((part_rows, columns)),
+            whole((term_rows, columns)),
         ],
         out_shape=[
             jax.ShapeDtypeStruct((steps, seqs, span, 4 * width), BF16),
@@ -866,6 +878,7 @@
             jax.ShapeDtypeStruct((8, logits.shape[-1]), F32),
             jax.ShapeDtypeStruct((8, head_size), F32),
             jax.ShapeDtypeStruct((part_rows, columns), F32),
+            jax.ShapeDtypeStruct((term_rows, columns), BF16),
         ],
         scratch_shapes=[
             pltpu.VMEM((seqs, heads, head_size, head_size), F32),
@@ -877,13 +890,19 @@
             pltpu.SemaphoreType.DMA((10,)),
             pltpu.SemaphoreType.DMA((10,)),
             pltpu.SemaphoreType.DMA((4,)),
+            pltpu.VMEM((depth, term_rows, columns), BF16),
+            pltpu.VMEM((depth - 1, 2, term_rows, columns), BF16),
+            pltpu.SemaphoreType.DMA((2, depth - 1)),
+            pltpu.SemaphoreType.DMA((2, depth - 1)),
+            pltpu.SemaphoreType.DMA((depth // 2,)),
+            pltpu.SemaphoreType.DMA((2, depth // 2)),
         ],
         compiler_params=pltpu.CompilerParams(
             collective_id=collective_id, has_side_effects=True, vmem_limit_bytes=VMEM_LIMIT
         ),
         cost_estimate=lasting(55),
         name="mixer_backward",
-    )(mixed, mixed, gate, logits, taps, params, gain, memory, inverse, fresh, out, grad, part)
+    )(mixed, mixed, gate, logits, taps, params, gain, memory, inverse, fresh, out, grad, part, term)
 
 
 def gather_rows(value, axis):
@@ -1011,6 +1030,17 @@
             pl.when(leaves)(copy.wait_send)
 
 
+def greet_near(peers):
+    place, depth = lax.axis_index("dp"), lax.axis_size("dp")
+    barrier = pltpu.get_barrier_semaphore()
+    mesh_ids = pl.DeviceIdType.MESH
+    for peer in peers:
+        pl.semaphore_signal(barrier, inc=1, device_id={"seq": peer}, device_id_type=mesh_ids)
+    for peer in (lax.rem(place + 1, depth), lax.rem(place + depth - 1, depth)):
+        pl.semaphore_signal(barrier, inc=1, device_id={"dp": peer}, device_id_type=mesh_ids)
+    pl.semaphore_wait(barrier, len(peers) + 2)
+
+
 def greet_all(ring, depth):
     me, place = lax.axis_index("seq"), lax.axis_index("dp")
     barrier = pltpu.get_barrier_semaphore()
@@ -1047,7 +1077,12 @@
     return copies
 
 
+def rank_head(rank, j, heads):
+    return rank // 2 + lax.axis_size("seq") // 2 * (heads * (rank % 2) + j)
+
+
 def plane_open_kernel(
+    heads,
     first_ref,
     weight_hbm,
     pair_hbm,
@@ -1080,22 +1115,33 @@
     greet_all(ring, depth)
     keeps, early = [], []
     own_rows = pl.ds(pl.multiple_of(me * rows, rows), rows)
-    for block in range(4):
-        target = weight_all_ref.at[place, own_rows, pl.ds(block * width, width)]
-
-        def source(peer, block=block):
-            start = pl.multiple_of((block * ring + peer) * width, width)
-            return weight_hbm.at[:, pl.ds(start, width)]
-
-        keep = pltpu.make_async_copy(source(me), target, local_sems.at[4 + block])
+    size = width // heads
+    for part in range(4 * heads):
+        block, j = part // heads, part % heads
+        target = weight_all_ref.at[place, own_rows, pl.ds(part * size, size)]
+
+        def source(peer, block=block, j=j):
+            start = (block * ring * heads + rank_head(peer, j, heads)) * size
+            return weight_hbm.at[:, pl.ds(pl.multiple_of(start, size), size)]
+
+        keep = pltpu.make_async_copy(source(me), target, local_sems.at[4 + part])
         keep.start()
         keeps.append(keep)
         for k in range(1, ring):
             peer = lax.rem(me + k, ring)
-            spot = block * (ring - 1) + k - 1
+            spot = part * (ring - 1) + k - 1
             copy = send_to(peer, source(peer), target, send_sems.at[spot], recv_sems.at[spot])
             copy.start()
             early.append(copy)
+    for copy in early:
+        copy.wait_recv()
+    for keep in keeps:
+        keep.wait()
+    base = 4 * heads * (ring - 1)
+    hops = chain_hops(weight_all_ref, *chain_sems)
+    first = gather_phases(first_ref, first_all_ref, send_sems, recv_sems, local_sems.at[1], base)
+    hop_start(hops[0])
+    next(first)
     load.wait()
     own = units // depth
     half = pair_ref.shape[1] // 2
@@ -1106,21 +1152,15 @@
                 start = g * half + (z * ring + s) * own
                 pieces.append(pair_ref[:, start : start + own])
         cut_ref[s] = jnp.concatenate(pieces, 1)
-    for copy in early:
-        copy.wait_recv()
-    for keep in keeps:
-        keep.wait()
-    base = 4 * (ring - 1)
-    hops = chain_hops(weight_all_ref, *chain_sems)
-    first = gather_phases(first_ref, first_all_ref, send_sems, recv_sems, local_sems.at[1], base)
-    hop_start(hops[0])
-    next(first)
     pair_keep = pltpu.make_async_copy(cut_ref.at[me], pair_all_ref.at[me], local_sems.at[2])
     pair_keep.start()
     later = exchange_copies(cut_ref, pair_all_ref.at[me], send_sems, recv_sems, base + 9)
-    next(first)
     hop_arrive(hops[0])
     hop_start(hops[1])
+    next(first)
+    for t in range(1, depth - 2):
+        hop_arrive(hops[t])
+        hop_start(hops[t + 1])
     next(first)
     next(first)
     lanes_load.wait()
@@ -1141,20 +1181,17 @@
     def _(r):
         logit_ref[r] = low_dot(first_all_ref[r], lanes_ref[...], NN)
 
-    spread_slot(place, True)()
-    for _, _, arrives, slot in hops[0]:
-        pl.when(arrives)(spread_slot(slot))
     saves = [pltpu.make_async_copy(first_all_ref, first_all_hbm, local_sems.at[0])]
     saves[0].start()
-    for t in range(1, depth - 1):
-        hop_arrive(hops[t])
-        if t + 1 < depth - 1:
-            hop_start(hops[t + 1])
-        else:
-            saves.append(pltpu.make_async_copy(weight_all_ref, weight_all_hbm, local_sems.at[1]))
-            saves[1].start()
-        for _, _, arrives, slot in hops[t]:
+    spread_slot(place, True)()
+    for hop in hops[:-1]:
+        for _, _, arrives, slot in hop:
             pl.when(arrives)(spread_slot(slot))
+    hop_arrive(hops[-1])
+    saves.append(pltpu.make_async_copy(weight_all_ref, weight_all_hbm, local_sems.at[1]))
+    saves[1].start()
+    for _, _, arrives, slot in hops[-1]:
+        pl.when(arrives)(spread_slot(slot))
 
     @pl.loop(0, ring)
     def _(r):
@@ -1171,17 +1208,17 @@
         save.wait()
 
 
-def plane_open(first, weight, pair, lanes, collective_id):
+def plane_open(first, weight, pair, lanes, heads, collective_id):
     ring, depth = lax.axis_size("seq"), lax.axis_size("dp")
     rows, columns = first.shape
     weight_rows = weight.shape[0]
     width = weight.shape[1] // (4 * ring)
-    total = 5 * (ring - 1) + 9
+    total = (4 * heads + 1) * (ring - 1) + 9
     cut = jax.ShapeDtypeStruct((ring, weight_rows, pair.shape[1] // ring), pair.dtype)
     first_shape, weight_shape = (ring, rows, columns), (depth, ring * weight_rows, 4 * width)
     vmem, anywhere = pl.BlockSpec(memory_space=pltpu.VMEM), pl.BlockSpec(memory_space=pl.ANY)
     return pl.pallas_call(
-        plane_open_kernel,
+        functools.partial(plane_open_kernel, heads),
         out_shape=[
             jax.ShapeDtypeStruct(first_shape, BF16),
             jax.ShapeDtypeStruct(weight_shape, BF16),
@@ -1201,7 +1238,7 @@
             pltpu.VMEM((ring, rows, 4 * width), F32),
             pltpu.SemaphoreType.DMA((total,)),
             pltpu.SemaphoreType.DMA((total,)),
-            pltpu.SemaphoreType.DMA((8,)),
+            pltpu.SemaphoreType.DMA((4 + 4 * heads,)),
         ]
         + [pltpu.SemaphoreType.DMA((depth - 1,))] * 4,
         compiler_params=pltpu.CompilerParams(
@@ -1210,6 +1247,39 @@
         cost_estimate=lasting(150),
         name="plane_open",
     )(first, weight, pair, lanes)
+
+
+def trade_in_steps(rows_ref, rows_out_ref, send_sems, recv_sems, local_sems, heads):
+    me = lax.axis_index("seq")
+    core = lax.rem(me, 2)
+    sibling = me + 1 - 2 * core
+    rows = rows_out_ref.shape[0] // (2 * heads)
+
+    def rows_of(ref, spot):
+        return ref.at[pl.ds(pl.multiple_of(spot * rows, rows), rows)]
+
+    copies, keeps = [], []
+    for j in range(heads):
+        target = rows_of(rows_out_ref, 2 * j + core)
+        theirs = rows_of(rows_ref, heads * (1 - core) + j)
+        copies.append(send_to(sibling, theirs, target, send_sems.at[9 + j], recv_sems.at[9 + j]))
+        keeps.append(
+            pltpu.make_async_copy(rows_of(rows_ref, heads * core + j), target, local_sems.at[1 + j])
+        )
+    step, steps = pl.program_id(0), pl.num_programs(0)
+
+    @pl.when(step == 0)
+    def _():
+        for copy in copies + keeps:
+            copy.start()
+
+    @pl.when(step == steps - 1)
+    def _():
+        for copy in copies:
+            copy.wait_recv()
+            copy.wait_send()
+        for keep in keeps:
+            keep.wait()
 
 
 def gather_in_steps(own_ref, all_ref, send_sems, recv_sems, local_sem):
@@ -1316,7 +1386,7 @@
 
     @pl.when(step == 0)
     def _():
-        greet((sibling, across, along))
+        greet_near((sibling, across, along))
         for k in range(4):
             loads[k].start()
             copies[k].start()
@@ -1361,8 +1431,111 @@
             copy.wait_send()
 
 
+def sums_in_steps(
+    term_ref, share_ref, held_ref, land_ref, up_sems, down_sems, load_sems, trade_sems
+):
+    depth, rows, _ = held_ref.shape
+    place = lax.axis_index("dp")
+    above, below = lax.rem(place + 1, depth), lax.rem(place + depth - 1, depth)
+    last = depth - 1
+    mesh_ids = pl.DeviceIdType.MESH
+    me = lax.axis_index("seq")
+    core = lax.rem(me, 2)
+    heads = depth // 2
+    loads, trades = [], []
+    for j in range(heads):
+        target = held_ref.at[heads * core + j]
+
+        def rows_of(spot):
+            return term_ref.at[pl.ds(pl.multiple_of(spot * rows, rows), rows)]
+
+        loads.append(pltpu.make_async_copy(rows_of(2 * j + core), target, load_sems.at[j]))
+        trades.append(
+            send_to(
+                me + 1 - 2 * core,
+                rows_of(2 * j + 1 - core),
+                target,
+                trade_sems.at[0, j],
+                trade_sems.at[1, j],
+            )
+        )
+    hops = []
+    for r in range(last):
+        hop = []
+        for k, (peer, sems, block, leaves, mine, arrives) in enumerate(
+            (
+                (above, up_sems, place + last - r, place < r + 1, place + last - 1 - r, place > 0),
+                (below, down_sems, place - last + r, place > last - 1 - r, place - last + 1 + r, place < last),
+            )
+        ):
+            inside = (mine >= 0) & (mine <= last)
+            spot = lax.rem(block + depth, depth)
+            copy = pltpu.make_async_remote_copy(
+                src_ref=held_ref.at[spot],
+                dst_ref=land_ref.at[r, k],
+                send_sem=sems.at[0, r],
+                recv_sem=sems.at[1, r],
+                device_id={"dp": peer},
+                device_id_type=mesh_ids,
+            )
+            hop.append((copy, leaves, arrives & inside, lax.rem(mine + depth, depth)))
+        hops.append(hop)
+    step, steps = pl.program_id(0), pl.num_programs(0)
+
+    def start(r):
+        for copy, leaves, _, _ in hops[r]:
+            pl.when(leaves)(copy.start)
+
+    def arrive(r):
+        for k, (copy, _, arrives, block) in enumerate(hops[r]):
+
+            @pl.when(arrives)
+            def _(copy=copy, block=block, k=k):
+                copy.wait_recv()
+                total = held_ref[block].astype(F32) + land_ref[r, k].astype(F32)
+                held_ref[block] = total.astype(BF16)
+
+    @pl.when(step == 0)
+    def _():
+        for copy in loads + trades:
+            copy.start()
+
+    @pl.when(step == 1)
+    def _():
+        for load in loads:
+            load.wait()
+        for trade in trades:
+            trade.wait_recv()
+            trade.wait_send()
+        start(0)
+
+    for r, turn in enumerate((3, 5, steps - 1)):
+
+        @pl.when(step == turn)
+        def _(r=r):
+            arrive(r)
+            if r + 1 < last:
+                start(r + 1)
+            else:
+                for hop in hops:
+                    for copy, leaves, _, _ in hop:
+                        pl.when(leaves)(copy.wait_send)
+                share_ref[...] = held_ref[place]
+
+
 def small_sum_kernel(
-    own_ref, cut_ref, all_ref, joined_ref, swapped_ref, stage_ref, total_ref, send_sems, recv_sems, local_sem
+    heads,
+    own_ref,
+    cut_ref,
+    all_ref,
+    shared_ref,
+    joined_ref,
+    swapped_ref,
+    stage_ref,
+    total_ref,
+    send_sems,
+    recv_sems,
+    local_sem,
 ):
     depth, ring = stage_ref.shape[0], all_ref.shape[0]
     place, me = lax.axis_index("dp"), lax.axis_index("seq")
@@ -1407,32 +1580,41 @@
         copy.start()
         second.append(copy)
     all_ref[me] = total
-    for copy in second + swaps:
+    for copy in second:
+        copy.wait_recv()
+    shared_rows = shared_ref.shape[0]
+    shared = all_ref[0, :shared_rows]
+    for s in range(1, ring):
+        shared = shared + all_ref[s, :shared_rows]
+    shared_ref[...] = shared
+    for copy in swaps:
         copy.wait_recv()
     keep.wait()
-    width = cut_ref.shape[2] // 4
-    for block in range(4):
+    size = cut_ref.shape[2] // (4 * heads)
+    for part in range(4 * heads):
+        block, j = part // heads, part % heads
         for s in range(ring):
-            start = (block * ring + s) * width
-            joined_ref[:, start : start + width] = swapped_ref[
-                s, :, block * width : (block + 1) * width
+            start = (block * ring * heads + rank_head(s, j, heads)) * size
+            joined_ref[:, start : start + size] = swapped_ref[
+                s, :, part * size : (part + 1) * size
             ].astype(F32)
     for copy in first + second + swaps:
         copy.wait_send()
 
 
-def small_sum(own, cut, collective_id):
+def small_sum(own, shared_rows, cut, heads, collective_id):
     depth, ring = lax.axis_size("dp"), lax.axis_size("seq")
     count = depth + 2 * ring - 3
     vmem, anywhere = pl.BlockSpec(memory_space=pltpu.VMEM), pl.BlockSpec(memory_space=pl.ANY)
     return pl.pallas_call(
-        small_sum_kernel,
+        functools.partial(small_sum_kernel, heads),
         out_shape=[
             jax.ShapeDtypeStruct((ring,) + own.shape, F32),
+            jax.ShapeDtypeStruct((shared_rows, own.shape[1]), F32),
             jax.ShapeDtypeStruct((cut.shape[1], ring * cut.shape[2]), F32),
         ],
         in_specs=[vmem, anywhere],
-        out_specs=[vmem, vmem],
+        out_specs=[vmem, vmem, vmem],
         scratch_shapes=[
             pltpu.VMEM(cut.shape, cut.dtype),
             pltpu.VMEM((depth,) + own.shape, F32),
@@ -1452,7 +1634,7 @@
     greet([lax.rem(me + k, ring) for k in range(1, ring)])
 
 
-def plane_scatter_dot_kernel(count, dims, fill, swaps, *refs):
+def plane_scatter_dot_kernel(count, dims, fill, swaps, back, *refs):
     refs = list(refs)
 
     def take(size):
@@ -1461,25 +1643,36 @@
         return taken
 
     left_hbm, right_hbm, fill_hbm = take(count), take(count), take(int(fill))
-    cut_refs = take(swaps)
+    cut_refs, back_hbm = take(swaps), take(2 * back)
     (sum_ref,) = take(1)
     terms = take(count if fill else 0)
     spread_refs, swapped_refs = take(swaps), take(swaps)
     lefts, rights, fill_refs = take(count), take(count), take(int(fill))
     out_ref, own_ref, near_ref, far_in_ref, side_in_ref = take(5)
-    send_sems, recv_sems, load_sems = refs
+    send_sems, recv_sems, load_sems = take(3)
     loads = []
     for k in range(count):
         for source, target in ((left_hbm[k], lefts[k]), (right_hbm[k], rights[k])):
             load = pltpu.make_async_copy(source, target, load_sems.at[len(loads)])
             load.start()
             loads.append(load)
+    me, sibling, across, along = plane_peers()
+    far = along + across - me
+    flip = sibling - me
+    if back:
+        error_ref, down_ref, error_sems, down_sem = refs
+        error_order = [far + flip, far, across + flip, across, along + flip, along, sibling, me]
+        down_load = pltpu.make_async_copy(back_hbm[1], down_ref, down_sem)
+        down_load.start()
+        error_loads = [
+            pltpu.make_async_copy(back_hbm[0].at[slab], error_ref.at[k % 2], error_sems.at[k % 2])
+            for k, slab in enumerate(error_order)
+        ]
+        error_loads[0].start()
+        error_loads[1].start()
     if fill:
         fill_load = pltpu.make_async_copy(fill_hbm[0], fill_refs[0], load_sems.at[2 * count])
         fill_load.start()
-    me, sibling, across, along = plane_peers()
-    far = along + across - me
-    flip = sibling - me
     rows, columns = sum_ref.shape
     half = rows // 2
     upper, lower = pl.ds(0, half), pl.ds(half, half)
@@ -1497,9 +1690,29 @@
         greet((sibling, across, along))
     for load in loads:
         load.wait()
+    if back:
+        down_load.wait()
     wide = 512
+    turns = iter(range(8))
+
+    def feed_back(slab):
+        k = next(turns)
+        error_loads[k].wait()
+        units = down_ref.shape[0]
+        grad = low_dot(error_ref[k % 2], down_ref[...], NT)
+        gate = lefts[0][slab, :, :units].astype(F32)
+        up = lefts[0][slab, :, units:].astype(F32)
+        opening = sigmoid(gate)
+        gate_err = grad * up * (opening * (1.0 + gate * (1.0 - opening)))
+        up_err = grad * (gate * opening)
+        lefts[0][slab] = jnp.concatenate([gate_err, up_err], 1).astype(BF16)
+        if k + 2 < len(error_loads):
+            error_loads[k + 2].start()
 
     def slab_dot(slab, target):
+        if back:
+            feed_back(slab)
+
         @pl.loop(0, columns // wide)
         def _(i):
             at = pl.ds(pl.multiple_of(i * wide, wide), wide)
@@ -1593,24 +1806,32 @@
         copy.wait_send()
 
 
-def plane_scatter_dot(lefts, rights, dims, collective_id, fill=None, cut=None):
+def plane_scatter_dot(lefts, rights, dims, collective_id, fill=None, cut=None, back=()):
     count = len(lefts)
     ring, rows, _ = lefts[0].shape
     columns = rights[0].shape[1 - dims[1][0]]
     filled = fill is not None
     fills = [fill] if filled else []
     vmem, anywhere = pl.BlockSpec(memory_space=pltpu.VMEM), pl.BlockSpec(memory_space=pl.ANY)
+    back_scratch = []
+    if back:
+        back_scratch = [
+            pltpu.VMEM((2,) + back[0].shape[1:], BF16),
+            pltpu.VMEM(back[1].shape, BF16),
+            pltpu.SemaphoreType.DMA((2,)),
+            pltpu.SemaphoreType.DMA,
+        ]
     cuts = [] if cut is None else [cut]
     total = 10 + len(cuts) * (ring - 1)
     term_shapes = [
         jax.ShapeDtypeStruct((fill.shape[1], left.shape[2]), BF16) for left in lefts if filled
     ]
     return pl.pallas_call(
-        functools.partial(plane_scatter_dot_kernel, count, dims, filled, len(cuts)),
+        functools.partial(plane_scatter_dot_kernel, count, dims, filled, len(cuts), len(back) // 2),
         out_shape=[jax.ShapeDtypeStruct((rows, columns), F32)]
         + term_shapes
         + [jax.ShapeDtypeStruct((cut.shape[1], ring * cut.shape[2]), F32) for cut in cuts],
-        in_specs=[anywhere] * (2 * count + len(fills) + len(cuts)),
+        in_specs=[anywhere] * (2 * count + len(fills) + len(cuts) + len(back)),
         out_specs=[vmem] * (1 + len(term_shapes) + len(cuts)),
         scratch_shapes=[pltpu.VMEM(cut.shape, BF16) for cut in cuts]
         + [pltpu.VMEM(left.shape, BF16) for left in lefts]
@@ -1625,13 +1846,14 @@
             pltpu.SemaphoreType.DMA((total,)),
             pltpu.SemaphoreType.DMA((total,)),
             pltpu.SemaphoreType.DMA((2 * count + len(fills) + len(cuts),)),
-        ],
+        ]
+        + back_scratch,
         compiler_params=pltpu.CompilerParams(
             collective_id=collective_id, has_side_effects=True, vmem_limit_bytes=VMEM_LIMIT
         ),
         cost_estimate=lasting(45),
         name="plane_scatter_dot",
-    )(*lefts, *rights, *fills, *cuts)
+    )(*lefts, *rights, *fills, *cuts, *back)
 
 
 def gather_in_turn(own_ref, all_ref, send_sems, recv_sems, use):
@@ -1682,15 +1904,13 @@
 def gather_feed_kernel(
     own_hbm,
     pair_hbm,
-    down_hbm,
     error_hbm,
     all_hbm,
     activated_hbm,
-    pair_err_hbm,
+    pair_part_hbm,
     down_term_ref,
     own_ref,
     pair_ref,
-    down_ref,
     error_ref,
     all_ref,
     activated_out,
@@ -1705,7 +1925,6 @@
     for source, target in (
         (own_hbm, own_ref),
         (pair_hbm, pair_ref),
-        (down_hbm, down_ref),
         (error_hbm, error_ref),
     ):
         load = pltpu.make_async_copy(source, target, load_sems.at[len(loads)])
@@ -1718,7 +1937,7 @@
     tall = 256
     wide = 512
     rows, columns = own_ref.shape
-    units = down_ref.shape[0]
+    units = pair_ref.shape[1] // 2
 
 
     def use(slab):
@@ -1736,18 +1955,14 @@
             values = all_ref[slab, at, :]
             pair = low_dot(values, pair_ref[...], NN)
             gate, up = pair[:, :units], pair[:, units:]
-            grad = low_dot(error_ref[slab, at, :], down_ref[...], NT)
-            opening = sigmoid(gate)
-            gate_open = gate * opening
-            activated_out[turn, at, :] = (gate_open * up).astype(BF16)
-            gate_err = grad * up * (opening * (1.0 + gate * (1.0 - opening)))
-            pair_out[turn, at, :] = jnp.concatenate([gate_err, grad * gate_open], 1).astype(BF16)
+            activated_out[turn, at, :] = (gate * sigmoid(gate) * up).astype(BF16)
+            pair_out[turn, at, :] = pair.astype(BF16)
 
         batch = []
         for k, (source, target) in enumerate(
             (
                 (activated_out.at[turn], activated_hbm.at[slab]),
-                (pair_out.at[turn], pair_err_hbm.at[slab]),
+                (pair_out.at[turn], pair_part_hbm.at[slab]),
                 (all_ref.at[slab], all_hbm.at[slab]),
             )
         ):
@@ -1772,10 +1987,10 @@
             save.wait()
 
 
-def gather_feed(own, pair_own, down_own, error_all, collective_id):
+def gather_feed(own, pair_own, error_all, collective_id):
     ring = lax.axis_size("seq")
     rows, columns = own.shape
-    units = down_own.shape[0]
+    units = pair_own.shape[1] // 2
     anywhere = pl.BlockSpec(memory_space=pl.ANY)
     return pl.pallas_call(
         gather_feed_kernel,
@@ -1783,30 +1998,29 @@
             jax.ShapeDtypeStruct((ring, rows, columns), BF16),
             jax.ShapeDtypeStruct((ring, rows, units), BF16),
             jax.ShapeDtypeStruct((ring, rows, 2 * units), BF16),
-            jax.ShapeDtypeStruct(down_own.shape, BF16),
+            jax.ShapeDtypeStruct((units, columns), BF16),
         ],
-        in_specs=[anywhere] * 4,
+        in_specs=[anywhere] * 3,
         out_specs=[anywhere] * 3 + [pl.BlockSpec(memory_space=pltpu.VMEM)],
         scratch_shapes=[
             pltpu.VMEM((rows, columns), BF16),
             pltpu.VMEM(pair_own.shape, BF16),
-            pltpu.VMEM(down_own.shape, BF16),
             pltpu.VMEM((ring, rows, columns), BF16),
             pltpu.VMEM((ring, rows, columns), BF16),
             pltpu.VMEM((2, rows, units), BF16),
             pltpu.VMEM((2, rows, 2 * units), BF16),
-            pltpu.VMEM(down_own.shape, F32),
+            pltpu.VMEM((units, columns), F32),
             pltpu.SemaphoreType.DMA((9,)),
             pltpu.SemaphoreType.DMA((9,)),
-            pltpu.SemaphoreType.DMA((4,)),
+            pltpu.SemaphoreType.DMA((3,)),
             pltpu.SemaphoreType.DMA((2, 3)),
         ],
         compiler_params=pltpu.CompilerParams(
             collective_id=collective_id, has_side_effects=True, vmem_limit_bytes=VMEM_LIMIT
         ),
-        cost_estimate=lasting(60),
+        cost_estimate=lasting(46),
         name="gather_feed",
-    )(own, pair_own, down_own, error_all)
+    )(own, pair_own, error_all)
 
 
 def gather_branch_kernel(
@@ -1967,49 +2181,61 @@
 
     upstream = valid_rows * cotangent.reshape(row_count, model_width).astype(F32)
     out_err = upstream.astype(BF16)
-    turns = [(depth * s + z, ring * z + s) for s in range(ring) for z in range(depth)]
-    down_own = gather_rows(down_weight, "dp")
-    out_own = gather_rows(lax.ppermute(output_weight, ("dp", "seq"), turns), "dp")
+    out_rows = gather_rows(output_weight, "dp")
+    own_heads = [rank_head(rank, j, heads) for j in range(heads)]
 
     def own_lanes(pair):
         rows = pair.shape[0]
-        decay_part = lax.dynamic_slice(pair, (0, rank * heads), (rows, heads))
-        other = pair.shape[1] - head_count
-        if other:
-            strength_part = lax.dynamic_slice(pair, (0, head_count + rank * heads), (rows, heads))
-            decay_part = jnp.concatenate([decay_part, strength_part], 1)
-        return jnp.pad(decay_part, ((0, 0), (0, 128 - decay_part.shape[1])))
+        lanes = [
+            lax.dynamic_slice(pair, (0, start + head), (rows, 1))
+            for start in range(0, pair.shape[1], head_count)
+            for head in own_heads
+        ]
+        return jnp.pad(jnp.concatenate(lanes, 1), ((0, 0), (0, 128 - len(lanes))))
 
     decay_own = own_lanes(decay_weight)
     params = jnp.pad(own_lanes(jnp.stack([decay_log, decay_bias])), ((0, 6), (0, 0)))
-    taps = lax.dynamic_slice(
-        conv_weight.reshape(tap_count, 3, key_width), (0, 0, rank * width), (tap_count, 3, width)
-    ).reshape(tap_count, 3 * width)
+    taps = jnp.concatenate(
+        [
+            lax.dynamic_slice(
+                conv_weight, (0, block * key_width + head * head_size), (tap_count, head_size)
+            )
+            for block in range(3)
+            for head in own_heads
+        ],
+        1,
+    )
     gain = head_gain.reshape(1, head_size)
 
     def chunks(value):
         return value.reshape(ring, seqs, span, value.shape[-1])
 
     normed_all, in_own, pair_cut, mixed, gate_raw, logits = plane_open(
-        normed_low, input_weight, gate_up_weight, decay_own, 1
+        normed_low, input_weight, gate_up_weight, decay_own, heads, 1
     )
     normed_all = normed_all.reshape(all_rows, model_width)
     in_own = in_own.reshape(model_width, 4 * width)
     pair_own = gather_rows(pair_cut.reshape(ring * weight_rows, 2 * units), "dp")
-    mixed, out_own, down_own = lax.optimization_barrier((mixed, out_own, down_own))
+    mixed, out_rows, down_weight = lax.optimization_barrier((mixed, out_rows, down_weight))
+    down_own = gather_rows(down_weight, "dp")
     mixed, gate_raw, logits = chunks(mixed), chunks(gate_raw), chunks(logits)
-    gated, memory, inverse, fresh, mixer_out, out_err_all = run_forward(
-        mixed, gate_raw, logits, taps, params, gain, heads, out_err, 5
+    gated, memory, inverse, fresh, mixer_out, out_err_all, out_own = run_forward(
+        mixed, gate_raw, logits, taps, params, gain, heads, out_err, out_rows, 5
     )
     gated = gated.reshape(ring, row_count, width)
     hidden = tokens + plane_scatter_dot([gated], [out_own], NN, 2)[0]
     second_low = rms_norm(hidden, second_gain).astype(BF16)
-    second_all, activated, pair_err, down_term = gather_feed(
-        second_low, pair_own, down_own, out_err_all, 3
+    second_all, activated, pair_part, down_term = gather_feed(
+        second_low, pair_own, out_err_all, 3
     )
     down_share = scatter_rows(down_term, "dp").astype(F32)
     second_grad, pair_term = plane_scatter_dot(
-        [pair_err], [pair_own], NT, 4, second_all.reshape(all_rows, model_width)
+        [pair_part],
+        [pair_own],
+        NT,
+        4,
+        second_all.reshape(all_rows, model_width),
+        back=(out_err_all, down_own),
     )
     pair_share = scatter_rows(pair_term, "dp")
     hidden_part, second_gain_grad = rms_back(hidden, second_gain, second_grad)
@@ -2018,7 +2244,7 @@
     gated_grad, output_term, down_part = gather_branch(
         branch_err, gated, out_own, activated, down_own, 11
     )
-    in_err, logit_grad, taps_grad, param_grad, gain_grad, final_part = run_backward(
+    in_err, logit_grad, taps_grad, param_grad, gain_grad, final_part, output_share = run_backward(
         mixed,
         gate_raw,
         logits,
@@ -2031,6 +2257,7 @@
         mixer_out,
         gated_grad.reshape(ring, seqs, span, width),
         down_part,
+        output_term,
         12,
     )
     result = valid_rows * (hidden + final_part)
@@ -2038,8 +2265,10 @@
     input_term, in_err, logit_grad, down_share, pair_share = lax.optimization_barrier(
         (input_term, in_err, logit_grad, down_share, pair_share)
     )
+    lanes = logit_grad.shape[-1]
+    decay_term = low_dot(normed_all, logit_grad.reshape(all_rows, lanes), TN)
+    decay_term, in_err = lax.optimization_barrier((decay_term, in_err))
     input_cut = scatter_rows(input_term, "dp")
-    lanes = logit_grad.shape[-1]
     decay_twice = decay_own + jnp.roll(decay_own, lanes // 2, 1)
     normed_grad, gate_up_share = plane_scatter_dot(
         [
@@ -2051,41 +2280,42 @@
         6,
         cut=pair_share.reshape(ring, weight_rows, 2 * units),
     )
-    output_term, input_cut, normed_grad = lax.optimization_barrier(
-        (output_term, input_cut, normed_grad)
-    )
-    output_share = lax.ppermute(
-        scatter_rows(output_term, "dp"), ("dp", "seq"), [(b, a) for a, b in turns]
-    ).astype(F32)
     token_part, first_gain_grad = rms_back(tokens, first_gain, normed_grad)
     inputs_grad = hidden_grad + token_part
-    decay_term = low_dot(normed_all, logit_grad.reshape(all_rows, lanes), TN)
     decay_term = decay_term[:, : 2 * heads] + decay_term[:, lanes // 2 : lanes // 2 + 2 * heads]
-    pieces = [
-        jnp.transpose(decay_term),
-        taps_grad[:tap_count],
-        param_grad[:2, : 2 * heads],
-        first_gain_grad,
-        second_gain_grad,
-        gain_grad[0],
-    ]
-    sizes = [piece.size for piece in pieces]
-    packed = jnp.concatenate([piece.reshape(-1) for piece in pieces])
+    shared = jnp.concatenate([first_gain_grad, second_gain_grad, gain_grad[0]])
+    shared = jnp.pad(shared, (0, -shared.size % 1024))
+    pieces = [jnp.transpose(decay_term), taps_grad[:tap_count], param_grad[:2]]
+    packed = jnp.concatenate([shared] + [piece.reshape(-1) for piece in pieces])
     packed = jnp.pad(packed, (0, -packed.size % 1024)).reshape(-1, 128)
-    summed, input_share = small_sum(packed, input_cut.reshape(ring, weight_rows, 4 * width), 7)
-    summed = summed.reshape(ring, -1)
+    packed, input_cut, inputs_grad, result = lax.optimization_barrier(
+        (packed, input_cut, inputs_grad, result)
+    )
+    summed, shared_sum, input_share = small_sum(
+        packed,
+        shared.size // 128,
+        input_cut.reshape(ring, weight_rows, 4 * width),
+        heads,
+        7,
+    )
+    shared_sum = shared_sum.reshape(-1)
+    first_gain_grad = shared_sum[:model_width]
+    second_gain_grad = shared_sum[model_width : 2 * model_width]
+    gain_grad = shared_sum[2 * model_width : 2 * model_width + head_size]
     parted = []
-    start = 0
-    for size in sizes:
-        parted.append(summed[:, start : start + size])
-        start += size
-    decay_sum, taps_sum, param_sum = parted[:3]
-    first_gain_grad, second_gain_grad, gain_grad = [part.sum(0) for part in parted[3:]]
-    decay_sum = decay_sum.reshape(ring, 2, heads, model_width)
-    decay_weight_grad = jnp.transpose(decay_sum, (3, 1, 0, 2)).reshape(model_width, 2 * head_count)
-    taps_sum = jnp.transpose(taps_sum.reshape(ring, tap_count, 3, width), (1, 2, 0, 3))
-    param_sum = jnp.transpose(param_sum.reshape(ring, 2, 2 * heads)[..., :heads], (1, 0, 2))
-    param_sum = param_sum.reshape(2, head_count)
+    start = shared.size // 128
+    for piece in pieces:
+        count = piece.size // 128
+        parted.append(summed[:, start : start + count])
+        start += count
+    decay_sum, taps_sum, param_sum = parted
+    chips = ring // 2
+    decay_sum = decay_sum.reshape(chips, 2, 2, heads, model_width)
+    decay_weight_grad = jnp.transpose(decay_sum, (4, 2, 1, 3, 0)).reshape(model_width, -1)
+    taps_sum = taps_sum.reshape(chips, 2, tap_count, 3, heads, head_size)
+    taps_sum = jnp.transpose(taps_sum, (2, 3, 1, 4, 0, 5))
+    param_sum = param_sum[:, :, :heads].reshape(chips, 2, 2, heads)
+    param_sum = jnp.transpose(param_sum, (2, 1, 3, 0)).reshape(2, head_count)
     return (
         result.reshape(inputs.shape),
         inputs_grad.reshape(inputs.shape),
@@ -2096,7 +2326,7 @@
         param_sum[0],
         param_sum[1],
         gain_grad,
-        output_share,
+        output_share.astype(F32),
         second_gain_grad,
         gate_up_share,
         down_share,
@@ -2138,7 +2368,7 @@
     ring = mesh.shape["seq"]
 
     def whole_device(*arrays):
-        heads_divide = ring == 8 and arrays[6].shape[0] % ring == 0
+        heads_divide = ring == 8 and 2 * arrays[6].shape[0] == ring * mesh.shape["dp"]
         return (split_heads_device if heads_divide else per_device)(*arrays)
 
     return jax.shard_map(

time: 657 us -> 601 us (0.915)
  Pallas kernels: 531 us -> 500 us
  waiting for transfers between devices: 36.8 us -> 11.6 us
  starting transfers between devices: 8.12 us -> 0.41 us
    pallas_call x2, Pallas kernels: 180 us -> 130 us  [the longest x1 104 us: plane_open(): pl.pallas_call(functools.partial(plane_open_kernel, heads), out_shape=[ja...]
    ppermute x2 -> x0, waiting for transfers between devices: 16.1 us -> none  [the longest x1 11.9 us: split_heads_device(): lax.ppermute(scatter_rows(output_term, 'dp'), ('dp', 'seq'), [(b, a) for...]
    pallas_call x3, Pallas kernels: 151 us -> 162 us  [plane_scatter_dot(): pl.pallas_call(functools.partial(plane_scatter_dot_kernel, count, dims, f...]
    reduce_scatter x4 -> x3, waiting for transfers between devices: 14.1 us -> 3.63 us  [scatter_rows(): return lax.psum_scatter(value, axis, scatter_dimension=0, tiled=True)]
    pallas_call x1, Pallas kernels: 51 us -> 59.3 us  [run_backward(): pl.pallas_call(mixer_backward, grid=(steps,), in_specs=[rows(3 * width),...]
    ppermute x2 -> x0, starting transfers between devices: 7.41 us -> none  [the longest x1 4.73 us: split_heads_device(): lax.ppermute(output_weight, ('dp', 'seq'), turns)]
  transfers between devices with their start and end apart: 9 -> 6, of which waited for: 4 -> 2; matrix products, arithmetic and copies ran while one was open for 8% -> 9% of each run, Pallas kernels for 73% -> 80%
where the time goes in v4:
time: 601 us; the launch traced here: 596 us
  Pallas kernels  500 us (83%)
  other arithmetic  25.8 us (4%)
  local copies, waits for them, and re-layouts  23 us (4%)
  matrix products  20.1 us (3%)
  between operations  14.8 us (2%)
  waiting for transfers between devices  11.6 us (2%)
    pallas_call x3, Pallas kernels, plane_scatter_dot(): pl.pallas_call(functools.partial(plane_scatter_dot_kernel, count, dims, f...  162 us
    pallas_call x1, Pallas kernels, plane_open(): pl.pallas_call(functools.partial(plane_open_kernel, heads), out_shape=[ja...  104 us
    pallas_call x1, Pallas kernels, run_backward(): pl.pallas_call(mixer_backward, grid=(steps,), in_specs=[rows(3 * width),...  59.3 us
    pallas_call x1, Pallas kernels, run_forward(): pl.pallas_call(mixer_forward, grid=(steps,), in_specs=[rows(3 * width), r...  55.8 us
    pallas_call x1, Pallas kernels, gather_feed(): pl.pallas_call(gather_feed_kernel, out_shape=[jax.ShapeDtypeStruct((ring,...  48.4 us
    pallas_call x1, Pallas kernels, gather_branch(): pl.pallas_call(gather_branch_kernel, out_shape=[jax.ShapeDtypeStruct((rin...  44.8 us
    pallas_call x1, Pallas kernels, small_sum(): pl.pallas_call(functools.partial(small_sum_kernel, heads), out_shape=[jax...  25.2 us
    dot_general x2, matrix products, low_dot(): lax.dot_general(left, right, (dims, ((), ())), preferred_element_type=F32)  20.1 us
  transfers between devices with their start and end apart: 6, of which 2 were waited for; matrix products, arithmetic and copies ran while one was open for 9% of the time, Pallas kernels for 80%

profile of v4, /device:TPU:1, one launch (start us, length us, event | category | flops | bytes accessed | tf_op | source)
XLA Modules:
  0.0 595.9 jit_solution(1455159598452911631)
XLA Ops:
  7.2 0.7 all-gather.4.cloned.1.call-update
  8.0 0.9 constant_dynamic-slice_fusion.11
  8.9 0.3 copy.50
  9.3 1.6 fusion.2
  10.9 0.1 pad_slice_fusion
  11.0 1.3 pad_add_fusion
  12.3 1.3 fusion.4.first_ref
  13.5 104.5 %plane_open.1 = (bf16[8,256,2048]{2,1,0:T(8,128)(2,1)}, bf16[4,512,1024]{2,1,0:T(8,128)(2,1)}, bf16[8,64,1408]{2,1,0:T(8,128)(2,1)}, bf16[8,256,768]{2,1,0:T(8,1...) custom-call(bf16[256,2048]{1,0:T(8,128)(2,1)} %fusion.4.first_ref, bf16[64,8192]{1,0:T(8,128)(2,1)} %weight_hbm.1, ...), custom_call_target="tpu_custom_call" | custom-call | bytes 525000000 | tf_op jit(solution)/shard_map/plane_open/pallas_call | solution.py:1220
  118.2 0.7 all-gather.8.cloned.1.call-update
  118.8 0.2 reduce-scatter.4.cloned.1.call-start
  119.1 0.1 constant_dynamic-slice_fusion.1
  119.3 0.6 pad.23.param_ref
  119.9 0.7 constant_dynamic-update-slice_fusion.5
  120.6 0.7 constant_dynamic-update-slice_fusion.4
  121.3 0.7 constant_dynamic-update-slice_fusion.3
  121.9 0.7 constant_dynamic-update-slice_fusion.2
  122.6 0.7 constant_dynamic-update-slice_fusion.1
  123.3 0.7 constant_dynamic-update-slice_fusion.taps_ref
  124.1 1.2 fusion.1.own_ref
  125.3 55.8 %mixer_forward.1 = (bf16[8,2,128,256]{3,2,1,0:T(8,128)(2,1)}, f32[8,2,2,128,128]{4,3,2,1,0:T(8,128)}, f32[8,2,2,128,128]{4,3,2,1,0:T(8,128)}, f32[8,2,128,256]{3...) custom-call(bf16[8,2,128,768]{3,2,1,0:T(8,128)(2,1)} %bitcast.84, ...), custom_call_target="tpu_custom_call" | custom-call | bytes 192500000 | tf_op jit(solution)/shard_map/mixer_forward/pallas_call | solution.py:782
  181.2 44.4 %plane_scatter_dot.3 = f32[256,2048]{1,0:T(8,128)} custom-call(bf16[8,256,256]{2,1,0:T(8,128)(2,1)} %bitcast.92, bf16[256,2048]{1,0:T(8,128)(2,1)} %get-tuple-element.72.refs_1_.weight_hbm), custom_call_target="tpu_custom_call" | custom-call | bytes 157500000 | tf_op jit(solution)/shard_map/plane_scatter_dot/pallas_call | solution.py:1829
  225.6 2.0 multiply_reduce_fusion.2
  227.5 1.2 multiply_convert_fusion.own_hbm
  228.8 48.4 %gather_feed.1 = (bf16[8,256,2048]{2,1,0:T(8,128)(2,1)}, bf16[8,256,704]{2,1,0:T(8,128)(2,1)}, bf16[8,256,1408]{2,1,0:T(8,128)(2,1)}, bf16[704,2048]{1,0:T(8,128)(2,1)}) custom-call(bf16[256,2048]{1,0:T(8,128)(2,1)} %multiply_convert_fusion.own_hbm, bf16[2048,1408]{1,0:T(8,128)(2,1)} %all-gather.6.cloned.1.call-done.pair_hbm.refs_1_, ...), custom_call_target="tpu_custom_call" | custom-call | bytes 161000000 | tf_op jit(solution)/shard_map/gather_feed/pallas_call | solution.py:1995
  277.2 6.6 %all-gather.8.cloned.1.call-done.refs_4_.down_hbm = bf16[704,2048]{1,0:T(8,128)(2,1)} async-done(((bf16[176,2048]{1,0:T(8,128)(2,1)}), bf16[704,2048]{1,0:T(8,128)(2,1)}) %all-gather.8.cloned.1.call-update) | async-done | bytes 2883600 | tf_op jit(solution)/shard_map/all_gather | solution.py:909
  283.8 60.8 %plane_scatter_dot.4 = (f32[256,2048]{1,0:T(8,128)}, bf16[2048,1408]{1,0:T(8,128)(2,1)}) custom-call(bf16[8,256,1408]{2,1,0:T(8,128)(2,1)} %get-tuple-element.75.refs_0_, bf16[2048,1408]{1,0:T(8,128)(2,1)} %all-gather.6.cloned.1.call-done.pair_hbm.refs_1_, bf16[2048,2048]{1,0:T(8,128)(2,1)} %bitcast.89, ...), custom_call_target="tpu_custom_call" | custom-call | bytes 157500000 | tf_op jit(solution)/shard_map/plane_scatter_dot/pallas_call | solution.py:1829
  344.7 2.3 multiply_reduce_fusion
  347.1 0.1 copy-done.4
  347.2 2.4 fusion.13
  349.6 44.8 %gather_branch.1 = (bf16[8,256,256]{2,1,0:T(8,128)(2,1)}, bf16[256,2048]{1,0:T(8,128)(2,1)}, bf16[8,256,2048]{2,1,0:T(8,128)(2,1)}) custom-call(bf16[256,2048]{1,0:T(8,128)(2,1)} %get-tuple-element.152.own_hbm, bf16[8,256,256]{2,1,0:T(8,128)(2,1)} %bitcast.93, bf16[256,2048]{1,0:T(8,128)(2,1)} %get-tuple-element.72.refs_1_.weight_hbm, ...), custom_call_target="tpu_custom_call" | custom-call | bytes 157500000 | tf_op jit(solution)/shard_map/gather_branch/pallas_call | solution.py:2095
  394.4 59.3 %mixer_backward.1 = (bf16[8,2,128,1024]{3,2,1,0:T(8,128)(2,1)}, bf16[8,2,128,128]{3,2,1,0:T(8,128)(2,1)}, f32[8,768]{1,0:T(8,128)}, f32[8,128]{1,0:T(8,128)}, f3...) custom-call(bf16[8,2,128,768]{3,2,1,0:T(8,128)(2,1)} %bitcast.85, ...), custom_call_target="tpu_custom_call" | custom-call | bytes 192500000 | tf_op jit(solution)/shard_map/mixer_backward/pallas_call | solution.py:846
  453.7 14.2 %convolution_convert_fusion = bf16[2048,1024]{1,0:T(8,128)(2,1)} fusion(bf16[2048,2048]{1,0:T(8,128)(2,1)} %bitcast.119, bf16[2048,1024]{1,0:T(8,128)(2,1)} %bitcast.95), kind=kOutput, calls=%fused_computation | convolution fusion | flops 8592031744 | bytes 16777216 | tf_op jit(solution)/shard_map/dot_general | solution.py:2136
  467.9 2.4 convert_element_type.70
  470.3 0.7 copy-done.11
  471.1 0.2 copy-done.7
  471.3 0.8 convert_element_type.71
  472.1 0.7 slice_bitcast_fusion.4
  472.8 0.7 slice_bitcast_fusion.2
  473.5 5.8 fusion.16
  479.3 57.2 %plane_scatter_dot.5 = (f32[256,2048]{1,0:T(8,128)}, f32[64,11264]{1,0:T(8,128)}) custom-call(bf16[8,256,1024]{2,1,0:T(8,128)(2,1)} %bitcast.96, bf16[8,256,128]{2,1,0:T(8,128)(2,1)} %bitcast.105, bf16[2048,1024]{1,0:T(8,128)(2,1)} %bitcast.94, bf16[2048,128]{1,0:T(8,128)(2,1)} %get-tuple-element.156.refs_3_, bf16[8,64,1408]{2,1,0:T(8,128)(2,1)} %bitcast.100), custom_call_target="tpu_custom_call" | custom-call | bytes 157500000 | tf_op jit(solution)/shard_map/plane_scatter_dot/pallas_call | solution.py:1829
  536.4 1.3 add_bitcast_fusion
  537.7 1.6 copy.51
  539.3 2.3 fusion.7
  541.6 0.6 fusion.10.own_ref
  542.3 4.9 fusion.9
  547.1 3.6 reduce-scatter.8.cloned.1.call-done
  550.8 25.2 %small_sum.1 = (f32[8,136,128]{2,1,0:T(8,128)}, f32[40,128]{1,0:T(8,128)}, f32[64,8192]{1,0:T(8,128)}) custom-call(f32[136,128]{1,0:T(8,128)} %fusion.10.own_ref, bf16[8,64,1024]{2,1,0:T(8,128)(2,1)} %bitcast.102), custom_call_target="tpu_custom_call" | custom-call | bytes 70000000 | tf_op jit(solution)/shard_map/small_sum/pallas_call | solution.py:1609
  576.0 1.3 slice_bitcast_fusion.3
  577.3 1.3 slice_bitcast_fusion
  578.7 0.8 slice.68
  579.4 0.9 slice.67
  580.3 1.0 slice.66
  581.3 0.1 copy.59
  581.4 0.1 copy.56
  581.5 0.6 squeeze.11
  582.1 0.1 copy.55
  582.2 0.6 squeeze.10
  582.8 0.1 reshape.224
  583.0 0.2 copy.52
  583.1 0.8 reshape.225
  584.0 0.7 reshape.227
  584.7 1.3 copy.68
  586.0 1.3 copy-done.5
  587.3 1.6 copy.69
  (54 shorter events, 0.7 us)
Async XLA Ops:
  7.2 111.0 %all-gather.4.cloned.1.call-start = ((), (), s32[]{:S(2)}) async-start(), calls=%async_computation.3 | async-start | bytes 1310720 | tf_op jit(solution)/shard_map/all_gather | solution.py:909
  7.9 220.8 %all-gather.6.cloned.1.call-start = ((), (), s32[]{:S(2)}) async-start(), calls=%async_computation.4 | async-start | bytes 7208960 | tf_op jit(solution)/shard_map/all_gather | solution.py:909
  9.3 3.0 copy-start
  9.3 3.0 copy-start.9
  118.0 1.1 copy-start.12
  118.0 1.1 copy-start.13
  118.0 6.0 %copy-start.14 = (s32[2,1]{0,1:T(1,128)S(1)}, s32[2,1]{0,1:T(1,128)}, u32[]{:S(2)}) copy-start(s32[2,1]{0,1:T(1,128)} %param.15) | copy-start | bytes 28
  118.0 6.0 %copy-start.3 = (bf16[2,1,128,2048]{3,2,1,0:T(8,128)(2,1)S(1)}, bf16[2,1,128,2048]{3,2,1,0:T(8,128)(2,1)}, u32[]{:S(2)}) copy-start(bf16[2,1,128,2048]{3,2,1,0:T(8,128)(2,1)} %param.27) | copy-start | bytes 3145732
  118.1 165.7 %all-gather.8.cloned.1.call-start = ((), (), s32[]{:S(2)}) async-start(), calls=%async_computation.5 | async-start | bytes 3604480 | tf_op jit(solution)/shard_map/all_gather | solution.py:909
  118.8 349.1 %reduce-scatter.4.cloned.1.call-start = ((), (), s32[]{:S(2)}) async-start(), calls=%async_computation.6 | async-start | bytes 3604480 | tf_op jit(solution)/shard_map/reduce_scatter | solution.py:913
  124.0 1.3 copy-start.10
  225.6 2.0 copy-start.8
  277.2 193.1 %reduce-scatter.6.cloned.1.call-start = ((), (), s32[]{:S(2)}) async-start(), calls=%async_computation.7 | async-start | bytes 7208960 | tf_op jit(solution)/shard_map/reduce_scatter | solution.py:913
  344.7 206.1 %reduce-scatter.8.cloned.1.call-start = ((), (), s32[]{:S(2)}) async-start(), calls=%async_computation.8 | async-start | bytes 5242880 | tf_op jit(solution)/shard_map/reduce_scatter | solution.py:913
  344.7 2.3 copy-start.2
  344.7 2.5 copy-start.4
  470.3 0.7 copy-start.11
  470.3 1.0 copy-start.7
  539.3 3.0 copy-start.1
  576.0 8.7 %copy-start.6 = (f32[64,8192]{1,0:T(8,128)S(1)}, f32[64,8192]{1,0:T(8,128)}, u32[]{:S(2)}) copy-start(f32[64,8192]{1,0:T(8,128)} %get-tuple-element.186) | copy-start | bytes 6291460
  584.7 2.6 copy-start.5
Sparse Core Ops, SparseCore 0:
  9.6 31.8 all-gather.3
  118.2 106.7 all-gather.5
  226.6 57.2 all-gather.7
  286.0 54.7 reduce-scatter.3
  344.8 116.1 reduce-scatter.5
  470.5 80.2 reduce-scatter.7

commit v5 on v4

--- a/solution.py
+++ b/solution.py
@@ -532,14 +532,12 @@
     out_ref,
     grad_ref,
     part_ref,
-    term_ref,
     error_ref,
     logit_grad_ref,
     taps_grad_ref,
     param_grad_ref,
     gain_grad_ref,
     sum_ref,
-    share_ref,
     state_ref,
     halo_ref,
     *scatter_refs,
@@ -547,8 +545,7 @@
     seqs, span, _ = mixed_ref.shape
     heads, head_size = memory_ref.shape[1], memory_ref.shape[2]
     step = pl.program_id(0)
-    scatter_in_steps(part_ref, sum_ref, *scatter_refs[:7])
-    sums_in_steps(term_ref, share_ref, *scatter_refs[7:])
+    scatter_in_steps(part_ref, sum_ref, *scatter_refs)
 
     @pl.when(step == 0)
     def _():
@@ -818,12 +815,10 @@
 
 
 def run_backward(
-    mixed, gate, logits, taps, params, gain, memory, inverse, fresh, out, grad, part, term, collective_id
+    mixed, gate, logits, taps, params, gain, memory, inverse, fresh, out, grad, part, collective_id
 ):
     steps, seqs, span, _ = mixed.shape
     _, part_rows, columns = part.shape
-    depth = lax.axis_size("dp")
-    term_rows = term.shape[0] // depth
     heads, head_size = memory.shape[2], memory.shape[3]
     width = heads * head_size
     edge = 16
@@ -860,7 +855,6 @@
             rows(width),
             rows(width),
             pl.BlockSpec(memory_space=pl.ANY),
-            pl.BlockSpec(memory_space=pl.ANY),
         ],
         out_specs=[
             rows(4 * width),
@@ -869,7 +863,6 @@
             whole((8, logits.shape[-1])),
             whole((8, head_size)),
             whole((part_rows, columns)),
-            whole((term_rows, columns)),
         ],
         out_shape=[
             jax.ShapeDtypeStruct((steps, seqs, span, 4 * width), BF16),
@@ -878,7 +871,6 @@
             jax.ShapeDtypeStruct((8, logits.shape[-1]), F32),
             jax.ShapeDtypeStruct((8, head_size), F32),
             jax.ShapeDtypeStruct((part_rows, columns), F32),
-            jax.ShapeDtypeStruct((term_rows, columns), BF16),
         ],
         scratch_shapes=[
             pltpu.VMEM((seqs, heads, head_size, head_size), F32),
@@ -890,19 +882,13 @@
             pltpu.SemaphoreType.DMA((10,)),
             pltpu.SemaphoreType.DMA((10,)),
             pltpu.SemaphoreType.DMA((4,)),
-            pltpu.VMEM((depth, term_rows, columns), BF16),
-            pltpu.VMEM((depth - 1, 2, term_rows, columns), BF16),
-            pltpu.SemaphoreType.DMA((2, depth - 1)),
-            pltpu.SemaphoreType.DMA((2, depth - 1)),
-            pltpu.SemaphoreType.DMA((depth // 2,)),
-            pltpu.SemaphoreType.DMA((2, depth // 2)),
         ],
         compiler_params=pltpu.CompilerParams(
             collective_id=collective_id, has_side_effects=True, vmem_limit_bytes=VMEM_LIMIT
         ),
         cost_estimate=lasting(55),
         name="mixer_backward",
-    )(mixed, mixed, gate, logits, taps, params, gain, memory, inverse, fresh, out, grad, part, term)
+    )(mixed, mixed, gate, logits, taps, params, gain, memory, inverse, fresh, out, grad, part)
 
 
 def gather_rows(value, axis):
@@ -980,15 +966,17 @@
     yield
 
 
-def chain_hops(all_ref, up_send, up_recv, down_send, down_recv):
+def chain_hops(all_ref, half, up_send, up_recv, down_send, down_recv):
     depth = all_ref.shape[0]
+    columns = all_ref.shape[2] // 2
+    own = pl.ds(half * columns, columns)
     place = lax.axis_index("dp")
     above, below = lax.rem(place + 1, depth), lax.rem(place + depth - 1, depth)
 
     def hop(slot, peer, send_sem, recv_sem):
         return pltpu.make_async_remote_copy(
-            src_ref=all_ref.at[slot],
-            dst_ref=all_ref.at[slot],
+            src_ref=all_ref.at[slot, :, own],
+            dst_ref=all_ref.at[slot, :, own],
             send_sem=send_sem,
             recv_sem=recv_sem,
             device_id={"dp": peer},
@@ -997,8 +985,10 @@
 
     hops = []
     for t in range(depth - 1):
-        up = hop(lax.rem(place + depth - t, depth), above, up_send.at[t], up_recv.at[t])
-        down = hop(lax.rem(place + t, depth), below, down_send.at[t], down_recv.at[t])
+        spot = half * (depth - 1) + t
+        up_slot, down_slot = lax.rem(place + depth - t, depth), lax.rem(place + t, depth)
+        up = hop(up_slot, above, up_send.at[spot], up_recv.at[spot])
+        down = hop(down_slot, below, down_send.at[spot], down_recv.at[spot])
         below_slot, above_slot = place + depth - 1 - t, place + 1 + t
         hops.append(
             (
@@ -1030,29 +1020,14 @@
             pl.when(leaves)(copy.wait_send)
 
 
-def greet_near(peers):
-    place, depth = lax.axis_index("dp"), lax.axis_size("dp")
-    barrier = pltpu.get_barrier_semaphore()
-    mesh_ids = pl.DeviceIdType.MESH
-    for peer in peers:
-        pl.semaphore_signal(barrier, inc=1, device_id={"seq": peer}, device_id_type=mesh_ids)
-    for peer in (lax.rem(place + 1, depth), lax.rem(place + depth - 1, depth)):
-        pl.semaphore_signal(barrier, inc=1, device_id={"dp": peer}, device_id_type=mesh_ids)
-    pl.semaphore_wait(barrier, len(peers) + 2)
-
-
 def greet_all(ring, depth):
     me, place = lax.axis_index("seq"), lax.axis_index("dp")
     barrier = pltpu.get_barrier_semaphore()
-    for axis, index, size in (("seq", me, ring), ("dp", place, depth)):
-        for k in range(1, size):
-            pl.semaphore_signal(
-                barrier,
-                inc=1,
-                device_id={axis: lax.rem(index + k, size)},
-                device_id_type=pl.DeviceIdType.MESH,
-            )
-    pl.semaphore_wait(barrier, ring + depth - 2)
+    peers = [{"seq": lax.rem(me + k, ring)} for k in range(1, ring)]
+    peers += [{"dp": lax.rem(place + k, depth)} for k in range(1, depth)]
+    for peer in peers:
+        pl.semaphore_signal(barrier, inc=1, device_id=peer, device_id_type=pl.DeviceIdType.MESH)
+    pl.semaphore_wait(barrier, len(peers))
 
 
 def spread_units(piece, target_ref, depth):
@@ -1133,14 +1108,15 @@
             copy = send_to(peer, source(peer), target, send_sems.at[spot], recv_sems.at[spot])
             copy.start()
             early.append(copy)
-    for copy in early:
-        copy.wait_recv()
-    for keep in keeps:
-        keep.wait()
     base = 4 * heads * (ring - 1)
-    hops = chain_hops(weight_all_ref, *chain_sems)
+    chains = [chain_hops(weight_all_ref, g, *chain_sems) for g in range(2)]
+    for g, chain in enumerate(chains):
+        for copy in early[g * base // 2 : (g + 1) * base // 2]:
+            copy.wait_recv()
+        for keep in keeps[2 * g * heads : 2 * (g + 1) * heads]:
+            keep.wait()
+        hop_start(chain[0])
     first = gather_phases(first_ref, first_all_ref, send_sems, recv_sems, local_sems.at[1], base)
-    hop_start(hops[0])
     next(first)
     load.wait()
     own = units // depth
@@ -1155,12 +1131,12 @@
     pair_keep = pltpu.make_async_copy(cut_ref.at[me], pair_all_ref.at[me], local_sems.at[2])
     pair_keep.start()
     later = exchange_copies(cut_ref, pair_all_ref.at[me], send_sems, recv_sems, base + 9)
-    hop_arrive(hops[0])
-    hop_start(hops[1])
-    next(first)
-    for t in range(1, depth - 2):
-        hop_arrive(hops[t])
-        hop_start(hops[t + 1])
+    for t in range(depth - 2):
+        for chain in chains:
+            hop_arrive(chain[t])
+            hop_start(chain[t + 1])
+        if t == 0:
+            next(first)
     next(first)
     next(first)
     lanes_load.wait()
@@ -1184,13 +1160,14 @@
     saves = [pltpu.make_async_copy(first_all_ref, first_all_hbm, local_sems.at[0])]
     saves[0].start()
     spread_slot(place, True)()
-    for hop in hops[:-1]:
+    for hop in chains[0][:-1]:
         for _, _, arrives, slot in hop:
             pl.when(arrives)(spread_slot(slot))
-    hop_arrive(hops[-1])
+    for chain in chains:
+        hop_arrive(chain[-1])
     saves.append(pltpu.make_async_copy(weight_all_ref, weight_all_hbm, local_sems.at[1]))
     saves[1].start()
-    for _, _, arrives, slot in hops[-1]:
+    for _, _, arrives, slot in chains[0][-1]:
         pl.when(arrives)(spread_slot(slot))
 
     @pl.loop(0, ring)
@@ -1200,7 +1177,8 @@
 
     for copy in later:
         copy.wait_recv()
-    hop_finish(hops)
+    for chain in chains:
+        hop_finish(chain)
     for copy in early + later:
         copy.wait_send()
     pair_keep.wait()
@@ -1240,7 +1218,7 @@
             pltpu.SemaphoreType.DMA((total,)),
             pltpu.SemaphoreType.DMA((4 + 4 * heads,)),
         ]
-        + [pltpu.SemaphoreType.DMA((depth - 1,))] * 4,
+        + [pltpu.SemaphoreType.DMA((2 * (depth - 1),))] * 4,
         compiler_params=pltpu.CompilerParams(
             collective_id=collective_id, has_side_effects=True, vmem_limit_bytes=VMEM_LIMIT
         ),
@@ -1386,7 +1364,7 @@
 
     @pl.when(step == 0)
     def _():
-        greet_near((sibling, across, along))
+        greet((sibling, across, along))
         for k in range(4):
             loads[k].start()
             copies[k].start()
@@ -1431,7 +1409,7 @@
             copy.wait_send()
 
 
-def sums_in_steps(
+def sum_phases(
     term_ref, share_ref, held_ref, land_ref, up_sems, down_sems, load_sems, trade_sems
 ):
     depth, rows, _ = held_ref.shape
@@ -1480,11 +1458,9 @@
             )
             hop.append((copy, leaves, arrives & inside, lax.rem(mine + depth, depth)))
         hops.append(hop)
-    step, steps = pl.program_id(0), pl.num_programs(0)
-
-    def start(r):
-        for copy, leaves, _, _ in hops[r]:
-            pl.when(leaves)(copy.start)
+    def start(r, from_end):
+        for end, (copy, leaves, _, _) in zip((0, last), hops[r]):
+            pl.when(leaves & ((place == end) == from_end))(copy.start)
 
     def arrive(r):
         for k, (copy, _, arrives, block) in enumerate(hops[r]):
@@ -1495,54 +1471,58 @@
                 total = held_ref[block].astype(F32) + land_ref[r, k].astype(F32)
                 held_ref[block] = total.astype(BF16)
 
-    @pl.when(step == 0)
-    def _():
-        for copy in loads + trades:
-            copy.start()
-
-    @pl.when(step == 1)
-    def _():
-        for load in loads:
-            load.wait()
-        for trade in trades:
-            trade.wait_recv()
-            trade.wait_send()
-        start(0)
-
-    for r, turn in enumerate((3, 5, steps - 1)):
-
-        @pl.when(step == turn)
-        def _(r=r):
-            arrive(r)
-            if r + 1 < last:
-                start(r + 1)
-            else:
-                for hop in hops:
-                    for copy, leaves, _, _ in hop:
-                        pl.when(leaves)(copy.wait_send)
-                share_ref[...] = held_ref[place]
+    for copy in loads + trades:
+        copy.start()
+    yield
+    for load in loads:
+        load.wait()
+    for trade in trades:
+        trade.wait_recv()
+    for r in range(last):
+        start(r, True)
+    for r in range(last):
+        start(r, False)
+        yield
+        arrive(r)
+    share_ref[...] = held_ref[place].astype(F32)
+    for trade in trades:
+        trade.wait_send()
+    for hop in hops:
+        for copy, leaves, _, _ in hop:
+            pl.when(leaves)(copy.wait_send)
+    yield
 
 
 def small_sum_kernel(
     heads,
     own_ref,
     cut_ref,
+    term_ref,
+    first_ref,
+    second_ref,
+    third_ref,
+    decay_ref,
+    taps_ref,
+    param_ref,
+    joined_ref,
+    share_ref,
     all_ref,
-    shared_ref,
-    joined_ref,
     swapped_ref,
     stage_ref,
     total_ref,
     send_sems,
     recv_sems,
     local_sem,
+    *sum_refs,
 ):
-    depth, ring = stage_ref.shape[0], all_ref.shape[0]
+    depth, ring = stage_ref.shape[0], cut_ref.shape[0]
     place, me = lax.axis_index("dp"), lax.axis_index("seq")
     mesh_ids = pl.DeviceIdType.MESH
     columns = [lax.rem(place + k, depth) for k in range(1, depth)]
     plane = [lax.rem(me + k, ring) for k in range(1, ring)]
     greet_all(ring, depth)
+    sums = sum_phases(term_ref, share_ref, *sum_refs)
+    next(sums)
     keep = pltpu.make_async_copy(cut_ref.at[me], swapped_ref.at[me], local_sem)
     keep.start()
     first = []
@@ -1561,6 +1541,7 @@
         cut_ref, swapped_ref.at[me], send_sems, recv_sems, depth + ring - 2
     )
     stage_ref[place] = own_ref[...]
+    next(sums)
     for copy in first:
         copy.wait_recv()
     total = stage_ref[0]
@@ -1580,13 +1561,22 @@
         copy.start()
         second.append(copy)
     all_ref[me] = total
+    next(sums)
+    next(sums)
     for copy in second:
         copy.wait_recv()
-    shared_rows = shared_ref.shape[0]
-    shared = all_ref[0, :shared_rows]
-    for s in range(1, ring):
-        shared = shared + all_ref[s, :shared_rows]
-    shared_ref[...] = shared
+    start = 0
+    for target in (first_ref, second_ref, third_ref):
+        rows = target.shape[0]
+        shared = all_ref[0, start : start + rows]
+        for s in range(1, ring):
+            shared = shared + all_ref[s, start : start + rows]
+        target[...] = shared
+        start += rows
+    for target in (decay_ref, taps_ref, param_ref):
+        rows = target.shape[1]
+        target[...] = all_ref[:, start : start + rows]
+        start += rows
     for copy in swaps:
         copy.wait_recv()
     keep.wait()
@@ -1597,36 +1587,46 @@
             start = (block * ring * heads + rank_head(s, j, heads)) * size
             joined_ref[:, start : start + size] = swapped_ref[
                 s, :, part * size : (part + 1) * size
-            ].astype(F32)
+            ]
+    next(sums)
     for copy in first + second + swaps:
         copy.wait_send()
 
 
-def small_sum(own, shared_rows, cut, heads, collective_id):
+def small_sum(own, shared_counts, own_counts, cut, term, heads, collective_id):
     depth, ring = lax.axis_size("dp"), lax.axis_size("seq")
     count = depth + 2 * ring - 3
+    term_rows, columns = term.shape[0] // depth, term.shape[1]
     vmem, anywhere = pl.BlockSpec(memory_space=pltpu.VMEM), pl.BlockSpec(memory_space=pl.ANY)
     return pl.pallas_call(
         functools.partial(small_sum_kernel, heads),
         out_shape=[
-            jax.ShapeDtypeStruct((ring,) + own.shape, F32),
-            jax.ShapeDtypeStruct((shared_rows, own.shape[1]), F32),
-            jax.ShapeDtypeStruct((cut.shape[1], ring * cut.shape[2]), F32),
+            *[jax.ShapeDtypeStruct((count, own.shape[1]), F32) for count in shared_counts],
+            *[jax.ShapeDtypeStruct((ring, count, own.shape[1]), F32) for count in own_counts],
+            jax.ShapeDtypeStruct((cut.shape[1], ring * cut.shape[2]), cut.dtype),
+            jax.ShapeDtypeStruct((term_rows, columns), F32),
         ],
-        in_specs=[vmem, anywhere],
-        out_specs=[vmem, vmem, vmem],
+        in_specs=[vmem, anywhere, anywhere],
+        out_specs=[vmem] * 8,
         scratch_shapes=[
+            pltpu.VMEM((ring,) + own.shape, F32),
             pltpu.VMEM(cut.shape, cut.dtype),
             pltpu.VMEM((depth,) + own.shape, F32),
             pltpu.VMEM(own.shape, F32),
             pltpu.SemaphoreType.DMA((count,)),
             pltpu.SemaphoreType.DMA((count,)),
             pltpu.SemaphoreType.DMA,
+            pltpu.VMEM((depth, term_rows, columns), BF16),
+            pltpu.VMEM((depth - 1, 2, term_rows, columns), BF16),
+            pltpu.SemaphoreType.DMA((2, depth - 1)),
+            pltpu.SemaphoreType.DMA((2, depth - 1)),
+            pltpu.SemaphoreType.DMA((depth // 2,)),
+            pltpu.SemaphoreType.DMA((2, depth // 2)),
         ],
         compiler_params=pltpu.CompilerParams(collective_id=collective_id, has_side_effects=True),
         cost_estimate=lasting(20),
         name="small_sum",
-    )(own, cut)
+    )(own, cut, term)
 
 
 def greet_plane(ring):
@@ -1634,7 +1634,7 @@
     greet([lax.rem(me + k, ring) for k in range(1, ring)])
 
 
-def plane_scatter_dot_kernel(count, dims, fill, swaps, back, *refs):
+def plane_scatter_dot_kernel(count, dims, fill, swaps, back, ends, low, *refs):
     refs = list(refs)
 
     def take(size):
@@ -1642,37 +1642,50 @@
         del refs[:size]
         return taken
 
-    left_hbm, right_hbm, fill_hbm = take(count), take(count), take(int(fill))
-    cut_refs, back_hbm = take(swaps), take(2 * back)
+    left_hbm, right_hbm, fill_hbm = take(count), take(count), take(int(len(fill) > 0))
+    cut_refs, back_hbm, end_hbm = take(swaps), take(2 * back), take(3 * ends)
     (sum_ref,) = take(1)
-    terms = take(count if fill else 0)
-    spread_refs, swapped_refs = take(swaps), take(swaps)
-    lefts, rights, fill_refs = take(count), take(count), take(int(fill))
+    terms, spread_refs = take(len(fill)), take(swaps)
+    gain_grads, low_refs = take(ends), take(int(low))
+    swapped_refs = take(swaps)
+    lefts, rights, fill_refs = take(count), take(count), take(int(len(fill) > 0))
     out_ref, own_ref, near_ref, far_in_ref, side_in_ref = take(5)
-    send_sems, recv_sems, load_sems = take(3)
-    loads = []
-    for k in range(count):
-        for source, target in ((left_hbm[k], lefts[k]), (right_hbm[k], rights[k])):
-            load = pltpu.make_async_copy(source, target, load_sems.at[len(loads)])
-            load.start()
-            loads.append(load)
+    send_sems, recv_sems, load_sems, slab_sems = take(4)
     me, sibling, across, along = plane_peers()
     far = along + across - me
     flip = sibling - me
+    slab_order = [far + flip, far, across + flip, across, along + flip, along, sibling, me]
+    loads, slab_loads = [], []
+    for k in range(count):
+        load = pltpu.make_async_copy(right_hbm[k], rights[k], load_sems.at[k])
+        load.start()
+        loads.append(load)
+    for n, slab in enumerate(slab_order):
+        for k in range(count):
+            load = pltpu.make_async_copy(
+                left_hbm[k].at[slab], lefts[k].at[slab], slab_sems.at[k * len(slab_order) + n]
+            )
+            load.start()
+            slab_loads.append(load)
+    if ends:
+        base_ref, up_ref, end_sems = take(3)
+        end_loads = [
+            pltpu.make_async_copy(end_hbm[0], base_ref, end_sems.at[0]),
+            pltpu.make_async_copy(end_hbm[1], up_ref, end_sems.at[1]),
+        ]
+        gain_grads[0][...] = jnp.zeros_like(gain_grads[0])
     if back:
         error_ref, down_ref, error_sems, down_sem = refs
-        error_order = [far + flip, far, across + flip, across, along + flip, along, sibling, me]
         down_load = pltpu.make_async_copy(back_hbm[1], down_ref, down_sem)
         down_load.start()
         error_loads = [
             pltpu.make_async_copy(back_hbm[0].at[slab], error_ref.at[k % 2], error_sems.at[k % 2])
-            for k, slab in enumerate(error_order)
+            for k, slab in enumerate(slab_order)
         ]
         error_loads[0].start()
         error_loads[1].start()
     if fill:
-        fill_load = pltpu.make_async_copy(fill_hbm[0], fill_refs[0], load_sems.at[2 * count])
-        fill_load.start()
+        fill_load = pltpu.make_async_copy(fill_hbm[0], fill_refs[0], load_sems.at[count])
     rows, columns = sum_ref.shape
     half = rows // 2
     upper, lower = pl.ds(0, half), pl.ds(half, half)
@@ -1680,7 +1693,7 @@
     if swaps:
         greet_plane(lefts[0].shape[0])
         keep = pltpu.make_async_copy(
-            cut_refs[0].at[me], swapped_refs[0].at[me], load_sems.at[2 * count]
+            cut_refs[0].at[me], swapped_refs[0].at[me], load_sems.at[count + 1]
         )
         keep.start()
         swapped = exchange_copies(
@@ -1690,6 +1703,9 @@
         greet((sibling, across, along))
     for load in loads:
         load.wait()
+    if ends:
+        for load in end_loads:
+            load.start()
     if back:
         down_load.wait()
     wide = 512
@@ -1710,6 +1726,8 @@
             error_loads[k + 2].start()
 
     def slab_dot(slab, target):
+        for _ in range(count):
+            slab_loads.pop(0).wait()
         if back:
             feed_back(slab)
 
@@ -1743,6 +1761,8 @@
         nears.append(send(k, sibling, out_ref.at[k], near_ref.at[k]))
 
     near_slab(0, far)
+    if fill:
+        fill_load.start()
     slab_dot(far, own_ref.at[0])
     near_slab(1, across)
     nears[0].wait_recv()
@@ -1781,9 +1801,9 @@
         def _(i):
             at = pl.ds(pl.multiple_of(i * tall, tall), tall)
             turned = fill_refs[0][:, at]
-            for k in range(count):
+            for term, k in zip(terms, fill):
                 wide_left = lefts[k][...].reshape(-1, lefts[k].shape[2])
-                terms[k][at, :] = low_dot(turned, wide_left, TN).astype(BF16)
+                term[at, :] = low_dot(turned, wide_left, TN).astype(term.dtype)
 
     nears[3].wait_recv()
 
@@ -1791,22 +1811,36 @@
         @pl.loop(0, half // step)
         def _(i):
             at = pl.ds(pl.multiple_of(start + i * step, step), step)
-            sum_ref[at] = (
+            total = (
                 own_ref[3, at].astype(F32)
                 + near_ref[3, at].astype(F32)
                 + side_in_ref[0, at].astype(F32)
                 + side_in_ref[1, at].astype(F32)
             )
+            if ends:
+                base = base_ref[at].astype(F32)
+                scale = lax.rsqrt(jnp.mean(base * base, -1, keepdims=True) + 1e-05)
+                normal = base * scale
+                weighted = total * end_hbm[2][...]
+                inner = jnp.mean(weighted * normal, -1, keepdims=True)
+                gain_grads[0][0:1, :] += jnp.sum(total * normal, 0, keepdims=True)
+                total = up_ref[at].astype(F32) + scale * (weighted - normal * inner)
+            sum_ref[at] = total
+            if low:
+                low_refs[0][at] = total.astype(BF16)
 
     for copy in copies[2:]:
         copy.wait_recv()
+    if ends:
+        for load in end_loads:
+            load.wait()
     finish(0, 0)
     finish(1, half)
     for copy in nears + copies + swapped:
         copy.wait_send()
 
 
-def plane_scatter_dot(lefts, rights, dims, collective_id, fill=None, cut=None, back=()):
+def plane_scatter_dot(lefts, rights, dims, collective_id, fill=None, fill_lefts=(0,), term_type=BF16, cut=None, back=(), ends=(), low=False):
     count = len(lefts)
     ring, rows, _ = lefts[0].shape
     columns = rights[0].shape[1 - dims[1][0]]
@@ -1823,16 +1857,37 @@
         ]
     cuts = [] if cut is None else [cut]
     total = 10 + len(cuts) * (ring - 1)
+    fill_lefts = fill_lefts if filled else ()
     term_shapes = [
-        jax.ShapeDtypeStruct((fill.shape[1], left.shape[2]), BF16) for left in lefts if filled
+        jax.ShapeDtypeStruct((fill.shape[1], lefts[k].shape[2]), term_type) for k in fill_lefts
     ]
+    end_shapes = [jax.ShapeDtypeStruct((8, columns), F32)] if ends else []
+    end_shapes += [jax.ShapeDtypeStruct((rows, columns), BF16)] if low else []
+    end_scratch = []
+    if ends:
+        end_scratch = [
+            pltpu.VMEM(ends[0].shape, ends[0].dtype),
+            pltpu.VMEM(ends[1].shape, ends[1].dtype),
+            pltpu.SemaphoreType.DMA((2,)),
+        ]
     return pl.pallas_call(
-        functools.partial(plane_scatter_dot_kernel, count, dims, filled, len(cuts), len(back) // 2),
+        functools.partial(
+            plane_scatter_dot_kernel,
+            count,
+            dims,
+            fill_lefts,
+            len(cuts),
+            len(back) // 2,
+            len(ends) // 3,
+            low,
+        ),
         out_shape=[jax.ShapeDtypeStruct((rows, columns), F32)]
         + term_shapes
-        + [jax.ShapeDtypeStruct((cut.shape[1], ring * cut.shape[2]), F32) for cut in cuts],
-        in_specs=[anywhere] * (2 * count + len(fills) + len(cuts) + len(back)),
-        out_specs=[vmem] * (1 + len(term_shapes) + len(cuts)),
+        + [jax.ShapeDtypeStruct((cut.shape[1], ring * cut.shape[2]), BF16) for cut in cuts]
+        + end_shapes,
+        in_specs=[anywhere] * (2 * count + len(fills) + len(cuts) + len(back) + len(ends[:2]))
+        + [vmem] * len(ends[2:]),
+        out_specs=[vmem] * (1 + len(term_shapes) + len(cuts) + len(end_shapes)),
         scratch_shapes=[pltpu.VMEM(cut.shape, BF16) for cut in cuts]
         + [pltpu.VMEM(left.shape, BF16) for left in lefts]
         + [pltpu.VMEM(right.shape, BF16) for right in rights]
@@ -1845,15 +1900,17 @@
             pltpu.VMEM((2, rows, columns), BF16),
             pltpu.SemaphoreType.DMA((total,)),
             pltpu.SemaphoreType.DMA((total,)),
-            pltpu.SemaphoreType.DMA((2 * count + len(fills) + len(cuts),)),
+            pltpu.SemaphoreType.DMA((count + 2,)),
+            pltpu.SemaphoreType.DMA((8 * count,)),
         ]
+        + end_scratch
         + back_scratch,
         compiler_params=pltpu.CompilerParams(
             collective_id=collective_id, has_side_effects=True, vmem_limit_bytes=VMEM_LIMIT
         ),
         cost_estimate=lasting(45),
         name="plane_scatter_dot",
-    )(*lefts, *rights, *fills, *cuts, *back)
+    )(*lefts, *rights, *fills, *cuts, *back, *ends)
 
 
 def gather_in_turn(own_ref, all_ref, send_sems, recv_sems, use):
@@ -2123,15 +2180,6 @@
     )(own, gated, weight, activated, down_own)
 
 
-def rms_back(values, gain, grad):
-    scale = lax.rsqrt(jnp.mean(values * values, -1, keepdims=True) + 1e-05)
-    weighted = grad * gain
-    part = scale * weighted - values * (
-        scale * scale * scale * jnp.mean(weighted * values, -1, keepdims=True)
-    )
-    return (part, jnp.sum(grad * values * scale, 0))
-
-
 def low_dot(left, right, dims):
     return lax.dot_general(left, right, (dims, ((), ())), preferred_element_type=F32)
 
@@ -2229,22 +2277,21 @@
         second_low, pair_own, out_err_all, 3
     )
     down_share = scatter_rows(down_term, "dp").astype(F32)
-    second_grad, pair_term = plane_scatter_dot(
+    hidden_grad, pair_term, second_gain_grad, branch_err = plane_scatter_dot(
         [pair_part],
         [pair_own],
         NT,
         4,
         second_all.reshape(all_rows, model_width),
         back=(out_err_all, down_own),
+        ends=(hidden, out_err, second_gain.reshape(1, model_width)),
+        low=True,
     )
     pair_share = scatter_rows(pair_term, "dp")
-    hidden_part, second_gain_grad = rms_back(hidden, second_gain, second_grad)
-    hidden_grad = upstream + hidden_part
-    branch_err = hidden_grad.astype(BF16)
     gated_grad, output_term, down_part = gather_branch(
         branch_err, gated, out_own, activated, down_own, 11
     )
-    in_err, logit_grad, taps_grad, param_grad, gain_grad, final_part, output_share = run_backward(
+    in_err, logit_grad, taps_grad, param_grad, gain_grad, final_part = run_backward(
         mixed,
         gate_raw,
         logits,
@@ -2257,7 +2304,6 @@
         mixer_out,
         gated_grad.reshape(ring, seqs, span, width),
         down_part,
-        output_term,
         12,
     )
     result = valid_rows * (hidden + final_part)
@@ -2266,11 +2312,9 @@
         (input_term, in_err, logit_grad, down_share, pair_share)
     )
     lanes = logit_grad.shape[-1]
-    decay_term = low_dot(normed_all, logit_grad.reshape(all_rows, lanes), TN)
-    decay_term, in_err = lax.optimization_barrier((decay_term, in_err))
     input_cut = scatter_rows(input_term, "dp")
     decay_twice = decay_own + jnp.roll(decay_own, lanes // 2, 1)
-    normed_grad, gate_up_share = plane_scatter_dot(
+    inputs_grad, decay_term, gate_up_share, first_gain_grad = plane_scatter_dot(
         [
             in_err.reshape(ring, row_count, 4 * width),
             logit_grad.reshape(ring, row_count, lanes),
@@ -2278,37 +2322,54 @@
         [in_own, decay_twice],
         NT,
         6,
+        normed_all,
+        (1,),
+        F32,
         cut=pair_share.reshape(ring, weight_rows, 2 * units),
-    )
-    token_part, first_gain_grad = rms_back(tokens, first_gain, normed_grad)
-    inputs_grad = hidden_grad + token_part
+        ends=(
+            inputs.reshape(row_count, model_width),
+            hidden_grad,
+            first_gain.reshape(1, model_width),
+        ),
+    )
     decay_term = decay_term[:, : 2 * heads] + decay_term[:, lanes // 2 : lanes // 2 + 2 * heads]
-    shared = jnp.concatenate([first_gain_grad, second_gain_grad, gain_grad[0]])
-    shared = jnp.pad(shared, (0, -shared.size % 1024))
-    pieces = [jnp.transpose(decay_term), taps_grad[:tap_count], param_grad[:2]]
-    packed = jnp.concatenate([shared] + [piece.reshape(-1) for piece in pieces])
+    pieces = [
+        first_gain_grad[0],
+        second_gain_grad[0],
+        gain_grad[0],
+        jnp.transpose(decay_term),
+        taps_grad[:tap_count],
+        param_grad[:2],
+    ]
+    counts = [piece.size // 128 for piece in pieces]
+    packed = jnp.concatenate([piece.reshape(-1) for piece in pieces])
     packed = jnp.pad(packed, (0, -packed.size % 1024)).reshape(-1, 128)
-    packed, input_cut, inputs_grad, result = lax.optimization_barrier(
-        (packed, input_cut, inputs_grad, result)
-    )
-    summed, shared_sum, input_share = small_sum(
+    gate_up_share = gate_up_share.astype(F32)
+    packed, input_cut, gate_up_share, result = lax.optimization_barrier(
+        (packed, input_cut, gate_up_share, result)
+    )
+    (
+        first_gain_grad,
+        second_gain_grad,
+        gain_grad,
+        decay_sum,
+        taps_sum,
+        param_sum,
+        input_share,
+        output_share,
+    ) = small_sum(
         packed,
-        shared.size // 128,
+        counts[:3],
+        counts[3:],
         input_cut.reshape(ring, weight_rows, 4 * width),
+        output_term,
         heads,
         7,
     )
-    shared_sum = shared_sum.reshape(-1)
-    first_gain_grad = shared_sum[:model_width]
-    second_gain_grad = shared_sum[model_width : 2 * model_width]
-    gain_grad = shared_sum[2 * model_width : 2 * model_width + head_size]
-    parted = []
-    start = shared.size // 128
-    for piece in pieces:
-        count = piece.size // 128
-        parted.append(summed[:, start : start + count])
-        start += count
-    decay_sum, taps_sum, param_sum = parted
+    input_share = input_share.astype(F32)
+    first_gain_grad, second_gain_grad, gain_grad = [
+        total.reshape(-1) for total in (first_gain_grad, second_gain_grad, gain_grad)
+    ]
     chips = ring // 2
     decay_sum = decay_sum.reshape(chips, 2, 2, heads, model_width)
     decay_weight_grad = jnp.transpose(decay_sum, (4, 2, 1, 3, 0)).reshape(model_width, -1)
@@ -2326,7 +2387,7 @@
         param_sum[0],
         param_sum[1],
         gain_grad,
-        output_share.astype(F32),
+        output_share,
         second_gain_grad,
         gate_up_share,
         down_share,

time: 601 us -> 590 us (0.982)
  other arithmetic: 25.8 us -> 19.7 us
    pallas_call x1, Pallas kernels: 59.3 us -> 51 us  [run_backward(): pl.pallas_call(mixer_backward, grid=(steps,), in_specs=[rows(3 * width),...]
    reduce_sum x3 -> x0, other arithmetic: 6.54 us -> none  [the longest x1 2.3 us: rms_back(): return (part, jnp.sum(grad * values * scale, 0))]
    dot_general x2 -> x1, matrix products: 20.1 us -> 14.2 us  [low_dot(): lax.dot_general(left, right, (dims, ((), ())), preferred_element_type=F32)]
  transfers between devices with their start and end apart: 6 -> 6, of which waited for: 2 -> 2; matrix products, arithmetic and copies ran while one was open for 9% -> 7% of each run, Pallas kernels for 80% -> 80%
where the time goes in v5:
time: 590 us; the launch traced here: 582 us
  Pallas kernels  497 us (84%)
  local copies, waits for them, and re-layouts  22.5 us (4%)
  other arithmetic  19.7 us (3%)
  between operations  14.7 us (2%)
  matrix products  14.2 us (2%)
  waiting for transfers between devices  13.1 us (2%)
    pallas_call x3, Pallas kernels, plane_scatter_dot(): pl.pallas_call(functools.partial(plane_scatter_dot_kernel, count, dims, f...  167 us
    pallas_call x1, Pallas kernels, plane_open(): pl.pallas_call(functools.partial(plane_open_kernel, heads), out_shape=[ja...  101 us
    pallas_call x1, Pallas kernels, run_forward(): pl.pallas_call(mixer_forward, grid=(steps,), in_specs=[rows(3 * width), r...  55.5 us
    pallas_call x1, Pallas kernels, run_backward(): pl.pallas_call(mixer_backward, grid=(steps,), in_specs=[rows(3 * width),...  51 us
    pallas_call x1, Pallas kernels, gather_feed(): pl.pallas_call(gather_feed_kernel, out_shape=[jax.ShapeDtypeStruct((ring,...  48.1 us
    pallas_call x1, Pallas kernels, gather_branch(): pl.pallas_call(gather_branch_kernel, out_shape=[jax.ShapeDtypeStruct((rin...  44.9 us
    pallas_call x1, Pallas kernels, small_sum(): pl.pallas_call(functools.partial(small_sum_kernel, heads), out_shape=[*[j...  29.2 us
    dot_general x1, matrix products, low_dot(): lax.dot_general(left, right, (dims, ((), ())), preferred_element_type=F32)  14.2 us
  transfers between devices with their start and end apart: 6, of which 2 were waited for; matrix products, arithmetic and copies ran while one was open for 7% of the time, Pallas kernels for 80%

profile of v5, /device:TPU:1, one launch (start us, length us, event | category | flops | bytes accessed | tf_op | source)
XLA Modules:
  0.0 582.1 jit_solution(1471338797872581158)
XLA Ops:
  7.2 0.7 all-gather.4.cloned.1.call-update
  8.0 0.9 constant_dynamic-slice_fusion.11
  8.9 0.3 copy.50
  9.3 1.6 multiply_reduce_fusion.1
  10.9 0.1 pad_slice_fusion
  11.0 1.3 pad_add_fusion
  12.3 1.3 fusion.1.first_ref
  13.5 101.3 %plane_open.1 = (bf16[8,256,2048]{2,1,0:T(8,128)(2,1)}, bf16[4,512,1024]{2,1,0:T(8,128)(2,1)}, bf16[8,64,1408]{2,1,0:T(8,128)(2,1)}, bf16[8,256,768]{2,1,0:T(8,1...) custom-call(bf16[256,2048]{1,0:T(8,128)(2,1)} %fusion.1.first_ref, bf16[64,8192]{1,0:T(8,128)(2,1)} %weight_hbm.1, ...), custom_call_target="tpu_custom_call" | custom-call | bytes 525000000 | tf_op jit(solution)/shard_map/plane_open/pallas_call | solution.py:1198
  114.9 0.0 all-gather.8.cloned.1.call-start
  115.0 0.7 all-gather.8.cloned.1.call-update
  115.6 0.5 reduce-scatter.4.cloned.1.call-start
  116.2 0.1 constant_dynamic-slice_fusion.1
  116.3 0.1 select_maximum_fusion
  116.4 0.6 pad.19.param_ref
  117.0 0.7 constant_dynamic-update-slice_fusion.5
  117.7 0.7 constant_dynamic-update-slice_fusion.4
  118.4 0.7 constant_dynamic-update-slice_fusion.3
  119.1 0.7 constant_dynamic-update-slice_fusion.2
  119.8 0.7 constant_dynamic-update-slice_fusion.1
  120.4 0.7 constant_dynamic-update-slice_fusion.taps_ref
  121.1 0.1 compare_convert_fusion
  121.2 1.2 fusion.2.own_ref.refs_6_
  122.4 55.5 %mixer_forward.1 = (bf16[8,2,128,256]{3,2,1,0:T(8,128)(2,1)}, f32[8,2,2,128,128]{4,3,2,1,0:T(8,128)}, f32[8,2,2,128,128]{4,3,2,1,0:T(8,128)}, f32[8,2,128,256]{3...) custom-call(bf16[8,2,128,768]{3,2,1,0:T(8,128)(2,1)} %bitcast.62, ...), custom_call_target="tpu_custom_call" | custom-call | bytes 192500000 | tf_op jit(solution)/shard_map/mixer_forward/pallas_call | solution.py:779
  178.0 43.7 %plane_scatter_dot.3 = f32[256,2048]{1,0:T(8,128)} custom-call(bf16[8,256,256]{2,1,0:T(8,128)(2,1)} %bitcast.74, bf16[256,2048]{1,0:T(8,128)(2,1)} %get-tuple-element.78.refs_1_.weight_hbm), custom_call_target="tpu_custom_call" | custom-call | bytes 157500000 | tf_op jit(solution)/shard_map/plane_scatter_dot/pallas_call | solution.py:1873
  221.7 2.0 multiply_reduce_fusion
  223.6 1.4 multiply_convert_fusion.own_hbm
  225.1 48.1 %gather_feed.1 = (bf16[8,256,2048]{2,1,0:T(8,128)(2,1)}, bf16[8,256,704]{2,1,0:T(8,128)(2,1)}, bf16[8,256,1408]{2,1,0:T(8,128)(2,1)}, bf16[704,2048]{1,0:T(8,128)(2,1)}) custom-call(bf16[256,2048]{1,0:T(8,128)(2,1)} %multiply_convert_fusion.own_hbm, bf16[2048,1408]{1,0:T(8,128)(2,1)} %all-gather.6.cloned.1.call-done.pair_hbm.refs_1_, ...), custom_call_target="tpu_custom_call" | custom-call | bytes 161000000 | tf_op jit(solution)/shard_map/gather_feed/pallas_call | solution.py:2052
  273.2 0.0 reduce-scatter.6.cloned.1.call-start
  273.3 7.2 %all-gather.8.cloned.1.call-done.refs_4_.down_hbm = bf16[704,2048]{1,0:T(8,128)(2,1)} async-done(((bf16[176,2048]{1,0:T(8,128)(2,1)}), bf16[704,2048]{1,0:T(8,128)(2,1)}) %all-gather.8.cloned.1.call-update) | async-done | bytes 2883600 | tf_op jit(solution)/shard_map/all_gather | solution.py:895
  280.5 63.8 %plane_scatter_dot.4 = (f32[256,2048]{1,0:T(8,128)}, bf16[2048,1408]{1,0:T(8,128)(2,1)}, f32[8,2048]{1,0:T(8,128)}, bf16[256,2048]{1,0:T(8,128)(2,1)}) custom-call(bf16[8,256,1408]{2,1,0:T(8,128)(2,1)} %get-tuple-element.81.refs_0_, bf16[2048,1408]{1,0:T(8,128)(2,1)} %all-gather.6.cloned.1.call-done.pair_hbm.refs_1_, bf16[2048,2048]{1,0:T(8,128)(2,1)} %bitcast.68, ...), custom_call_target="tpu_custom_call" | custom-call | bytes 157500000 | tf_op jit(solution)/shard_map/plane_scatter_dot/pallas_call | solution.py:1873
  344.3 0.0 reduce-scatter.8.cloned.1.call-start
  344.4 44.9 %gather_branch.1 = (bf16[8,256,256]{2,1,0:T(8,128)(2,1)}, bf16[256,2048]{1,0:T(8,128)(2,1)}, bf16[8,256,2048]{2,1,0:T(8,128)(2,1)}) custom-call(bf16[256,2048]{1,0:T(8,128)(2,1)} %get-tuple-element.84.own_hbm, bf16[8,256,256]{2,1,0:T(8,128)(2,1)} %bitcast.75, bf16[256,2048]{1,0:T(8,128)(2,1)} %get-tuple-element.78.refs_1_.weight_hbm, ...), custom_call_target="tpu_custom_call" | custom-call | bytes 157500000 | tf_op jit(solution)/shard_map/gather_branch/pallas_call | solution.py:2152
  389.3 51.0 %mixer_backward.1 = (bf16[8,2,128,1024]{3,2,1,0:T(8,128)(2,1)}, bf16[8,2,128,128]{3,2,1,0:T(8,128)(2,1)}, f32[8,768]{1,0:T(8,128)}, f32[8,128]{1,0:T(8,128)}, f32[8,128]{1,0:T(8,128)}, /*index=5*/f32[256,2048]{1,0:T(8,128)}) custom-call(bf16[8,2,128,768]{3,2,1,0:T(8,128)(2,1)} %bitcast.63, bf16[8,2,128,768]{3,2,1,0:T(8,128)(2,1)} %bitcast.64, ...), custom_call_target="tpu_custom_call" | custom-call | bytes 192500000 | tf_op jit(solution)/shard_map/mixer_backward/pallas_call | solution.py:841
  440.2 14.2 %convolution_convert_fusion = bf16[2048,1024]{1,0:T(8,128)(2,1)} fusion(bf16[2048,2048]{1,0:T(8,128)(2,1)} %bitcast.66, bf16[2048,1024]{1,0:T(8,128)(2,1)} %bitcast.72), kind=kOutput, calls=%fused_computation | convolution fusion | flops 8592031744 | bytes 16777216 | tf_op jit(solution)/shard_map/dot_general | solution.py:2184
  454.5 2.4 convert_element_type.63
  456.9 1.0 slice.40
  457.9 0.6 copy-done.1
  458.5 3.2 add_multiply_fusion
  461.7 59.8 %plane_scatter_dot.5 = (f32[256,2048]{1,0:T(8,128)}, f32[2048,128]{1,0:T(8,128)}, bf16[64,11264]{1,0:T(8,128)(2,1)}, f32[8,2048]{1,0:T(8,128)}) custom-call(bf16[8,256,1024]{2,1,0:T(8,128)(2,1)} %bitcast.73, bf16[8,256,128]{2,1,0:T(8,128)(2,1)} %bitcast.85, bf16[2048,1024]{1,0:T(8,128)(2,1)} %bitcast.71, bf16[2048,128]{1,0:T(8,128)(2,1)} %get-tuple-element.162.refs_3_, ...), custom_call_target="tpu_custom_call" | custom-call | bytes 157500000 | tf_op jit(solution)/shard_map/plane_scatter_dot/pallas_call | solution.py:1873
  521.4 0.8 slice.39
  522.3 2.0 add_bitcast_fusion
  524.3 0.3 copy.51
  524.6 1.8 convert_element_type.64
  526.4 0.7 constant_dynamic-update-slice_fusion.10
  527.1 0.7 constant_dynamic-update-slice_fusion.7
  527.8 0.6 pad_bitcast_fusion.own_ref
  528.4 4.4 reduce-scatter.8.cloned.1.call-done
  532.8 29.2 %small_sum.1 = (f32[16,128]{1,0:T(8,128)}, f32[16,128]{1,0:T(8,128)}, f32[1,128]{1,0:T(1,128)}, f32[8,64,128]{2,1,0:T(8,128)}, f32[8,24,128]{2,1,0:T(8,128)}, /*...) custom-call(f32[128,128]{1,0:T(8,128)} %pad_bitcast_fusion.own_ref, ...), custom_call_target="tpu_custom_call" | custom-call | bytes 70000000 | tf_op jit(solution)/shard_map/small_sum/pallas_call | solution.py:1601
  562.0 0.9 copy.59
  563.0 0.1 copy.56
  563.1 0.6 squeeze.19
  563.7 0.1 copy.55
  563.8 0.6 squeeze.18
  564.3 0.9 copy.53
  565.3 0.7 reshape.207
  566.0 1.1 reshape.204
  567.1 0.9 copy.52
  568.0 1.7 reshape.205
  569.7 1.5 convert_element_type.65
  571.2 1.3 copy.76
  572.5 0.6 copy.77
  573.1 0.5 copy.78
  573.6 0.8 copy.79
  574.4 0.6 copy.80
  (58 shorter events, 0.4 us)
Async XLA Ops:
  7.2 107.8 %all-gather.4.cloned.1.call-start = ((), (), s32[]{:S(2)}) async-start(), calls=%async_computation.3 | async-start | bytes 1310720 | tf_op jit(solution)/shard_map/all_gather | solution.py:895
  7.9 217.2 %all-gather.6.cloned.1.call-start = ((), (), s32[]{:S(2)}) async-start(), calls=%async_computation.4 | async-start | bytes 7208960 | tf_op jit(solution)/shard_map/all_gather | solution.py:895
  9.3 3.0 copy-start.2
  9.3 3.0 copy-start.9
  114.8 1.4 copy-start.14
  114.8 1.4 copy-start.15
  114.9 6.3 %copy-start.16 = (s32[2,1]{0,1:T(1,128)S(1)}, s32[2,1]{0,1:T(1,128)}, u32[]{:S(2)}) copy-start(s32[2,1]{0,1:T(1,128)} %param.15) | copy-start | bytes 28
  114.9 6.3 %copy-start.6 = (bf16[2,1,128,2048]{3,2,1,0:T(8,128)(2,1)S(1)}, bf16[2,1,128,2048]{3,2,1,0:T(8,128)(2,1)}, u32[]{:S(2)}) copy-start(bf16[2,1,128,2048]{3,2,1,0:T(8,128)(2,1)} %param.27) | copy-start | bytes 3145732
  114.9 165.6 %all-gather.8.cloned.1.call-start = ((), (), s32[]{:S(2)}) async-start(), calls=%async_computation.5 | async-start | bytes 3604480 | tf_op jit(solution)/shard_map/all_gather | solution.py:895
  115.6 338.8 %reduce-scatter.4.cloned.1.call-start = ((), (), s32[]{:S(2)}) async-start(), calls=%async_computation.6 | async-start | bytes 3604480 | tf_op jit(solution)/shard_map/reduce_scatter | solution.py:899
  121.1 1.3 copy-start.8
  221.6 2.0 copy-start.10
  223.6 49.6 %copy-start = (f32[256,2048]{1,0:T(8,128)}, f32[256,2048]{1,0:T(8,128)S(1)}, u32[]{:S(2)}) copy-start(f32[256,2048]{1,0:T(8,128)S(1)} %get-tuple-element.161.refs_5_) | copy-start | bytes 6291460
  273.2 183.6 %reduce-scatter.6.cloned.1.call-start = ((), (), s32[]{:S(2)}) async-start(), calls=%async_computation.7 | async-start | bytes 7208960 | tf_op jit(solution)/shard_map/reduce_scatter | solution.py:899
  344.3 188.5 %reduce-scatter.8.cloned.1.call-start = ((), (), s32[]{:S(2)}) async-start(), calls=%async_computation.8 | async-start | bytes 5242880 | tf_op jit(solution)/shard_map/reduce_scatter | solution.py:899
  456.9 1.0 copy-start.13
  456.9 1.6 copy-start.1
  522.3 2.3 copy-start.4
  562.0 7.7 %copy-start.5 = (bf16[64,8192]{1,0:T(8,128)(2,1)S(1)}, bf16[64,8192]{1,0:T(8,128)(2,1)}, u32[]{:S(2)}) copy-start(bf16[64,8192]{1,0:T(8,128)(2,1)} %get-tuple-element.112) | copy-start | bytes 3145732
  567.1 4.1 copy-start.3
  571.2 1.3 copy-start.12
  571.2 1.9 copy-start.17
  571.2 2.5 copy-start.7
  571.2 3.2 copy-start.11
Sparse Core Ops, SparseCore 0:
  9.6 35.8 all-gather.3
  115.0 106.6 all-gather.5
  223.3 57.1 all-gather.7
  282.7 54.8 reduce-scatter.3
  344.4 100.8 reduce-scatter.5
  457.0 75.7 reduce-scatter.7

commit v6 on v5

--- a/solution.py
+++ b/solution.py
@@ -1163,17 +1163,35 @@
     for hop in chains[0][:-1]:
         for _, _, arrives, slot in hop:
             pl.when(arrives)(spread_slot(slot))
-    for chain in chains:
+    def close(g, slot=None):
+        def run():
+            columns = slice(2 * g * width, 2 * (g + 1) * width)
+
+            @pl.loop(0, ring)
+            def _(r):
+                total = total_ref[r, :, columns]
+                if slot is not None:
+                    at = pl.ds(pl.multiple_of(slot * deep, deep), deep)
+                    total = total + low_dot(
+                        first_all_ref[r, :, at], weight_all_ref[slot, :, columns], NN
+                    )
+                if g == 0:
+                    mixed_ref[r, :, : 2 * width] = total.astype(BF16)
+                else:
+                    mixed_ref[r, :, 2 * width :] = total[:, :width].astype(BF16)
+                    gate_ref[r] = total[:, width:]
+
+        return run
+
+    for g, chain in enumerate(chains):
         hop_arrive(chain[-1])
-    saves.append(pltpu.make_async_copy(weight_all_ref, weight_all_hbm, local_sems.at[1]))
-    saves[1].start()
-    for _, _, arrives, slot in chains[0][-1]:
-        pl.when(arrives)(spread_slot(slot))
-
-    @pl.loop(0, ring)
-    def _(r):
-        mixed_ref[r] = total_ref[r, :, : 3 * width].astype(BF16)
-        gate_ref[r] = total_ref[r, :, 3 * width :]
+        if g == len(chains) - 1:
+            saves.append(pltpu.make_async_copy(weight_all_ref, weight_all_hbm, local_sems.at[1]))
+            saves[1].start()
+        (_, _, from_below, low_slot), (_, _, from_above, high_slot) = chain[-1]
+        pl.when(from_below)(close(g, low_slot))
+        pl.when(from_above)(close(g, high_slot))
+        pl.when(jnp.logical_not(from_below | from_above))(close(g))
 
     for copy in later:
         copy.wait_recv()
@@ -1537,9 +1555,6 @@
         )
         copy.start()
         first.append(copy)
-    swaps = exchange_copies(
-        cut_ref, swapped_ref.at[me], send_sems, recv_sems, depth + ring - 2
-    )
     stage_ref[place] = own_ref[...]
     next(sums)
     for copy in first:
@@ -1560,6 +1575,9 @@
         )
         copy.start()
         second.append(copy)
+    swaps = exchange_copies(
+        cut_ref, swapped_ref.at[me], send_sems, recv_sems, depth + ring - 2
+    )
     all_ref[me] = total
     next(sums)
     next(sums)

time: 590 us -> 589 us (level)
  no operation moved by 1% of the time
where the time goes in v6:
time: 589 us; the launch traced here: 583 us
  Pallas kernels  498 us (85%)
  local copies, waits for them, and re-layouts  22.5 us (4%)
  other arithmetic  19.7 us (3%)
  between operations  14.7 us (2%)
  matrix products  14.2 us (2%)
  waiting for transfers between devices  13 us (2%)
    pallas_call x3, Pallas kernels, plane_scatter_dot(): pl.pallas_call(functools.partial(plane_scatter_dot_kernel, count, dims, f...  167 us
    pallas_call x1, Pallas kernels, plane_open(): pl.pallas_call(functools.partial(plane_open_kernel, heads), out_shape=[ja...  99.8 us
    pallas_call x1, Pallas kernels, run_forward(): pl.pallas_call(mixer_forward, grid=(steps,), in_specs=[rows(3 * width), r...  55.5 us
    pallas_call x1, Pallas kernels, run_backward(): pl.pallas_call(mixer_backward, grid=(steps,), in_specs=[rows(3 * width),...  51 us
    pallas_call x1, Pallas kernels, gather_feed(): pl.pallas_call(gather_feed_kernel, out_shape=[jax.ShapeDtypeStruct((ring,...  48.2 us
    pallas_call x1, Pallas kernels, gather_branch(): pl.pallas_call(gather_branch_kernel, out_shape=[jax.ShapeDtypeStruct((rin...  44.9 us
    pallas_call x1, Pallas kernels, small_sum(): pl.pallas_call(functools.partial(small_sum_kernel, heads), out_shape=[*[j...  31.7 us
    dot_general x1, matrix products, low_dot(): lax.dot_general(left, right, (dims, ((), ())), preferred_element_type=F32)  14.2 us
  transfers between devices with their start and end apart: 6, of which 2 were waited for; matrix products, arithmetic and copies ran while one was open for 7% of the time, Pallas kernels for 80%

profile of v6, /device:TPU:1, one launch (start us, length us, event | category | flops | bytes accessed | tf_op | source)
XLA Modules:
  0.0 583.1 jit_solution(1594331838505042318)
XLA Ops:
  7.2 0.7 all-gather.4.cloned.1.call-update
  8.0 0.9 constant_dynamic-slice_fusion.11
  8.9 0.3 copy.50
  9.3 1.6 multiply_reduce_fusion.1
  10.9 0.1 pad_slice_fusion
  11.0 1.3 pad_add_fusion
  12.3 1.3 fusion.1.first_ref
  13.5 99.8 %plane_open.1 = (bf16[8,256,2048]{2,1,0:T(8,128)(2,1)}, bf16[4,512,1024]{2,1,0:T(8,128)(2,1)}, bf16[8,64,1408]{2,1,0:T(8,128)(2,1)}, bf16[8,256,768]{2,1,0:T(8,1...) custom-call(bf16[256,2048]{1,0:T(8,128)(2,1)} %fusion.1.first_ref, bf16[64,8192]{1,0:T(8,128)(2,1)} %weight_hbm.1, ...), custom_call_target="tpu_custom_call" | custom-call | bytes 525000000 | tf_op jit(solution)/shard_map/plane_open/pallas_call | solution.py:1216
  113.4 0.0 all-gather.8.cloned.1.call-start
  113.5 0.7 all-gather.8.cloned.1.call-update
  114.2 0.5 reduce-scatter.4.cloned.1.call-start
  114.8 0.1 constant_dynamic-slice_fusion.1
  114.8 0.1 select_maximum_fusion
  114.9 0.6 pad.19.param_ref
  115.5 0.7 constant_dynamic-update-slice_fusion.5
  116.2 0.7 constant_dynamic-update-slice_fusion.4
  116.9 0.7 constant_dynamic-update-slice_fusion.3
  117.6 0.7 constant_dynamic-update-slice_fusion.2
  118.3 0.7 constant_dynamic-update-slice_fusion.1
  119.0 0.7 constant_dynamic-update-slice_fusion.taps_ref
  119.7 0.1 compare_convert_fusion
  119.7 1.2 fusion.2.own_ref.refs_6_
  121.0 55.5 %mixer_forward.1 = (bf16[8,2,128,256]{3,2,1,0:T(8,128)(2,1)}, f32[8,2,2,128,128]{4,3,2,1,0:T(8,128)}, f32[8,2,2,128,128]{4,3,2,1,0:T(8,128)}, f32[8,2,128,256]{3...) custom-call(bf16[8,2,128,768]{3,2,1,0:T(8,128)(2,1)} %bitcast.62, ...), custom_call_target="tpu_custom_call" | custom-call | bytes 192500000 | tf_op jit(solution)/shard_map/mixer_forward/pallas_call | solution.py:779
  176.5 43.6 %plane_scatter_dot.3 = f32[256,2048]{1,0:T(8,128)} custom-call(bf16[8,256,256]{2,1,0:T(8,128)(2,1)} %bitcast.74, bf16[256,2048]{1,0:T(8,128)(2,1)} %get-tuple-element.78.refs_1_.weight_hbm), custom_call_target="tpu_custom_call" | custom-call | bytes 157500000 | tf_op jit(solution)/shard_map/plane_scatter_dot/pallas_call | solution.py:1891
  220.1 2.0 multiply_reduce_fusion
  222.1 1.4 multiply_convert_fusion.own_hbm
  223.5 48.2 %gather_feed.1 = (bf16[8,256,2048]{2,1,0:T(8,128)(2,1)}, bf16[8,256,704]{2,1,0:T(8,128)(2,1)}, bf16[8,256,1408]{2,1,0:T(8,128)(2,1)}, bf16[704,2048]{1,0:T(8,128)(2,1)}) custom-call(bf16[256,2048]{1,0:T(8,128)(2,1)} %multiply_convert_fusion.own_hbm, bf16[2048,1408]{1,0:T(8,128)(2,1)} %all-gather.6.cloned.1.call-done.pair_hbm.refs_1_, ...), custom_call_target="tpu_custom_call" | custom-call | bytes 161000000 | tf_op jit(solution)/shard_map/gather_feed/pallas_call | solution.py:2070
  271.7 0.0 reduce-scatter.6.cloned.1.call-start
  271.8 7.2 %all-gather.8.cloned.1.call-done.refs_4_.down_hbm = bf16[704,2048]{1,0:T(8,128)(2,1)} async-done(((bf16[176,2048]{1,0:T(8,128)(2,1)}), bf16[704,2048]{1,0:T(8,128)(2,1)}) %all-gather.8.cloned.1.call-update) | async-done | bytes 2883600 | tf_op jit(solution)/shard_map/all_gather | solution.py:895
  279.0 63.8 %plane_scatter_dot.4 = (f32[256,2048]{1,0:T(8,128)}, bf16[2048,1408]{1,0:T(8,128)(2,1)}, f32[8,2048]{1,0:T(8,128)}, bf16[256,2048]{1,0:T(8,128)(2,1)}) custom-call(bf16[8,256,1408]{2,1,0:T(8,128)(2,1)} %get-tuple-element.81.refs_0_, bf16[2048,1408]{1,0:T(8,128)(2,1)} %all-gather.6.cloned.1.call-done.pair_hbm.refs_1_, bf16[2048,2048]{1,0:T(8,128)(2,1)} %bitcast.68, ...), custom_call_target="tpu_custom_call" | custom-call | bytes 157500000 | tf_op jit(solution)/shard_map/plane_scatter_dot/pallas_call | solution.py:1891
  342.8 0.0 reduce-scatter.8.cloned.1.call-start
  342.8 44.9 %gather_branch.1 = (bf16[8,256,256]{2,1,0:T(8,128)(2,1)}, bf16[256,2048]{1,0:T(8,128)(2,1)}, bf16[8,256,2048]{2,1,0:T(8,128)(2,1)}) custom-call(bf16[256,2048]{1,0:T(8,128)(2,1)} %get-tuple-element.84.own_hbm, bf16[8,256,256]{2,1,0:T(8,128)(2,1)} %bitcast.75, bf16[256,2048]{1,0:T(8,128)(2,1)} %get-tuple-element.78.refs_1_.weight_hbm, ...), custom_call_target="tpu_custom_call" | custom-call | bytes 157500000 | tf_op jit(solution)/shard_map/gather_branch/pallas_call | solution.py:2170
  387.7 51.0 %mixer_backward.1 = (bf16[8,2,128,1024]{3,2,1,0:T(8,128)(2,1)}, bf16[8,2,128,128]{3,2,1,0:T(8,128)(2,1)}, f32[8,768]{1,0:T(8,128)}, f32[8,128]{1,0:T(8,128)}, f32[8,128]{1,0:T(8,128)}, /*index=5*/f32[256,2048]{1,0:T(8,128)}) custom-call(bf16[8,2,128,768]{3,2,1,0:T(8,128)(2,1)} %bitcast.63, bf16[8,2,128,768]{3,2,1,0:T(8,128)(2,1)} %bitcast.64, ...), custom_call_target="tpu_custom_call" | custom-call | bytes 192500000 | tf_op jit(solution)/shard_map/mixer_backward/pallas_call | solution.py:841
  438.7 14.2 %convolution_convert_fusion = bf16[2048,1024]{1,0:T(8,128)(2,1)} fusion(bf16[2048,2048]{1,0:T(8,128)(2,1)} %bitcast.66, bf16[2048,1024]{1,0:T(8,128)(2,1)} %bitcast.72), kind=kOutput, calls=%fused_computation | convolution fusion | flops 8592031744 | bytes 16777216 | tf_op jit(solution)/shard_map/dot_general | solution.py:2202
  453.0 2.4 convert_element_type.63
  455.4 1.0 slice.40
  456.4 0.6 copy-done.1
  457.0 3.2 add_multiply_fusion
  460.1 59.8 %plane_scatter_dot.5 = (f32[256,2048]{1,0:T(8,128)}, f32[2048,128]{1,0:T(8,128)}, bf16[64,11264]{1,0:T(8,128)(2,1)}, f32[8,2048]{1,0:T(8,128)}) custom-call(bf16[8,256,1024]{2,1,0:T(8,128)(2,1)} %bitcast.73, bf16[8,256,128]{2,1,0:T(8,128)(2,1)} %bitcast.85, bf16[2048,1024]{1,0:T(8,128)(2,1)} %bitcast.71, bf16[2048,128]{1,0:T(8,128)(2,1)} %get-tuple-element.162.refs_3_, ...), custom_call_target="tpu_custom_call" | custom-call | bytes 157500000 | tf_op jit(solution)/shard_map/plane_scatter_dot/pallas_call | solution.py:1891
  519.9 0.8 slice.39
  520.7 2.0 add_bitcast_fusion
  522.7 0.3 copy.51
  523.1 1.8 convert_element_type.64
  524.9 0.7 constant_dynamic-update-slice_fusion.10
  525.6 0.7 constant_dynamic-update-slice_fusion.7
  526.2 0.6 pad_bitcast_fusion.own_ref
  526.9 4.4 reduce-scatter.8.cloned.1.call-done
  531.3 31.7 %small_sum.1 = (f32[16,128]{1,0:T(8,128)}, f32[16,128]{1,0:T(8,128)}, f32[1,128]{1,0:T(1,128)}, f32[8,64,128]{2,1,0:T(8,128)}, f32[8,24,128]{2,1,0:T(8,128)}, /*...) custom-call(f32[128,128]{1,0:T(8,128)} %pad_bitcast_fusion.own_ref, ...), custom_call_target="tpu_custom_call" | custom-call | bytes 70000000 | tf_op jit(solution)/shard_map/small_sum/pallas_call | solution.py:1619
  563.1 0.9 copy.59
  564.0 0.1 copy.56
  564.1 0.6 squeeze.19
  564.7 0.1 copy.55
  564.8 0.6 squeeze.18
  565.4 0.9 copy.53
  566.3 0.7 reshape.207
  567.0 1.1 reshape.204
  568.1 0.9 copy.52
  569.0 1.7 reshape.205
  570.8 1.5 convert_element_type.65
  572.2 1.3 copy.76
  573.6 0.6 copy.77
  574.2 0.5 copy.78
  574.7 0.8 copy.79
  575.5 0.6 copy.80
  (58 shorter events, 0.4 us)
Async XLA Ops:
  7.2 106.3 %all-gather.4.cloned.1.call-start = ((), (), s32[]{:S(2)}) async-start(), calls=%async_computation.3 | async-start | bytes 1310720 | tf_op jit(solution)/shard_map/all_gather | solution.py:895
  7.9 215.6 %all-gather.6.cloned.1.call-start = ((), (), s32[]{:S(2)}) async-start(), calls=%async_computation.4 | async-start | bytes 7208960 | tf_op jit(solution)/shard_map/all_gather | solution.py:895
  9.3 3.0 copy-start.2
  9.3 3.0 copy-start.9
  113.4 1.4 copy-start.14
  113.4 1.4 copy-start.15
  113.4 6.3 %copy-start.16 = (s32[2,1]{0,1:T(1,128)S(1)}, s32[2,1]{0,1:T(1,128)}, u32[]{:S(2)}) copy-start(s32[2,1]{0,1:T(1,128)} %param.15) | copy-start | bytes 28
  113.4 6.3 %copy-start.6 = (bf16[2,1,128,2048]{3,2,1,0:T(8,128)(2,1)S(1)}, bf16[2,1,128,2048]{3,2,1,0:T(8,128)(2,1)}, u32[]{:S(2)}) copy-start(bf16[2,1,128,2048]{3,2,1,0:T(8,128)(2,1)} %param.27) | copy-start | bytes 3145732
  113.4 165.5 %all-gather.8.cloned.1.call-start = ((), (), s32[]{:S(2)}) async-start(), calls=%async_computation.5 | async-start | bytes 3604480 | tf_op jit(solution)/shard_map/all_gather | solution.py:895
  114.2 338.8 %reduce-scatter.4.cloned.1.call-start = ((), (), s32[]{:S(2)}) async-start(), calls=%async_computation.6 | async-start | bytes 3604480 | tf_op jit(solution)/shard_map/reduce_scatter | solution.py:899
  119.7 1.3 copy-start.8
  220.1 2.0 copy-start.10
  222.0 49.6 %copy-start = (f32[256,2048]{1,0:T(8,128)}, f32[256,2048]{1,0:T(8,128)S(1)}, u32[]{:S(2)}) copy-start(f32[256,2048]{1,0:T(8,128)S(1)} %get-tuple-element.161.refs_5_) | copy-start | bytes 6291460
  271.7 183.6 %reduce-scatter.6.cloned.1.call-start = ((), (), s32[]{:S(2)}) async-start(), calls=%async_computation.7 | async-start | bytes 7208960 | tf_op jit(solution)/shard_map/reduce_scatter | solution.py:899
  342.8 188.6 %reduce-scatter.8.cloned.1.call-start = ((), (), s32[]{:S(2)}) async-start(), calls=%async_computation.8 | async-start | bytes 5242880 | tf_op jit(solution)/shard_map/reduce_scatter | solution.py:899
  455.3 1.0 copy-start.13
  455.3 1.6 copy-start.1
  520.7 2.3 copy-start.4
  563.1 7.7 %copy-start.5 = (bf16[64,8192]{1,0:T(8,128)(2,1)S(1)}, bf16[64,8192]{1,0:T(8,128)(2,1)}, u32[]{:S(2)}) copy-start(bf16[64,8192]{1,0:T(8,128)(2,1)} %get-tuple-element.112) | copy-start | bytes 3145732
  568.1 4.1 copy-start.3
  572.2 1.3 copy-start.12
  572.2 1.9 copy-start.17
  572.2 2.5 copy-start.7
  572.2 3.2 copy-start.11
Sparse Core Ops, SparseCore 0:
  9.6 35.8 all-gather.3
  113.5 106.5 all-gather.5
  221.7 57.2 all-gather.7
  281.1 54.8 reduce-scatter.3
  342.9 100.8 reduce-scatter.5
  455.5 75.8 reduce-scatter.7
